TPU v7x, 256 devices: a whole 4x4x8 slice. The times are simulated.
256 devices in a mesh: dp: 16 (over x_lo, y, core), pipe: 16 (over x_hi, z).
Axes of the slice: x: 4 (x_hi: 2, x_lo: 2; x = x_hi * 2 + x_lo), y: 4, z: 8, core: 2. Of those that a mesh axis runs over, the one named last changes fastest.
Arguments:
- hidden: bfloat16 [512, 4608], P(('dp', 'pipe')), may hold values from -6 to 6
- norm_gain: float32 [4608], replicated, may hold values from 0.5 to 1.5
- weight: bfloat16 [131072, 4608], P(('dp', 'pipe')), may hold values from -0.25 to 0.25
- targets: int32 [512], replicated, may hold values from 0 to 131071
Outputs:
- token_loss: float32 [512], P(('dp', 'pipe'))
- grad_hidden: float32 [512, 4608], P(('dp', 'pipe'))
- grad_weight: bfloat16 [131072, 4608], P(('dp', 'pipe'))
- grad_gain: float32 [4608], replicated
All inputs are finite; a program needn't handle non-finite values.
Results may differ from a plain program's by a relative error of at most 0.0055.
Values may be sent and summed in bfloat16 or wider, within the bound.
No kernel may reach another device: no remote copies, remote signals or barrier semaphores. Data moves between devices by JAX's collectives and lax.ppermute only.
A program may use at most 128 MiB of HBM per device.

v0:
```python
import jax
import jax.numpy as jnp
from jax import lax
from jax.experimental import pallas as pl
from jax.experimental.pallas import tpu as pltpu
from jax.sharding import Mesh, PartitionSpec as P

epsilon = 1e-06
cap_value = 30.0
entropy_weight = 0.2

AXES = ("x_lo", "y", "core", "x_hi", "z")
PLANE = ("x_lo", "y", "x_hi")
WIDTH = 4608
HALF = WIDTH // 2
TOKENS = 512
NEAR = TOKENS // 2
VOCAB_ROWS = 512
PIECE = 16
STEP = 768
STEPS = WIDTH // STEP
HALF_STEPS = HALF // STEP

RING = (0, 2, 1, 3)


def shift_y(block, step):
    return lax.ppermute(block, "y", [(p, (p + step) % 4) for p in range(4)])


def shift_x(block, step):
    pairs = [(RING[p], RING[(p + step) % 4]) for p in range(4)]
    return lax.ppermute(block, ("x_lo", "x_hi"), pairs)


def swap_cores(block):
    return lax.ppermute(block, "core", [(0, 1), (1, 0)])


def gather_over(block, axes, size):
    copies = jnp.broadcast_to(block[None], (size,) + block.shape)
    return lax.all_to_all(copies, axes, 0, 0, tiled=True)


def sum_over(block, axes, size):
    return jnp.sum(gather_over(block, axes, size), axis=0)


def gather_ring(block, shift):
    across, up, down = shift(block, 2), shift(block, 3), shift(block, 1)
    return [block, up, across, down]


def send_ring(blocks, shift):
    across, up, down = shift(blocks[2], 2), shift(blocks[1], 1), shift(blocks[3], 3)
    return [blocks[0], up, across, down]


def total(blocks):
    return sum(block.astype(jnp.float32) for block in blocks)


def piece_row(core, y, x):
    piece = ((lax.rem(x, 2) * 4 + y) * 2 + core) * 2 + lax.div(x, 2)
    return pl.multiple_of(piece * PIECE, PIECE)


def step_columns(step):
    return pl.ds(pl.multiple_of(step * STEP, STEP), STEP)


def steps(body, first=0, last=STEPS):
    lax.fori_loop(first, last, lambda j, carry: (body(j), carry)[1], 0)


def forward_kernel(place, targets, weight, *rest):
    blocks = rest[:16]
    gathered, capped_out, stats_out, weight_held, rows_held, logits, weight_sems, row_sems, out_sem = rest[16:]
    core, y, x, position = place[0], place[1], place[2], place[3]

    def half_rows(half):
        return rows_held.at[:, half * HALF : (half + 1) * HALF]

    def weight_copy(j):
        columns = step_columns(j)
        return pltpu.make_async_copy(weight.at[:, columns], weight_held.at[:, columns], weight_sems.at[j])

    def place_blocks(half):
        def pieces(inner, carry):
            for far in range(2):
                owner = core if far == 0 else 1 - core
                for outer in range(4):
                    up_y, up_x = (outer, inner) if half == 0 else (inner, outer)
                    row = piece_row(owner, lax.rem(y + up_y, 4), lax.rem(x + up_x, 4))
                    pltpu.make_async_copy(
                        blocks[far * 8 + half * 4 + outer].at[inner],
                        half_rows(half).at[pl.ds(row, PIECE), :],
                        row_sems.at[half],
                    ).start()
            return carry

        lax.fori_loop(0, 4, pieces, 0)

    def multiply(j):
        weight_copy(j).wait()
        columns = step_columns(j)
        logits[...] += lax.dot_general(
            weight_held[:, columns],
            rows_held[:, columns],
            (((1,), (1,)), ((), ())),
            preferred_element_type=jnp.float32,
        )

    steps(lambda j: weight_copy(j).start(), 0, HALF_STEPS)
    place_blocks(0)
    steps(lambda j: weight_copy(j).start(), HALF_STEPS, STEPS)
    place_blocks(1)
    logits[...] = jnp.zeros_like(logits)
    pltpu.make_async_copy(half_rows(0), half_rows(0), row_sems.at[0]).wait()
    steps(multiply, 0, HALF_STEPS)
    pltpu.make_async_copy(half_rows(1), half_rows(1), row_sems.at[1]).wait()
    out_copy = pltpu.make_async_copy(rows_held, gathered, out_sem)
    out_copy.start()
    steps(multiply, HALF_STEPS, STEPS)

    def finish(k, carry):
        rows = pl.ds(pl.multiple_of(k * 64, 64), 64)
        capped = cap_value * jnp.tanh(logits[rows, :] / cap_value)
        capped_out[rows, :] = capped
        powers = jnp.exp(capped - cap_value)
        entry = position * VOCAB_ROWS + k * 64 + lax.broadcasted_iota(jnp.int32, capped.shape, 0)
        hit = targets[...] == entry
        return (
            carry[0] + jnp.sum(powers, axis=0, keepdims=True),
            carry[1] + jnp.sum(powers * capped, axis=0, keepdims=True),
            carry[2] + jnp.sum(jnp.where(hit, capped, 0.0), axis=0, keepdims=True),
        )

    sums = lax.fori_loop(0, VOCAB_ROWS // 64, finish, (jnp.zeros((1, TOKENS), jnp.float32),) * 3)
    for k in range(3):
        stats_out[k : k + 1, :] = sums[k]
    out_copy.wait()


SCALARS = pl.BlockSpec(memory_space=pltpu.SMEM)
IN_VMEM = pl.BlockSpec(memory_space=pltpu.VMEM)
IN_HBM = pl.BlockSpec(memory_space=pltpu.HBM)
ANYWHERE = pl.BlockSpec(memory_space=pl.ANY)


def forward(place, targets, weight, blocks):
    return pl.pallas_call(
        forward_kernel,
        out_shape=(
            jax.ShapeDtypeStruct((TOKENS, WIDTH), jnp.bfloat16),
            jax.ShapeDtypeStruct((VOCAB_ROWS, TOKENS), jnp.float32),
            jax.ShapeDtypeStruct((3, TOKENS), jnp.float32),
        ),
        in_specs=[SCALARS, IN_VMEM, IN_HBM] + [ANYWHERE] * 16,
        out_specs=(IN_HBM, IN_VMEM, IN_VMEM),
        scratch_shapes=[
            pltpu.VMEM((VOCAB_ROWS, WIDTH), jnp.bfloat16),
            pltpu.VMEM((TOKENS, WIDTH), jnp.bfloat16),
            pltpu.VMEM((VOCAB_ROWS, TOKENS), jnp.float32),
            pltpu.SemaphoreType.DMA((STEPS,)),
            pltpu.SemaphoreType.DMA((2,)),
            pltpu.SemaphoreType.DMA,
        ],
        compiler_params=pltpu.CompilerParams(vmem_limit_bytes=50 << 20),
        cost_estimate=pl.CostEstimate(
            flops=2 * VOCAB_ROWS * TOKENS * WIDTH, bytes_accessed=16 << 20, transcendentals=1 << 19
        ),
        name="forward",
    )(place, targets, weight, *blocks)


def far_kernel(
    place, targets, capped, totals, weight, grad_out, turned_out, far_out,
    weight_held, far_held, weight_sems, out_sems,
):
    core, position = place[0], place[3]

    def arrival(j):
        columns = step_columns(j)
        return pltpu.make_async_copy(weight.at[:, columns], weight_held.at[:, columns], weight_sems.at[j])

    def leaving(j):
        columns = step_columns(j)
        return pltpu.make_async_copy(far_held.at[:, columns], far_out.at[:, columns], out_sems.at[j])

    steps(lambda j: arrival(j).start())
    log_total = cap_value + jnp.log(totals[0:1, :])
    mean_logit = totals[1:2, :] / totals[0:1, :]

    def gradient(k):
        rows = pl.ds(pl.multiple_of(k * 128, 128), 128)
        values = capped[rows, :]
        probs = jnp.exp(values - log_total)
        entry = position * VOCAB_ROWS + k * 128 + lax.broadcasted_iota(jnp.int32, values.shape, 0)
        hit = (targets[...] == entry).astype(jnp.float32)
        raw_grad = probs - hit + entropy_weight * probs * (values - mean_logit)
        ratio = values / cap_value
        grad = raw_grad * (1.0 - ratio * ratio)
        grad_out[rows, :] = grad.astype(jnp.bfloat16)
        turned_out[:, :, :, rows] = grad.T.astype(jnp.bfloat16).reshape(8, 2, 32, 128)

    steps(gradient, 0, VOCAB_ROWS // 128)

    def multiply(j):
        arrival(j).wait()
        columns = step_columns(j)
        rows = turned_out[:, 1 - core].reshape(NEAR, VOCAB_ROWS)
        far_held[:, columns] = jnp.dot(
            rows, weight_held[:, columns], preferred_element_type=jnp.float32
        ).astype(jnp.bfloat16)
        leaving(j).start()

    steps(multiply)
    steps(lambda j: leaving(j).wait())


def far_gradient(place, targets, capped, totals, weight):
    return pl.pallas_call(
        far_kernel,
        out_shape=(
            jax.ShapeDtypeStruct((VOCAB_ROWS, TOKENS), jnp.bfloat16),
            jax.ShapeDtypeStruct((8, 2, 32, VOCAB_ROWS), jnp.bfloat16),
            jax.ShapeDtypeStruct((NEAR, WIDTH), jnp.bfloat16),
        ),
        in_specs=[SCALARS, IN_VMEM, IN_VMEM, IN_VMEM, IN_HBM],
        out_specs=(IN_VMEM, IN_VMEM, ANYWHERE),
        scratch_shapes=[
            pltpu.VMEM((VOCAB_ROWS, WIDTH), jnp.bfloat16),
            pltpu.VMEM((NEAR, WIDTH), jnp.bfloat16),
            pltpu.SemaphoreType.DMA((STEPS,)),
            pltpu.SemaphoreType.DMA((STEPS,)),
        ],
        compiler_params=pltpu.CompilerParams(vmem_limit_bytes=55 << 20),
        cost_estimate=pl.CostEstimate(
            flops=2 * VOCAB_ROWS * NEAR * WIDTH, bytes_accessed=9 << 20, transcendentals=1 << 18
        ),
        name="far_gradient",
    )(place, targets, capped, totals, weight)


def near_kernel(place, turned, weight, arrived, gathered, *rest):
    sends, gain_out = rest[:8], rest[8]
    weight_held, arrived_held, rows_held, first_held, second_held, in_sems, out_sems = rest[9:]
    core, y, x = place[0], place[1], place[2]

    def arrivals(j):
        columns = step_columns(j)
        return [
            pltpu.make_async_copy(weight.at[:, columns], weight_held.at[:, columns], in_sems.at[0, j]),
            pltpu.make_async_copy(arrived.at[:, columns], arrived_held.at[:, columns], in_sems.at[1, j]),
            pltpu.make_async_copy(
                gathered.at[:, core, :, columns], rows_held.at[:, :, columns], in_sems.at[2, j]
            ),
        ]

    def begin(j):
        for copy in arrivals(j):
            copy.start()

    def multiply(half, held, j):
        for copy in arrivals(j):
            copy.wait()
        columns = step_columns(j)
        rows = turned[:, core].reshape(NEAR, VOCAB_ROWS)
        part = jnp.dot(rows, weight_held[:, columns], preferred_element_type=jnp.float32)
        part = part + arrived_held[:, columns].astype(jnp.float32)
        gain_out[:, columns] = jnp.sum(
            part * rows_held[:, :, columns].reshape(NEAR, STEP).astype(jnp.float32), axis=0, keepdims=True
        )
        rounded = part.astype(jnp.bfloat16)
        own = step_columns(j - half * HALF_STEPS)
        for to_y in range(4):
            for to_x in range(4):
                up_y, up_x = lax.rem(to_y + 4 - y, 4), lax.rem(to_x + 4 - x, 4)
                outer, inner = (up_y, up_x) if half == 0 else (up_x, up_y)
                row = ((to_x % 2 * 4 + to_y) * 2 + to_x // 2) * PIECE
                held[outer, inner, :, own] = rounded[row : row + PIECE]

    steps(begin)
    leaving = []
    for half, held in ((0, first_held), (1, second_held)):
        first = half * HALF_STEPS
        steps(lambda j, half=half, held=held: multiply(half, held, j), first, first + HALF_STEPS)
        for k in range(4):
            copy = pltpu.make_async_copy(held.at[k], sends[half * 4 + k], out_sems.at[half * 4 + k])
            copy.start()
            leaving.append(copy)
    for copy in leaving:
        copy.wait()


def near_gradient(place, turned, weight, arrived, gathered):
    outs = pl.pallas_call(
        near_kernel,
        out_shape=[jax.ShapeDtypeStruct((4, PIECE, HALF), jnp.bfloat16)] * 8
        + [jax.ShapeDtypeStruct((1, WIDTH), jnp.float32)],
        in_specs=[SCALARS, IN_VMEM, IN_HBM, ANYWHERE, IN_HBM],
        out_specs=[ANYWHERE] * 8 + [IN_VMEM],
        scratch_shapes=[
            pltpu.VMEM((VOCAB_ROWS, WIDTH), jnp.bfloat16),
            pltpu.VMEM((NEAR, WIDTH), jnp.bfloat16),
            pltpu.VMEM((8, 32, WIDTH), jnp.bfloat16),
            pltpu.VMEM((4, 4, PIECE, HALF), jnp.bfloat16),
            pltpu.VMEM((4, 4, PIECE, HALF), jnp.bfloat16),
            pltpu.SemaphoreType.DMA((3, STEPS)),
            pltpu.SemaphoreType.DMA((8,)),
        ],
        compiler_params=pltpu.CompilerParams(vmem_limit_bytes=45 << 20),
        cost_estimate=pl.CostEstimate(
            flops=2 * VOCAB_ROWS * NEAR * WIDTH, bytes_accessed=12 << 20, transcendentals=0
        ),
        name="near_gradient",
    )(place, turned, weight, arrived, gathered)
    return outs[:4], outs[4:8], outs[8]


def weight_kernel(grad, gathered, out, rows_held, out_held, in_sems, out_sems):
    def arrival(j):
        columns = step_columns(j)
        return pltpu.make_async_copy(gathered.at[:, columns], rows_held.at[:, columns], in_sems.at[j])

    def leaving(j):
        columns = step_columns(j)
        return pltpu.make_async_copy(out_held.at[:, columns], out.at[:, columns], out_sems.at[j])

    def multiply(j):
        arrival(j).wait()
        columns = step_columns(j)
        out_held[:, columns] = jnp.dot(
            grad[...], rows_held[:, columns], preferred_element_type=jnp.float32
        ).astype(jnp.bfloat16)
        leaving(j).start()

    steps(lambda j: arrival(j).start())
    steps(multiply)
    steps(lambda j: leaving(j).wait())


def weight_gradient(grad, gathered):
    return pl.pallas_call(
        weight_kernel,
        out_shape=jax.ShapeDtypeStruct((VOCAB_ROWS, WIDTH), jnp.bfloat16),
        in_specs=[IN_VMEM, IN_HBM],
        out_specs=IN_HBM,
        scratch_shapes=[
            pltpu.VMEM((TOKENS, WIDTH), jnp.bfloat16),
            pltpu.VMEM((VOCAB_ROWS, WIDTH), jnp.bfloat16),
            pltpu.SemaphoreType.DMA((STEPS,)),
            pltpu.SemaphoreType.DMA((STEPS,)),
        ],
        compiler_params=pltpu.CompilerParams(vmem_limit_bytes=58 << 20),
        cost_estimate=pl.CostEstimate(
            flops=2 * VOCAB_ROWS * TOKENS * WIDTH, bytes_accessed=10 << 20, transcendentals=0
        ),
        name="weight_gradient",
    )(grad, gathered)


def on_device(hidden, norm_gain, weight, targets):
    core, y, position = lax.axis_index("core"), lax.axis_index("y"), lax.axis_index(AXES)
    x = lax.axis_index("x_hi") * 2 + lax.axis_index("x_lo")
    place = jnp.stack([core, y, x, position]).astype(jnp.int32)
    ids = targets.reshape(1, TOKENS)

    values = hidden.astype(jnp.float32)
    inverse = lax.rsqrt(jnp.mean(values * values, axis=-1, keepdims=True) + epsilon)
    unit_rows = values * inverse
    normed = (unit_rows * norm_gain).astype(jnp.bfloat16)

    line = gather_over(normed, "z", 8).reshape(PIECE, WIDTH)
    first_row = jnp.stack(gather_ring(line[:, :HALF], shift_x))
    second_row = jnp.stack(gather_ring(line[:, HALF:], shift_y))
    near_blocks = gather_ring(first_row, shift_y) + gather_ring(second_row, shift_x)
    arrived_blocks = lax.optimization_barrier(near_blocks[1:4] + near_blocks[5:])
    near_blocks = [near_blocks[0], *arrived_blocks[:3], near_blocks[4], *arrived_blocks[3:]]
    far_blocks = [swap_cores(block) for block in near_blocks]

    gathered, capped, stats = forward(place, ids, weight, near_blocks + far_blocks)
    stats = stats + swap_cores(stats)
    stats = sum_over(stats, PLANE, 16)
    stats = sum_over(stats, "z", 8)

    grad, turned, far_part = far_gradient(place, ids, capped, stats, weight)
    arrived = swap_cores(far_part)
    first_sends, second_sends, gain_part = near_gradient(
        place, turned, weight, arrived, gathered.reshape(8, 2, 32, WIDTH)
    )
    first_parts = send_ring(first_sends, shift_y)
    second_parts = send_ring(second_sends, shift_x)
    gain_part, second_parts[3] = lax.optimization_barrier((gain_part, second_parts[3]))
    gain_part = sum_over(gain_part, PLANE, 16)
    first_half = total(first_parts).astype(jnp.bfloat16)
    second_half = total(second_parts).astype(jnp.bfloat16)
    first_line = total(send_ring([first_half[k] for k in range(4)], shift_x))
    second_line = total(send_ring([second_half[k] for k in range(4)], shift_y))
    line_part = jnp.concatenate([first_line, second_line], axis=1).astype(jnp.bfloat16)
    gain_high = lax.reduce_precision(gain_part, 8, 7)
    gain_rows = jnp.concatenate([gain_high, gain_part - gain_high], axis=0).astype(jnp.bfloat16)
    message = jnp.concatenate(
        [line_part.reshape(8, 2, WIDTH), jnp.broadcast_to(gain_rows[None], (8, 2, WIDTH))], axis=1
    )
    message, grad = lax.optimization_barrier((message, grad))
    line_parts = lax.all_to_all(message, "z", 0, 0, tiled=True)
    grad_weight = weight_gradient(grad, gathered)
    line_sum = jnp.sum(line_parts.astype(jnp.float32), axis=0)
    grad_normed = line_sum[:2]
    gain_part = line_sum[2] + line_sum[3]
    grad_gain = (gain_part + swap_cores(gain_part)) / norm_gain

    total_exp, total_weighted, target_logit = stats
    log_total = cap_value + jnp.log(total_exp)
    mean_logit = total_weighted / total_exp
    every_loss = log_total - target_logit - entropy_weight * (log_total - mean_logit)
    token_loss = lax.dynamic_slice_in_dim(every_loss, position * 2, 2, 0)
    scaled = norm_gain * grad_normed
    grad_hidden = (
        scaled - unit_rows * jnp.mean(scaled * unit_rows, axis=-1, keepdims=True)
    ) * inverse
    return (token_loss, grad_hidden, grad_weight, grad_gain)


def solution(mesh):
    fine = Mesh(mesh.devices.reshape(2, 4, 2, 2, 8), AXES)
    rows = P(AXES, None)
    return jax.shard_map(
        on_device,
        mesh=fine,
        in_specs=(rows, P(), rows, P()),
        out_specs=(P(AXES), rows, rows, P()),
        check_vma=False,
    )
```

profile of v0, /device:TPU:32, one launch (start us, length us, event | category | flops | bytes accessed | tf_op | source)
XLA Modules:
  0.0 167.7 jit_solution(6529897310600925912)
XLA Ops:
  2.4 16.3 %all_to_all.25 = bf16[8,2,4608]{2,1,0:T(2,128)(2,1)S(1)} all-to-all(bf16[8,2,4608]{2,1,0:T(2,128)(2,1)S(1)} %broadcast_in_dim.12), channel_id=1, replica_groups=mesh['x_lo'=2,'y'=4,'core'=2,'x_hi'=2,'z'=8] {'z'}, dimensions={0} | all-to-all | bytes 294912 | tf_op jit(solution)/shard_map/all_to_all | solution.py:42
  18.9 3.1 %collective-permute-start.1 = (bf16[16,2304]{1,0:T(8,128)(2,1)S(1)}, bf16[16,2304]{1,0:T(8,128)(2,1)S(1)}, u32[]{:S(2)}, u32[]{:S(2)}) collective-permute-start(bf16[16,2304]{1,0:T(8,128)(2,1)S(1)} %get-tuple-element.63), channel_id=1, source_target_pairs={{0,8},{128,136},{8,0},{136,128},{1,9},{129,137},{9,1},{137,129},{2... | collective-permute-start | bytes 221192 | tf_op jit(solution)/shard_map/ppermute | solution.py:33
  24.0 3.2 %collective-permute-start.7 = (bf16[16,2304]{1,0:T(8,128)(2,1)S(1)}, bf16[16,2304]{1,0:T(8,128)(2,1)S(1)}, u32[]{:S(2)}, u32[]{:S(2)}) collective-permute-start(bf16[16,2304]{1,0:T(8,128)(2,1)S(1)} %get-tuple-element.62), channel_id=1, source_target_pairs={{0,64},{32,96},{64,0},{96,32},{1,65},{33,97},{65,1},{97,33},{2,66}... | collective-permute-start | bytes 221192 | tf_op jit(solution)/shard_map/ppermute | solution.py:28
  30.4 2.9 %collective-permute-start.4 = (bf16[4,16,2304]{2,1,0:T(8,128)(2,1)S(1)}, bf16[4,16,2304]{2,1,0:T(8,128)(2,1)S(1)}, u32[]{:S(2)}, u32[]{:S(2)}) collective-permute-start(bf16[4,16,2304]{2,1,0:T(8,128)(2,1)S(1)} %pad_maximum_fusion.rest_0_), channel_id=1, source_target_pairs={{0,64},{32,96},{64,0},{96,32},{1,65},{33,97},{65,1},{97,33},{2,66}... | collective-permute-start | bytes 884744 | tf_op jit(solution)/shard_map/ppermute | solution.py:28
  35.9 3.2 %collective-permute-start.10 = (bf16[4,16,2304]{2,1,0:T(8,128)(2,1)S(1)}, bf16[4,16,2304]{2,1,0:T(8,128)(2,1)S(1)}, u32[]{:S(2)}, u32[]{:S(2)}) collective-permute-start(bf16[4,16,2304]{2,1,0:T(8,128)(2,1)S(1)} %pad_maximum_fusion.1.rest_4_), channel_id=1, source_target_pairs={{0,8},{128,136},{8,0},{136,128},{1,9},{129,137},{9,1},{137,129},{2... | collective-permute-start | bytes 884744 | tf_op jit(solution)/shard_map/ppermute | solution.py:33
  40.9 5.5 %collective-permute-start.9 = (bf16[4,16,2304]{2,1,0:T(8,128)(2,1)S(1)}, bf16[4,16,2304]{2,1,0:T(8,128)(2,1)S(1)}, u32[]{:S(2)}, u32[]{:S(2)}) collective-permute-start(bf16[4,16,2304]{2,1,0:T(8,128)(2,1)S(1)} %pad_maximum_fusion.1.rest_4_), channel_id=1, source_target_pairs={{0,136},{128,0},{8,128},{136,8},{1,137},{129,1},{9,129},{137,9},{2... | collective-permute-start | bytes 884744 | tf_op jit(solution)/shard_map/ppermute | solution.py:33
  47.6 3.1 %collective-permute-done.9.rest_5_ = bf16[4,16,2304]{2,1,0:T(8,128)(2,1)S(1)} collective-permute-done((bf16[4,16,2304]{2,1,0:T(8,128)(2,1)S(1)}, bf16[4,16,2304]{2,1,0:T(8,128)(2,1)S(1)}, u32[]{:S(2)}, u32[]{:S(2)}) %collective-permute-start.9) | collective-permute-done | bytes 294944 | tf_op jit(solution)/shard_map/ppermute | solution.py:33
  55.2 8.8 %forward.1 = (bf16[512,4608]{1,0:T(8,128)(2,1)}, f32[512,512]{1,0:T(8,128)}, f32[3,512]{1,0:T(4,128)S(1)}) custom-call(s32[4]{0:T(128)S(1)} %pad_add_fusion.place, s32[1,512]{1,0:T(1,128)S(1)} %bitcast.41, bf16[512,4608]{1,0:T(8,128)(2,1)} %weight.5, bf16[4,16,2304]{2,1,0:T(8,128)(2,1)S(1)} %pad_maximum_fusion.rest_0_, ...), custom_call_target="tpu_custom_call" | custom-call | flops 2415919104 | bytes 16777216 | tf_op jit(solution)/shard_map/forward/pallas_call | solution.py:152
  65.3 13.0 %all_to_all.26 = f32[16,3,512]{2,1,0:T(4,128)S(1)} all-to-all(f32[16,3,512]{2,1,0:T(4,128)S(1)} %broadcast_in_dim.13), channel_id=1, replica_groups=mesh['x_lo'=2,'y'=4,'core'=2,'x_hi'=2,'z'=8] {'x_lo','y','x_hi'}, dimensions={0} | all-to-all | bytes 196608 | tf_op jit(solution)/shard_map/all_to_all | solution.py:42
  78.3 10.4 %all_to_all.27 = f32[8,3,512]{2,1,0:T(4,128)S(1)} all-to-all(f32[8,3,512]{2,1,0:T(4,128)S(1)} %broadcast_in_dim.14), channel_id=1, replica_groups=mesh['x_lo'=2,'y'=4,'core'=2,'x_hi'=2,'z'=8] {'z'}, dimensions={0} | all-to-all | bytes 98304 | tf_op jit(solution)/shard_map/all_to_all | solution.py:42
  89.3 6.5 %far_gradient.1 = (bf16[512,512]{1,0:T(8,128)(2,1)}, bf16[8,2,32,512]{3,2,1,0:T(8,128)(2,1)}, bf16[256,4608]{1,0:T(8,128)(2,1)}) custom-call(s32[4]{0:T(128)} %copy-done.2, s32[1,512]{1,0:T(1,128)} %bitcast.40, f32[512,512]{1,0:T(8,128)} %get-tuple-element.36.capped, f32[3,512]{1,0:T(4,128)} %reduce_sum.58.totals, bf16[512,4608]{1,0:T(8,128)(2,1)} %weight.5), custom_call_target="tpu_custom_call" | custom-call | flops 1207959552 | bytes 9437184 | tf_op jit(solution)/shard_map/far_gradient/pallas_call | solution.py:223
  95.9 4.7 %collective-permute-done.21.arrived = bf16[256,4608]{1,0:T(8,128)(2,1)S(1)} collective-permute-done((bf16[256,4608]{1,0:T(8,128)(2,1)}, bf16[256,4608]{1,0:T(8,128)(2,1)S(1)}, u32[]{:S(2)}, u32[]{:S(2)}) %collective-permute-start.21) | collective-permute-done | bytes 2359328 | tf_op jit(solution)/shard_map/ppermute | solution.py:37
  101.7 5.0 %near_gradient.1 = (bf16[4,16,2304]{2,1,0:T(8,128)(2,1)S(1)}, bf16[4,16,2304]{2,1,0:T(8,128)(2,1)S(1)}, bf16[4,16,2304]{2,1,0:T(8,128)(2,1)S(1)}, bf16[4,16,2304...) custom-call(s32[4]{0:T(128)S(1)} %copy-done.3, ...), custom_call_target="tpu_custom_call" | custom-call | flops 1207959552 | bytes 12582912 | tf_op jit(solution)/shard_map/near_gradient/pallas_call | solution.py:298
  107.3 2.2 %collective-permute-start.23 = (bf16[4,16,2304]{2,1,0:T(8,128)(2,1)S(1)}, bf16[4,16,2304]{2,1,0:T(8,128)(2,1)S(1)}, u32[]{:S(2)}, u32[]{:S(2)}) collective-permute-start(bf16[4,16,2304]{2,1,0:T(8,128)(2,1)S(1)} %get-tuple-element.42), channel_id=1, source_target_pairs={{0,64},{32,96},{64,0},{96,32},{1,65},{33,97},{65,1},{97,33},{2,66}... | collective-permute-start | bytes 884744 | tf_op jit(solution)/shard_map/ppermute | solution.py:28
  111.2 2.2 %collective-permute-start.29 = (bf16[4,16,2304]{2,1,0:T(8,128)(2,1)S(1)}, bf16[4,16,2304]{2,1,0:T(8,128)(2,1)S(1)}, u32[]{:S(2)}, u32[]{:S(2)}) collective-permute-start(bf16[4,16,2304]{2,1,0:T(8,128)(2,1)S(1)} %get-tuple-element.46), channel_id=1, source_target_pairs={{0,8},{128,136},{8,0},{136,128},{1,9},{129,137},{9,1},{137,129},{2... | collective-permute-start | bytes 884744 | tf_op jit(solution)/shard_map/ppermute | solution.py:33
  113.3 10.1 %collective-permute-done.22 = bf16[4,16,2304]{2,1,0:T(8,128)(2,1)S(1)} collective-permute-done((bf16[4,16,2304]{2,1,0:T(8,128)(2,1)S(1)}, bf16[4,16,2304]{2,1,0:T(8,128)(2,1)S(1)}, u32[]{:S(2)}, u32[]{:S(2)}) %collective-permute-start.22) | collective-permute-done | bytes 294944 | tf_op jit(solution)/shard_map/ppermute | solution.py:28
  125.7 2.5 %collective-permute-start.27 = (bf16[16,2304]{1,0:T(8,128)(2,1)S(1)}, bf16[16,2304]{1,0:T(8,128)(2,1)S(1)}, u32[]{:S(2)}, u32[]{:S(2)}) collective-permute-start(bf16[16,2304]{1,0:T(8,128)(2,1)S(1)} %get-tuple-element.55), channel_id=1, source_target_pairs={{0,136},{128,0},{8,128},{136,8},{1,137},{129,1},{9,129},{137,9},{2... | collective-permute-start | bytes 221192 | tf_op jit(solution)/shard_map/ppermute | solution.py:33
  128.1 2.8 %collective-permute-done.30 = bf16[4,16,2304]{2,1,0:T(8,128)(2,1)S(1)} collective-permute-done((bf16[4,16,2304]{2,1,0:T(8,128)(2,1)S(1)}, bf16[4,16,2304]{2,1,0:T(8,128)(2,1)S(1)}, u32[]{:S(2)}, u32[]{:S(2)}) %collective-permute-start.30) | collective-permute-done | bytes 294944 | tf_op jit(solution)/shard_map/ppermute | solution.py:33
  133.2 3.2 %collective-permute-start.33 = (bf16[16,2304]{1,0:T(8,128)(2,1)S(1)}, bf16[16,2304]{1,0:T(8,128)(2,1)S(1)}, u32[]{:S(2)}, u32[]{:S(2)}) collective-permute-start(bf16[16,2304]{1,0:T(8,128)(2,1)S(1)} %get-tuple-element.58), channel_id=1, source_target_pairs={{0,96},{32,0},{64,32},{96,64},{1,97},{33,1},{65,33},{97,65},{2,98}... | collective-permute-start | bytes 221192 | tf_op jit(solution)/shard_map/ppermute | solution.py:28
  137.4 3.7 %all-to-all-start.3 = ((f32[16,1,4608]{2,1,0:T(1,128)}), f32[16,1,4608]{2,1,0:T(1,128)S(1)}, u32[]{:S(2)}, u32[]{:S(2)}) async-start(f32[16,1,4608]{2,1,0:T(1,128)} %broadcast_in_dim.16), calls=%async_computation.3 | async-start | bytes 589824 | tf_op jit(solution)/shard_map/all_to_all | solution.py:42
  141.0 3.5 %collective-permute-start.32 = (bf16[16,2304]{1,0:T(8,128)(2,1)S(1)}, bf16[16,2304]{1,0:T(8,128)(2,1)S(1)}, u32[]{:S(2)}, u32[]{:S(2)}) collective-permute-start(bf16[16,2304]{1,0:T(8,128)(2,1)S(1)} %get-tuple-element.59), channel_id=1, source_target_pairs={{0,64},{32,96},{64,0},{96,32},{1,65},{33,97},{65,1},{97,33},{2,66}... | collective-permute-start | bytes 221192 | tf_op jit(solution)/shard_map/ppermute | solution.py:28
  144.6 3.0 %collective-permute-done.32 = bf16[16,2304]{1,0:T(8,128)(2,1)S(1)} collective-permute-done((bf16[16,2304]{1,0:T(8,128)(2,1)S(1)}, bf16[16,2304]{1,0:T(8,128)(2,1)S(1)}, u32[]{:S(2)}, u32[]{:S(2)}) %collective-permute-start.32) | collective-permute-done | bytes 73760 | tf_op jit(solution)/shard_map/ppermute | solution.py:28
  151.2 4.8 %all-to-all-start.4 = ((bf16[8,4,4608]{2,1,0:T(4,128)(2,1)}), bf16[8,4,4608]{2,1,0:T(4,128)(2,1)S(1)}, u32[]{:S(2)}, u32[]{:S(2)}) async-start(bf16[8,4,4608]{2,1,0:T(4,128)(2,1)} %pad_maximum_fusion.2), calls=%async_computation.4 | async-start | bytes 589824 | tf_op jit(solution)/shard_map/all_to_all | solution.py:408
  156.6 6.7 %weight_gradient.1 = bf16[512,4608]{1,0:T(8,128)(2,1)} custom-call(bf16[512,512]{1,0:T(8,128)(2,1)} %get-tuple-element.53.grad, bf16[512,4608]{1,0:T(8,128)(2,1)} %get-tuple-element.39.gathered), custom_call_target="tpu_custom_call" | custom-call | flops 2415919104 | bytes 10485760 | tf_op jit(solution)/shard_map/weight_gradient/pallas_call | solution.py:345
  (108 shorter events, 36.7 us)
Async XLA Ops:
  18.9 9.4 %collective-permute-start.1 = (bf16[16,2304]{1,0:T(8,128)(2,1)S(1)}, bf16[16,2304]{1,0:T(8,128)(2,1)S(1)}, u32[]{:S(2)}, u32[]{:S(2)}) collective-permute-start(bf16[16,2304]{1,0:T(8,128)(2,1)S(1)} %get-tuple-element.63), channel_id=1, source_target_pairs={{0,8},{128,136},{8,0},{136,128},{1,9},{129,137},{9,1},{137,129},{2... | collective-permute-start | bytes 221192 | tf_op jit(solution)/shard_map/ppermute | solution.py:33
  22.0 7.3 %collective-permute-start = (bf16[16,2304]{1,0:T(8,128)(2,1)S(1)}, bf16[16,2304]{1,0:T(8,128)(2,1)S(1)}, u32[]{:S(2)}, u32[]{:S(2)}) collective-permute-start(bf16[16,2304]{1,0:T(8,128)(2,1)S(1)} %get-tuple-element.63), channel_id=1, source_target_pairs={{0,136},{128,0},{8,128},{136,8},{1,137},{129,1},{9,129},{137,9},{2... | collective-permute-start | bytes 221192 | tf_op jit(solution)/shard_map/ppermute | solution.py:33
  24.0 9.3 %collective-permute-start.7 = (bf16[16,2304]{1,0:T(8,128)(2,1)S(1)}, bf16[16,2304]{1,0:T(8,128)(2,1)S(1)}, u32[]{:S(2)}, u32[]{:S(2)}) collective-permute-start(bf16[16,2304]{1,0:T(8,128)(2,1)S(1)} %get-tuple-element.62), channel_id=1, source_target_pairs={{0,64},{32,96},{64,0},{96,32},{1,65},{33,97},{65,1},{97,33},{2,66}... | collective-permute-start | bytes 221192 | tf_op jit(solution)/shard_map/ppermute | solution.py:28
  27.2 7.4 %collective-permute-start.6 = (bf16[16,2304]{1,0:T(8,128)(2,1)S(1)}, bf16[16,2304]{1,0:T(8,128)(2,1)S(1)}, u32[]{:S(2)}, u32[]{:S(2)}) collective-permute-start(bf16[16,2304]{1,0:T(8,128)(2,1)S(1)} %get-tuple-element.62), channel_id=1, source_target_pairs={{0,96},{32,0},{64,32},{96,64},{1,97},{33,1},{65,33},{97,65},{2,98}... | collective-permute-start | bytes 221192 | tf_op jit(solution)/shard_map/ppermute | solution.py:28
  29.3 11.6 %collective-permute-start.5 = (bf16[4,16,2304]{2,1,0:T(8,128)(2,1)S(1)}, bf16[4,16,2304]{2,1,0:T(8,128)(2,1)S(1)}, u32[]{:S(2)}, u32[]{:S(2)}) collective-permute-start(bf16[4,16,2304]{2,1,0:T(8,128)(2,1)S(1)} %pad_maximum_fusion.rest_0_), channel_id=1, source_target_pairs={{0,32},{32,64},{64,96},{96,0},{1,33},{33,65},{65,97},{97,1},{2,34}... | collective-permute-start | bytes 884744 | tf_op jit(solution)/shard_map/ppermute | solution.py:28
  30.4 16.1 %collective-permute-start.4 = (bf16[4,16,2304]{2,1,0:T(8,128)(2,1)S(1)}, bf16[4,16,2304]{2,1,0:T(8,128)(2,1)S(1)}, u32[]{:S(2)}, u32[]{:S(2)}) collective-permute-start(bf16[4,16,2304]{2,1,0:T(8,128)(2,1)S(1)} %pad_maximum_fusion.rest_0_), channel_id=1, source_target_pairs={{0,64},{32,96},{64,0},{96,32},{1,65},{33,97},{65,1},{97,33},{2,66}... | collective-permute-start | bytes 884744 | tf_op jit(solution)/shard_map/ppermute | solution.py:28
  33.3 13.2 %collective-permute-start.3 = (bf16[4,16,2304]{2,1,0:T(8,128)(2,1)S(1)}, bf16[4,16,2304]{2,1,0:T(8,128)(2,1)S(1)}, u32[]{:S(2)}, u32[]{:S(2)}) collective-permute-start(bf16[4,16,2304]{2,1,0:T(8,128)(2,1)S(1)} %pad_maximum_fusion.rest_0_), channel_id=1, source_target_pairs={{0,96},{32,0},{64,32},{96,64},{1,97},{33,1},{65,33},{97,65},{2,98}... | collective-permute-start | bytes 884744 | tf_op jit(solution)/shard_map/ppermute | solution.py:28
  34.7 12.3 %collective-permute-start.11 = (bf16[4,16,2304]{2,1,0:T(8,128)(2,1)S(1)}, bf16[4,16,2304]{2,1,0:T(8,128)(2,1)S(1)}, u32[]{:S(2)}, u32[]{:S(2)}) collective-permute-start(bf16[4,16,2304]{2,1,0:T(8,128)(2,1)S(1)} %pad_maximum_fusion.1.rest_4_), channel_id=1, source_target_pairs={{0,128},{128,8},{8,136},{136,0},{1,129},{129,9},{9,137},{137,1},{2... | collective-permute-start | bytes 884744 | tf_op jit(solution)/shard_map/ppermute | solution.py:33
  35.9 11.7 %collective-permute-start.10 = (bf16[4,16,2304]{2,1,0:T(8,128)(2,1)S(1)}, bf16[4,16,2304]{2,1,0:T(8,128)(2,1)S(1)}, u32[]{:S(2)}, u32[]{:S(2)}) collective-permute-start(bf16[4,16,2304]{2,1,0:T(8,128)(2,1)S(1)} %pad_maximum_fusion.1.rest_4_), channel_id=1, source_target_pairs={{0,8},{128,136},{8,0},{136,128},{1,9},{129,137},{9,1},{137,129},{2... | collective-permute-start | bytes 884744 | tf_op jit(solution)/shard_map/ppermute | solution.py:33
  40.9 9.8 %collective-permute-start.9 = (bf16[4,16,2304]{2,1,0:T(8,128)(2,1)S(1)}, bf16[4,16,2304]{2,1,0:T(8,128)(2,1)S(1)}, u32[]{:S(2)}, u32[]{:S(2)}) collective-permute-start(bf16[4,16,2304]{2,1,0:T(8,128)(2,1)S(1)} %pad_maximum_fusion.1.rest_4_), channel_id=1, source_target_pairs={{0,136},{128,0},{8,128},{136,8},{1,137},{129,1},{9,129},{137,9},{2... | collective-permute-start | bytes 884744 | tf_op jit(solution)/shard_map/ppermute | solution.py:33
  106.7 16.7 %collective-permute-start.22 = (bf16[4,16,2304]{2,1,0:T(8,128)(2,1)S(1)}, bf16[4,16,2304]{2,1,0:T(8,128)(2,1)S(1)}, u32[]{:S(2)}, u32[]{:S(2)}) collective-permute-start(bf16[4,16,2304]{2,1,0:T(8,128)(2,1)S(1)} %get-tuple-element.41), channel_id=1, source_target_pairs={{0,32},{32,64},{64,96},{96,0},{1,33},{33,65},{65,97},{97,1},{2,34}... | collective-permute-start | bytes 884744 | tf_op jit(solution)/shard_map/ppermute | solution.py:28
  107.3 17.4 %collective-permute-start.23 = (bf16[4,16,2304]{2,1,0:T(8,128)(2,1)S(1)}, bf16[4,16,2304]{2,1,0:T(8,128)(2,1)S(1)}, u32[]{:S(2)}, u32[]{:S(2)}) collective-permute-start(bf16[4,16,2304]{2,1,0:T(8,128)(2,1)S(1)} %get-tuple-element.42), channel_id=1, source_target_pairs={{0,64},{32,96},{64,0},{96,32},{1,65},{33,97},{65,1},{97,33},{2,66}... | collective-permute-start | bytes 884744 | tf_op jit(solution)/shard_map/ppermute | solution.py:28
  109.4 15.2 %collective-permute-start.24 = (bf16[4,16,2304]{2,1,0:T(8,128)(2,1)S(1)}, bf16[4,16,2304]{2,1,0:T(8,128)(2,1)S(1)}, u32[]{:S(2)}, u32[]{:S(2)}) collective-permute-start(bf16[4,16,2304]{2,1,0:T(8,128)(2,1)S(1)} %get-tuple-element.43), channel_id=1, source_target_pairs={{0,96},{32,0},{64,32},{96,64},{1,97},{33,1},{65,33},{97,65},{2,98}... | collective-permute-start | bytes 884744 | tf_op jit(solution)/shard_map/ppermute | solution.py:28
  110.6 22.1 %collective-permute-start.28 = (bf16[4,16,2304]{2,1,0:T(8,128)(2,1)S(1)}, bf16[4,16,2304]{2,1,0:T(8,128)(2,1)S(1)}, u32[]{:S(2)}, u32[]{:S(2)}) collective-permute-start(bf16[4,16,2304]{2,1,0:T(8,128)(2,1)S(1)} %get-tuple-element.45), channel_id=1, source_target_pairs={{0,128},{128,8},{8,136},{136,0},{1,129},{129,9},{9,137},{137,1},{2... | collective-permute-start | bytes 884744 | tf_op jit(solution)/shard_map/ppermute | solution.py:33
  111.2 21.6 %collective-permute-start.29 = (bf16[4,16,2304]{2,1,0:T(8,128)(2,1)S(1)}, bf16[4,16,2304]{2,1,0:T(8,128)(2,1)S(1)}, u32[]{:S(2)}, u32[]{:S(2)}) collective-permute-start(bf16[4,16,2304]{2,1,0:T(8,128)(2,1)S(1)} %get-tuple-element.46), channel_id=1, source_target_pairs={{0,8},{128,136},{8,0},{136,128},{1,9},{129,137},{9,1},{137,129},{2... | collective-permute-start | bytes 884744 | tf_op jit(solution)/shard_map/ppermute | solution.py:33
  123.4 7.5 %collective-permute-start.30 = (bf16[4,16,2304]{2,1,0:T(8,128)(2,1)S(1)}, bf16[4,16,2304]{2,1,0:T(8,128)(2,1)S(1)}, u32[]{:S(2)}, u32[]{:S(2)}) collective-permute-start(bf16[4,16,2304]{2,1,0:T(8,128)(2,1)S(1)} %get-tuple-element.48), channel_id=1, source_target_pairs={{0,136},{128,0},{8,128},{136,8},{1,137},{129,1},{9,129},{137,9},{2... | collective-permute-start | bytes 884744 | tf_op jit(solution)/shard_map/ppermute | solution.py:33
  124.8 16.2 %collective-permute-start.25 = (bf16[16,2304]{1,0:T(8,128)(2,1)S(1)}, bf16[16,2304]{1,0:T(8,128)(2,1)S(1)}, u32[]{:S(2)}, u32[]{:S(2)}) collective-permute-start(bf16[16,2304]{1,0:T(8,128)(2,1)S(1)} %get-tuple-element.54), channel_id=1, source_target_pairs={{0,128},{128,8},{8,136},{136,0},{1,129},{129,9},{9,137},{137,1},{2... | collective-permute-start | bytes 221192 | tf_op jit(solution)/shard_map/ppermute | solution.py:33
  125.7 18.9 %collective-permute-start.27 = (bf16[16,2304]{1,0:T(8,128)(2,1)S(1)}, bf16[16,2304]{1,0:T(8,128)(2,1)S(1)}, u32[]{:S(2)}, u32[]{:S(2)}) collective-permute-start(bf16[16,2304]{1,0:T(8,128)(2,1)S(1)} %get-tuple-element.55), channel_id=1, source_target_pairs={{0,136},{128,0},{8,128},{136,8},{1,137},{129,1},{9,129},{137,9},{2... | collective-permute-start | bytes 221192 | tf_op jit(solution)/shard_map/ppermute | solution.py:33
  130.9 13.6 %collective-permute-start.26 = (bf16[16,2304]{1,0:T(8,128)(2,1)S(1)}, bf16[16,2304]{1,0:T(8,128)(2,1)S(1)}, u32[]{:S(2)}, u32[]{:S(2)}) collective-permute-start(bf16[16,2304]{1,0:T(8,128)(2,1)S(1)} %get-tuple-element.56), channel_id=1, source_target_pairs={{0,8},{128,136},{8,0},{136,128},{1,9},{129,137},{9,1},{137,129},{2... | collective-permute-start | bytes 221192 | tf_op jit(solution)/shard_map/ppermute | solution.py:33
  132.9 11.7 %collective-permute-start.31 = (bf16[16,2304]{1,0:T(8,128)(2,1)S(1)}, bf16[16,2304]{1,0:T(8,128)(2,1)S(1)}, u32[]{:S(2)}, u32[]{:S(2)}) collective-permute-start(bf16[16,2304]{1,0:T(8,128)(2,1)S(1)} %get-tuple-element.57), channel_id=1, source_target_pairs={{0,32},{32,64},{64,96},{96,0},{1,33},{33,65},{65,97},{97,1},{2,34}... | collective-permute-start | bytes 221192 | tf_op jit(solution)/shard_map/ppermute | solution.py:28
  133.2 11.4 %collective-permute-start.33 = (bf16[16,2304]{1,0:T(8,128)(2,1)S(1)}, bf16[16,2304]{1,0:T(8,128)(2,1)S(1)}, u32[]{:S(2)}, u32[]{:S(2)}) collective-permute-start(bf16[16,2304]{1,0:T(8,128)(2,1)S(1)} %get-tuple-element.58), channel_id=1, source_target_pairs={{0,96},{32,0},{64,32},{96,64},{1,97},{33,1},{65,33},{97,65},{2,98}... | collective-permute-start | bytes 221192 | tf_op jit(solution)/shard_map/ppermute | solution.py:28
  137.4 12.4 %all-to-all-start.3 = ((f32[16,1,4608]{2,1,0:T(1,128)}), f32[16,1,4608]{2,1,0:T(1,128)S(1)}, u32[]{:S(2)}, u32[]{:S(2)}) async-start(f32[16,1,4608]{2,1,0:T(1,128)} %broadcast_in_dim.16), calls=%async_computation.3 | async-start | bytes 589824 | tf_op jit(solution)/shard_map/all_to_all | solution.py:42
  141.0 6.5 %collective-permute-start.32 = (bf16[16,2304]{1,0:T(8,128)(2,1)S(1)}, bf16[16,2304]{1,0:T(8,128)(2,1)S(1)}, u32[]{:S(2)}, u32[]{:S(2)}) collective-permute-start(bf16[16,2304]{1,0:T(8,128)(2,1)S(1)} %get-tuple-element.59), channel_id=1, source_target_pairs={{0,64},{32,96},{64,0},{96,32},{1,65},{33,97},{65,1},{97,33},{2,66}... | collective-permute-start | bytes 221192 | tf_op jit(solution)/shard_map/ppermute | solution.py:28
  151.2 14.2 %all-to-all-start.4 = ((bf16[8,4,4608]{2,1,0:T(4,128)(2,1)}), bf16[8,4,4608]{2,1,0:T(4,128)(2,1)S(1)}, u32[]{:S(2)}, u32[]{:S(2)}) async-start(bf16[8,4,4608]{2,1,0:T(4,128)(2,1)} %pad_maximum_fusion.2), calls=%async_computation.4 | async-start | bytes 589824 | tf_op jit(solution)/shard_map/all_to_all | solution.py:408
  (20 other events, 159.7 us)
where the time goes:
time: 171 us; the launch traced here: 168 us
  starting transfers between devices  56.4 us (33%)
  blocking collectives  39.7 us (23%)
  waiting for transfers between devices  34.1 us (20%)
  Pallas kernels  26.9 us (16%)
  other arithmetic  6.63 us (4%)
  local copies, waits for them, and re-layouts  2.99 us (2%)
    all_to_all x3, blocking collectives, gather_over(): return lax.all_to_all(copies, axes, 0, 0, tiled=True)  39.7 us
    ppermute x12, starting transfers between devices, shift_x(): return lax.ppermute(block, ('x_lo', 'x_hi'), pairs)  24.2 us
    ppermute x12, starting transfers between devices, shift_y(): return lax.ppermute(block, 'y', [(p, (p + step) % 4) for p in range(4)])  21.5 us
    ppermute x12, waiting for transfers between devices, shift_y(): return lax.ppermute(block, 'y', [(p, (p + step) % 4) for p in range(4)])  14.9 us
    pallas_call x1, Pallas kernels, forward(): pl.pallas_call(forward_kernel, out_shape=(jax.ShapeDtypeStruct((TOKENS, W...  8.77 us
    ppermute x11, waiting for transfers between devices, swap_cores(): return lax.ppermute(block, 'core', [(0, 1), (1, 0)])  8.54 us
    pallas_call x1, Pallas kernels, weight_gradient(): pl.pallas_call(weight_kernel, out_shape=jax.ShapeDtypeStruct((VOCAB_ROWS,...  6.66 us
    ppermute x12, waiting for transfers between devices, shift_x(): return lax.ppermute(block, ('x_lo', 'x_hi'), pairs)  6.52 us
  transfers between devices with their start and end apart: 37, of which 17 were waited for; matrix products, arithmetic and copies ran while one was open for 2% of the time, Pallas kernels for 4%

commit v1 on v0

--- a/solution.py
+++ b/solution.py
@@ -235,7 +235,7 @@
             pltpu.SemaphoreType.DMA((STEPS,)),
             pltpu.SemaphoreType.DMA((STEPS,)),
         ],
-        compiler_params=pltpu.CompilerParams(vmem_limit_bytes=55 << 20),
+        compiler_params=pltpu.CompilerParams(vmem_limit_bytes=52 << 20),
         cost_estimate=pl.CostEstimate(
             flops=2 * VOCAB_ROWS * NEAR * WIDTH, bytes_accessed=9 << 20, transcendentals=1 << 18
         ),
@@ -353,7 +353,7 @@
             pltpu.SemaphoreType.DMA((STEPS,)),
             pltpu.SemaphoreType.DMA((STEPS,)),
         ],
-        compiler_params=pltpu.CompilerParams(vmem_limit_bytes=58 << 20),
+        compiler_params=pltpu.CompilerParams(vmem_limit_bytes=50 << 20),
         cost_estimate=pl.CostEstimate(
             flops=2 * VOCAB_ROWS * TOKENS * WIDTH, bytes_accessed=10 << 20, transcendentals=0
         ),
@@ -392,8 +392,9 @@
     )
     first_parts = send_ring(first_sends, shift_y)
     second_parts = send_ring(second_sends, shift_x)
-    gain_part, second_parts[3] = lax.optimization_barrier((gain_part, second_parts[3]))
+    gain_part, first_parts[2] = lax.optimization_barrier((gain_part, first_parts[2]))
     gain_part = sum_over(gain_part, PLANE, 16)
+    gain_part = gain_part + swap_cores(gain_part)
     first_half = total(first_parts).astype(jnp.bfloat16)
     second_half = total(second_parts).astype(jnp.bfloat16)
     first_line = total(send_ring([first_half[k] for k in range(4)], shift_x))
@@ -409,8 +410,7 @@
     grad_weight = weight_gradient(grad, gathered)
     line_sum = jnp.sum(line_parts.astype(jnp.float32), axis=0)
     grad_normed = line_sum[:2]
-    gain_part = line_sum[2] + line_sum[3]
-    grad_gain = (gain_part + swap_cores(gain_part)) / norm_gain
+    grad_gain = (line_sum[2] + line_sum[3]) / norm_gain
 
     total_exp, total_weighted, target_logit = stats
     log_total = cap_value + jnp.log(total_exp)

time: 171 us -> 157 us (0.918); the launches traced: 168 us -> 156 us
  waiting for transfers between devices: 34.1 us -> 24.9 us
  Pallas kernels: 26.9 us -> 24.9 us
    ppermute x12, waiting for transfers between devices: 14.9 us -> 9.92 us  [shift_y(): return lax.ppermute(block, 'y', [(p, (p + step) % 4) for p in range(4)])]
    ppermute x12, waiting for transfers between devices: 6.52 us -> 3.75 us  [shift_x(): return lax.ppermute(block, ('x_lo', 'x_hi'), pairs)]
    all_to_all x1, waiting for transfers between devices: 2.08 us -> 0.01 us  [gather_over(): return lax.all_to_all(copies, axes, 0, 0, tiled=True)]
  transfers between devices with their start and end apart: 37 -> 37, of which waited for: 17 -> 16; matrix products, arithmetic and copies ran while one was open for 2% -> 3% of each run, Pallas kernels for 4% -> 4%
where the time goes in v1:
time: 157 us; the launch traced here: 156 us
  starting transfers between devices  55.5 us (35%)
  blocking collectives  39.7 us (25%)
  waiting for transfers between devices  24.9 us (16%)
  Pallas kernels  24.9 us (16%)
  other arithmetic  8.12 us (5%)
  local copies, waits for them, and re-layouts  1.95 us (1%)
    all_to_all x3, blocking collectives, gather_over(): return lax.all_to_all(copies, axes, 0, 0, tiled=True)  39.7 us
    ppermute x12, starting transfers between devices, shift_x(): return lax.ppermute(block, ('x_lo', 'x_hi'), pairs)  24.4 us
    ppermute x12, starting transfers between devices, shift_y(): return lax.ppermute(block, 'y', [(p, (p + step) % 4) for p in range(4)])  20.4 us
    ppermute x12, waiting for transfers between devices, shift_y(): return lax.ppermute(block, 'y', [(p, (p + step) % 4) for p in range(4)])  9.92 us
    pallas_call x1, Pallas kernels, forward(): pl.pallas_call(forward_kernel, out_shape=(jax.ShapeDtypeStruct((TOKENS, W...  8.76 us
    ppermute x11, waiting for transfers between devices, swap_cores(): return lax.ppermute(block, 'core', [(0, 1), (1, 0)])  8.08 us
    pallas_call x1, Pallas kernels, weight_gradient(): pl.pallas_call(weight_kernel, out_shape=jax.ShapeDtypeStruct((VOCAB_ROWS,...  5.62 us
    pallas_call x1, Pallas kernels, far_gradient(): pl.pallas_call(far_kernel, out_shape=(jax.ShapeDtypeStruct((VOCAB_ROWS, T...  5.49 us
  transfers between devices with their start and end apart: 37, of which 16 were waited for; matrix products, arithmetic and copies ran while one was open for 3% of the time, Pallas kernels for 4%

profile of v1, /device:TPU:32, one launch (start us, length us, event | category | flops | bytes accessed | tf_op | source)
XLA Modules:
  0.0 156.0 jit_solution(2938045631550575510)
XLA Ops:
  2.4 16.3 %all_to_all.25 = bf16[8,2,4608]{2,1,0:T(2,128)(2,1)S(1)} all-to-all(bf16[8,2,4608]{2,1,0:T(2,128)(2,1)S(1)} %broadcast_in_dim.12), channel_id=1, replica_groups=mesh['x_lo'=2,'y'=4,'core'=2,'x_hi'=2,'z'=8] {'z'}, dimensions={0} | all-to-all | bytes 294912 | tf_op jit(solution)/shard_map/all_to_all | solution.py:42
  18.9 3.1 %collective-permute-start.1 = (bf16[16,2304]{1,0:T(8,128)(2,1)S(1)}, bf16[16,2304]{1,0:T(8,128)(2,1)S(1)}, u32[]{:S(2)}, u32[]{:S(2)}) collective-permute-start(bf16[16,2304]{1,0:T(8,128)(2,1)S(1)} %get-tuple-element.63), channel_id=1, source_target_pairs={{0,8},{128,136},{8,0},{136,128},{1,9},{129,137},{9,1},{137,129},{2... | collective-permute-start | bytes 221192 | tf_op jit(solution)/shard_map/ppermute | solution.py:33
  24.0 3.2 %collective-permute-start.7 = (bf16[16,2304]{1,0:T(8,128)(2,1)S(1)}, bf16[16,2304]{1,0:T(8,128)(2,1)S(1)}, u32[]{:S(2)}, u32[]{:S(2)}) collective-permute-start(bf16[16,2304]{1,0:T(8,128)(2,1)S(1)} %get-tuple-element.62), channel_id=1, source_target_pairs={{0,64},{32,96},{64,0},{96,32},{1,65},{33,97},{65,1},{97,33},{2,66}... | collective-permute-start | bytes 221192 | tf_op jit(solution)/shard_map/ppermute | solution.py:28
  30.4 2.9 %collective-permute-start.4 = (bf16[4,16,2304]{2,1,0:T(8,128)(2,1)S(1)}, bf16[4,16,2304]{2,1,0:T(8,128)(2,1)S(1)}, u32[]{:S(2)}, u32[]{:S(2)}) collective-permute-start(bf16[4,16,2304]{2,1,0:T(8,128)(2,1)S(1)} %pad_maximum_fusion.rest_0_), channel_id=1, source_target_pairs={{0,64},{32,96},{64,0},{96,32},{1,65},{33,97},{65,1},{97,33},{2,66}... | collective-permute-start | bytes 884744 | tf_op jit(solution)/shard_map/ppermute | solution.py:28
  35.9 3.2 %collective-permute-start.10 = (bf16[4,16,2304]{2,1,0:T(8,128)(2,1)S(1)}, bf16[4,16,2304]{2,1,0:T(8,128)(2,1)S(1)}, u32[]{:S(2)}, u32[]{:S(2)}) collective-permute-start(bf16[4,16,2304]{2,1,0:T(8,128)(2,1)S(1)} %pad_maximum_fusion.1.rest_4_), channel_id=1, source_target_pairs={{0,8},{128,136},{8,0},{136,128},{1,9},{129,137},{9,1},{137,129},{2... | collective-permute-start | bytes 884744 | tf_op jit(solution)/shard_map/ppermute | solution.py:33
  39.1 1.8 %collective-permute-done.5.rest_3_ = bf16[4,16,2304]{2,1,0:T(8,128)(2,1)S(1)} collective-permute-done((bf16[4,16,2304]{2,1,0:T(8,128)(2,1)S(1)}, bf16[4,16,2304]{2,1,0:T(8,128)(2,1)S(1)}, u32[]{:S(2)}, u32[]{:S(2)}) %collective-permute-start.5) | collective-permute-done | bytes 294944 | tf_op jit(solution)/shard_map/ppermute | solution.py:28
  40.9 5.5 %collective-permute-start.9 = (bf16[4,16,2304]{2,1,0:T(8,128)(2,1)S(1)}, bf16[4,16,2304]{2,1,0:T(8,128)(2,1)S(1)}, u32[]{:S(2)}, u32[]{:S(2)}) collective-permute-start(bf16[4,16,2304]{2,1,0:T(8,128)(2,1)S(1)} %pad_maximum_fusion.1.rest_4_), channel_id=1, source_target_pairs={{0,136},{128,0},{8,128},{136,8},{1,137},{129,1},{9,129},{137,9},{2... | collective-permute-start | bytes 884744 | tf_op jit(solution)/shard_map/ppermute | solution.py:33
  47.6 3.1 %collective-permute-done.9.rest_5_ = bf16[4,16,2304]{2,1,0:T(8,128)(2,1)S(1)} collective-permute-done((bf16[4,16,2304]{2,1,0:T(8,128)(2,1)S(1)}, bf16[4,16,2304]{2,1,0:T(8,128)(2,1)S(1)}, u32[]{:S(2)}, u32[]{:S(2)}) %collective-permute-start.9) | collective-permute-done | bytes 294944 | tf_op jit(solution)/shard_map/ppermute | solution.py:33
  55.2 8.8 %forward.1 = (bf16[512,4608]{1,0:T(8,128)(2,1)}, f32[512,512]{1,0:T(8,128)}, f32[3,512]{1,0:T(4,128)S(1)}) custom-call(s32[4]{0:T(128)S(1)} %pad_add_fusion.place, s32[1,512]{1,0:T(1,128)S(1)} %bitcast.40, bf16[512,4608]{1,0:T(8,128)(2,1)} %weight.5, bf16[4,16,2304]{2,1,0:T(8,128)(2,1)S(1)} %pad_maximum_fusion.rest_0_, ...), custom_call_target="tpu_custom_call" | custom-call | flops 2415919104 | bytes 16777216 | tf_op jit(solution)/shard_map/forward/pallas_call | solution.py:152
  65.2 13.0 %all_to_all.26 = f32[16,3,512]{2,1,0:T(4,128)S(1)} all-to-all(f32[16,3,512]{2,1,0:T(4,128)S(1)} %broadcast_in_dim.13), channel_id=1, replica_groups=mesh['x_lo'=2,'y'=4,'core'=2,'x_hi'=2,'z'=8] {'x_lo','y','x_hi'}, dimensions={0} | all-to-all | bytes 196608 | tf_op jit(solution)/shard_map/all_to_all | solution.py:42
  78.3 10.4 %all_to_all.27 = f32[8,3,512]{2,1,0:T(4,128)S(1)} all-to-all(f32[8,3,512]{2,1,0:T(4,128)S(1)} %broadcast_in_dim.14), channel_id=1, replica_groups=mesh['x_lo'=2,'y'=4,'core'=2,'x_hi'=2,'z'=8] {'z'}, dimensions={0} | all-to-all | bytes 98304 | tf_op jit(solution)/shard_map/all_to_all | solution.py:42
  88.7 5.5 %far_gradient.1 = (bf16[512,512]{1,0:T(8,128)(2,1)S(1)}, bf16[8,2,32,512]{3,2,1,0:T(8,128)(2,1)S(1)}, bf16[256,4608]{1,0:T(8,128)(2,1)}) custom-call(s32[4]{0:T(128)S(1)} %pad_add_fusion.place, s32[1,512]{1,0:T(1,128)S(1)} %bitcast.41, f32[512,512]{1,0:T(8,128)} %get-tuple-element.36.capped, f32[3,512]{1,0:T(4,128)S(1)} %reduce_sum.58.totals, ...), custom_call_target="tpu_custom_call" | custom-call | flops 1207959552 | bytes 9437184 | tf_op jit(solution)/shard_map/far_gradient/pallas_call | solution.py:223
  94.3 4.7 %collective-permute-done.21.arrived = bf16[256,4608]{1,0:T(8,128)(2,1)S(1)} collective-permute-done((bf16[256,4608]{1,0:T(8,128)(2,1)}, bf16[256,4608]{1,0:T(8,128)(2,1)S(1)}, u32[]{:S(2)}, u32[]{:S(2)}) %collective-permute-start.21) | collective-permute-done | bytes 2359328 | tf_op jit(solution)/shard_map/ppermute | solution.py:37
  99.0 5.0 %near_gradient.1 = (bf16[4,16,2304]{2,1,0:T(8,128)(2,1)S(1)}, bf16[4,16,2304]{2,1,0:T(8,128)(2,1)S(1)}, bf16[4,16,2304]{2,1,0:T(8,128)(2,1)S(1)}, bf16[4,16,2304...) custom-call(s32[4]{0:T(128)S(1)} %pad_add_fusion.place, ...), custom_call_target="tpu_custom_call" | custom-call | flops 1207959552 | bytes 12582912 | tf_op jit(solution)/shard_map/near_gradient/pallas_call | solution.py:298
  106.2 2.4 %collective-permute-start.24 = (bf16[4,16,2304]{2,1,0:T(8,128)(2,1)S(1)}, bf16[4,16,2304]{2,1,0:T(8,128)(2,1)}, u32[]{:S(2)}, u32[]{:S(2)}) collective-permute-start(bf16[4,16,2304]{2,1,0:T(8,128)(2,1)S(1)} %get-tuple-element.45), channel_id=1, source_target_pairs={{0,96},{32,0},{64,32},{96,64},{1,97},{33,1},{65,33},{97,65},{2,98}... | collective-permute-start | bytes 884744 | tf_op jit(solution)/shard_map/ppermute | solution.py:28
  109.1 2.2 %collective-permute-start.29 = (bf16[4,16,2304]{2,1,0:T(8,128)(2,1)S(1)}, bf16[4,16,2304]{2,1,0:T(8,128)(2,1)S(1)}, u32[]{:S(2)}, u32[]{:S(2)}) collective-permute-start(bf16[4,16,2304]{2,1,0:T(8,128)(2,1)S(1)} %get-tuple-element.48), channel_id=1, source_target_pairs={{0,8},{128,136},{8,0},{136,128},{1,9},{129,137},{9,1},{137,129},{2... | collective-permute-start | bytes 884744 | tf_op jit(solution)/shard_map/ppermute | solution.py:33
  111.3 4.4 %collective-permute-done.23 = bf16[4,16,2304]{2,1,0:T(8,128)(2,1)} collective-permute-done((bf16[4,16,2304]{2,1,0:T(8,128)(2,1)S(1)}, bf16[4,16,2304]{2,1,0:T(8,128)(2,1)}, u32[]{:S(2)}, u32[]{:S(2)}) %collective-permute-start.23) | collective-permute-done | bytes 294944 | tf_op jit(solution)/shard_map/ppermute | solution.py:28
  117.8 3.5 %all-to-all-start.3 = ((f32[16,1,4608]{2,1,0:T(1,128)}), f32[16,1,4608]{2,1,0:T(1,128)S(1)}, u32[]{:S(2)}, u32[]{:S(2)}) async-start(f32[16,1,4608]{2,1,0:T(1,128)} %broadcast_in_dim.16), calls=%async_computation.3 | async-start | bytes 589824 | tf_op jit(solution)/shard_map/all_to_all | solution.py:42
  122.7 1.9 %collective-permute-start.25 = (bf16[16,2304]{1,0:T(8,128)(2,1)S(1)}, bf16[16,2304]{1,0:T(8,128)(2,1)S(1)}, u32[]{:S(2)}, u32[]{:S(2)}) collective-permute-start(bf16[16,2304]{1,0:T(8,128)(2,1)S(1)} %get-tuple-element.54), channel_id=1, source_target_pairs={{0,128},{128,8},{8,136},{136,0},{1,129},{129,9},{9,137},{137,1},{2... | collective-permute-start | bytes 221192 | tf_op jit(solution)/shard_map/ppermute | solution.py:33
  126.0 2.1 %collective-permute-start.26 = (bf16[16,2304]{1,0:T(8,128)(2,1)S(1)}, bf16[16,2304]{1,0:T(8,128)(2,1)S(1)}, u32[]{:S(2)}, u32[]{:S(2)}) collective-permute-start(bf16[16,2304]{1,0:T(8,128)(2,1)S(1)} %get-tuple-element.56), channel_id=1, source_target_pairs={{0,8},{128,136},{8,0},{136,128},{1,9},{129,137},{9,1},{137,129},{2... | collective-permute-start | bytes 221192 | tf_op jit(solution)/shard_map/ppermute | solution.py:33
  135.4 3.3 %collective-permute-done.32 = bf16[16,2304]{1,0:T(8,128)(2,1)S(1)} collective-permute-done((bf16[16,2304]{1,0:T(8,128)(2,1)S(1)}, bf16[16,2304]{1,0:T(8,128)(2,1)S(1)}, u32[]{:S(2)}, u32[]{:S(2)}) %collective-permute-start.32) | collective-permute-done | bytes 73760 | tf_op jit(solution)/shard_map/ppermute | solution.py:28
  140.0 4.8 %all-to-all-start.4 = ((bf16[8,4,4608]{2,1,0:T(4,128)(2,1)}), bf16[8,4,4608]{2,1,0:T(4,128)(2,1)S(1)}, u32[]{:S(2)}, u32[]{:S(2)}) async-start(bf16[8,4,4608]{2,1,0:T(4,128)(2,1)} %pad_maximum_fusion.2), calls=%async_computation.4 | async-start | bytes 589824 | tf_op jit(solution)/shard_map/all_to_all | solution.py:409
  145.4 5.6 %weight_gradient.1 = bf16[512,4608]{1,0:T(8,128)(2,1)} custom-call(bf16[512,512]{1,0:T(8,128)(2,1)S(1)} %get-tuple-element.53.grad, bf16[512,4608]{1,0:T(8,128)(2,1)} %get-tuple-element.39.gathered), custom_call_target="tpu_custom_call" | custom-call | flops 2415919104 | bytes 10485760 | tf_op jit(solution)/shard_map/weight_gradient/pallas_call | solution.py:345
  151.0 3.2 %all-to-all-done.4 = bf16[8,4,4608]{2,1,0:T(4,128)(2,1)S(1)} async-done(((bf16[8,4,4608]{2,1,0:T(4,128)(2,1)}), bf16[8,4,4608]{2,1,0:T(4,128)(2,1)S(1)}, u32[]{:S(2)}, u32[]{:S(2)}) %all-to-all-start.4) | async-done | bytes 294944 | tf_op jit(solution)/shard_map/all_to_all | solution.py:409
  (103 shorter events, 35.2 us)
Async XLA Ops:
  18.9 9.4 %collective-permute-start.1 = (bf16[16,2304]{1,0:T(8,128)(2,1)S(1)}, bf16[16,2304]{1,0:T(8,128)(2,1)S(1)}, u32[]{:S(2)}, u32[]{:S(2)}) collective-permute-start(bf16[16,2304]{1,0:T(8,128)(2,1)S(1)} %get-tuple-element.63), channel_id=1, source_target_pairs={{0,8},{128,136},{8,0},{136,128},{1,9},{129,137},{9,1},{137,129},{2... | collective-permute-start | bytes 221192 | tf_op jit(solution)/shard_map/ppermute | solution.py:33
  22.0 7.3 %collective-permute-start = (bf16[16,2304]{1,0:T(8,128)(2,1)S(1)}, bf16[16,2304]{1,0:T(8,128)(2,1)S(1)}, u32[]{:S(2)}, u32[]{:S(2)}) collective-permute-start(bf16[16,2304]{1,0:T(8,128)(2,1)S(1)} %get-tuple-element.63), channel_id=1, source_target_pairs={{0,136},{128,0},{8,128},{136,8},{1,137},{129,1},{9,129},{137,9},{2... | collective-permute-start | bytes 221192 | tf_op jit(solution)/shard_map/ppermute | solution.py:33
  23.1 6.1 %collective-permute-start.2 = (bf16[16,2304]{1,0:T(8,128)(2,1)S(1)}, bf16[16,2304]{1,0:T(8,128)(2,1)S(1)}, u32[]{:S(2)}, u32[]{:S(2)}) collective-permute-start(bf16[16,2304]{1,0:T(8,128)(2,1)S(1)} %get-tuple-element.63), channel_id=1, source_target_pairs={{0,128},{128,8},{8,136},{136,0},{1,129},{129,9},{9,137},{137,1},{2... | collective-permute-start | bytes 221192 | tf_op jit(solution)/shard_map/ppermute | solution.py:33
  24.0 9.3 %collective-permute-start.7 = (bf16[16,2304]{1,0:T(8,128)(2,1)S(1)}, bf16[16,2304]{1,0:T(8,128)(2,1)S(1)}, u32[]{:S(2)}, u32[]{:S(2)}) collective-permute-start(bf16[16,2304]{1,0:T(8,128)(2,1)S(1)} %get-tuple-element.62), channel_id=1, source_target_pairs={{0,64},{32,96},{64,0},{96,32},{1,65},{33,97},{65,1},{97,33},{2,66}... | collective-permute-start | bytes 221192 | tf_op jit(solution)/shard_map/ppermute | solution.py:28
  27.2 7.4 %collective-permute-start.6 = (bf16[16,2304]{1,0:T(8,128)(2,1)S(1)}, bf16[16,2304]{1,0:T(8,128)(2,1)S(1)}, u32[]{:S(2)}, u32[]{:S(2)}) collective-permute-start(bf16[16,2304]{1,0:T(8,128)(2,1)S(1)} %get-tuple-element.62), channel_id=1, source_target_pairs={{0,96},{32,0},{64,32},{96,64},{1,97},{33,1},{65,33},{97,65},{2,98}... | collective-permute-start | bytes 221192 | tf_op jit(solution)/shard_map/ppermute | solution.py:28
  28.3 6.4 %collective-permute-start.8 = (bf16[16,2304]{1,0:T(8,128)(2,1)S(1)}, bf16[16,2304]{1,0:T(8,128)(2,1)S(1)}, u32[]{:S(2)}, u32[]{:S(2)}) collective-permute-start(bf16[16,2304]{1,0:T(8,128)(2,1)S(1)} %get-tuple-element.62), channel_id=1, source_target_pairs={{0,32},{32,64},{64,96},{96,0},{1,33},{33,65},{65,97},{97,1},{2,34}... | collective-permute-start | bytes 221192 | tf_op jit(solution)/shard_map/ppermute | solution.py:28
  29.3 11.6 %collective-permute-start.5 = (bf16[4,16,2304]{2,1,0:T(8,128)(2,1)S(1)}, bf16[4,16,2304]{2,1,0:T(8,128)(2,1)S(1)}, u32[]{:S(2)}, u32[]{:S(2)}) collective-permute-start(bf16[4,16,2304]{2,1,0:T(8,128)(2,1)S(1)} %pad_maximum_fusion.rest_0_), channel_id=1, source_target_pairs={{0,32},{32,64},{64,96},{96,0},{1,33},{33,65},{65,97},{97,1},{2,34}... | collective-permute-start | bytes 884744 | tf_op jit(solution)/shard_map/ppermute | solution.py:28
  30.4 16.1 %collective-permute-start.4 = (bf16[4,16,2304]{2,1,0:T(8,128)(2,1)S(1)}, bf16[4,16,2304]{2,1,0:T(8,128)(2,1)S(1)}, u32[]{:S(2)}, u32[]{:S(2)}) collective-permute-start(bf16[4,16,2304]{2,1,0:T(8,128)(2,1)S(1)} %pad_maximum_fusion.rest_0_), channel_id=1, source_target_pairs={{0,64},{32,96},{64,0},{96,32},{1,65},{33,97},{65,1},{97,33},{2,66}... | collective-permute-start | bytes 884744 | tf_op jit(solution)/shard_map/ppermute | solution.py:28
  33.3 13.2 %collective-permute-start.3 = (bf16[4,16,2304]{2,1,0:T(8,128)(2,1)S(1)}, bf16[4,16,2304]{2,1,0:T(8,128)(2,1)S(1)}, u32[]{:S(2)}, u32[]{:S(2)}) collective-permute-start(bf16[4,16,2304]{2,1,0:T(8,128)(2,1)S(1)} %pad_maximum_fusion.rest_0_), channel_id=1, source_target_pairs={{0,96},{32,0},{64,32},{96,64},{1,97},{33,1},{65,33},{97,65},{2,98}... | collective-permute-start | bytes 884744 | tf_op jit(solution)/shard_map/ppermute | solution.py:28
  34.7 12.3 %collective-permute-start.11 = (bf16[4,16,2304]{2,1,0:T(8,128)(2,1)S(1)}, bf16[4,16,2304]{2,1,0:T(8,128)(2,1)S(1)}, u32[]{:S(2)}, u32[]{:S(2)}) collective-permute-start(bf16[4,16,2304]{2,1,0:T(8,128)(2,1)S(1)} %pad_maximum_fusion.1.rest_4_), channel_id=1, source_target_pairs={{0,128},{128,8},{8,136},{136,0},{1,129},{129,9},{9,137},{137,1},{2... | collective-permute-start | bytes 884744 | tf_op jit(solution)/shard_map/ppermute | solution.py:33
  35.9 11.7 %collective-permute-start.10 = (bf16[4,16,2304]{2,1,0:T(8,128)(2,1)S(1)}, bf16[4,16,2304]{2,1,0:T(8,128)(2,1)S(1)}, u32[]{:S(2)}, u32[]{:S(2)}) collective-permute-start(bf16[4,16,2304]{2,1,0:T(8,128)(2,1)S(1)} %pad_maximum_fusion.1.rest_4_), channel_id=1, source_target_pairs={{0,8},{128,136},{8,0},{136,128},{1,9},{129,137},{9,1},{137,129},{2... | collective-permute-start | bytes 884744 | tf_op jit(solution)/shard_map/ppermute | solution.py:33
  40.9 9.8 %collective-permute-start.9 = (bf16[4,16,2304]{2,1,0:T(8,128)(2,1)S(1)}, bf16[4,16,2304]{2,1,0:T(8,128)(2,1)S(1)}, u32[]{:S(2)}, u32[]{:S(2)}) collective-permute-start(bf16[4,16,2304]{2,1,0:T(8,128)(2,1)S(1)} %pad_maximum_fusion.1.rest_4_), channel_id=1, source_target_pairs={{0,136},{128,0},{8,128},{136,8},{1,137},{129,1},{9,129},{137,9},{2... | collective-permute-start | bytes 884744 | tf_op jit(solution)/shard_map/ppermute | solution.py:33
  104.0 11.6 %collective-permute-start.23 = (bf16[4,16,2304]{2,1,0:T(8,128)(2,1)S(1)}, bf16[4,16,2304]{2,1,0:T(8,128)(2,1)}, u32[]{:S(2)}, u32[]{:S(2)}) collective-permute-start(bf16[4,16,2304]{2,1,0:T(8,128)(2,1)S(1)} %get-tuple-element.43), channel_id=1, source_target_pairs={{0,64},{32,96},{64,0},{96,32},{1,65},{33,97},{65,1},{97,33},{2,66}... | collective-permute-start | bytes 884744 | tf_op jit(solution)/shard_map/ppermute | solution.py:28
  105.3 16.1 %collective-permute-start.22 = (bf16[4,16,2304]{2,1,0:T(8,128)(2,1)S(1)}, bf16[4,16,2304]{2,1,0:T(8,128)(2,1)}, u32[]{:S(2)}, u32[]{:S(2)}) collective-permute-start(bf16[4,16,2304]{2,1,0:T(8,128)(2,1)S(1)} %get-tuple-element.41), channel_id=1, source_target_pairs={{0,32},{32,64},{64,96},{96,0},{1,33},{33,65},{65,97},{97,1},{2,34}... | collective-permute-start | bytes 884744 | tf_op jit(solution)/shard_map/ppermute | solution.py:28
  106.2 15.2 %collective-permute-start.24 = (bf16[4,16,2304]{2,1,0:T(8,128)(2,1)S(1)}, bf16[4,16,2304]{2,1,0:T(8,128)(2,1)}, u32[]{:S(2)}, u32[]{:S(2)}) collective-permute-start(bf16[4,16,2304]{2,1,0:T(8,128)(2,1)S(1)} %get-tuple-element.45), channel_id=1, source_target_pairs={{0,96},{32,0},{64,32},{96,64},{1,97},{33,1},{65,33},{97,65},{2,98}... | collective-permute-start | bytes 884744 | tf_op jit(solution)/shard_map/ppermute | solution.py:28
  108.5 17.5 %collective-permute-start.28 = (bf16[4,16,2304]{2,1,0:T(8,128)(2,1)S(1)}, bf16[4,16,2304]{2,1,0:T(8,128)(2,1)S(1)}, u32[]{:S(2)}, u32[]{:S(2)}) collective-permute-start(bf16[4,16,2304]{2,1,0:T(8,128)(2,1)S(1)} %get-tuple-element.47), channel_id=1, source_target_pairs={{0,128},{128,8},{8,136},{136,0},{1,129},{129,9},{9,137},{137,1},{2... | collective-permute-start | bytes 884744 | tf_op jit(solution)/shard_map/ppermute | solution.py:33
  109.1 19.0 %collective-permute-start.29 = (bf16[4,16,2304]{2,1,0:T(8,128)(2,1)S(1)}, bf16[4,16,2304]{2,1,0:T(8,128)(2,1)S(1)}, u32[]{:S(2)}, u32[]{:S(2)}) collective-permute-start(bf16[4,16,2304]{2,1,0:T(8,128)(2,1)S(1)} %get-tuple-element.48), channel_id=1, source_target_pairs={{0,8},{128,136},{8,0},{136,128},{1,9},{129,137},{9,1},{137,129},{2... | collective-permute-start | bytes 884744 | tf_op jit(solution)/shard_map/ppermute | solution.py:33
  115.6 12.5 %collective-permute-start.30 = (bf16[4,16,2304]{2,1,0:T(8,128)(2,1)S(1)}, bf16[4,16,2304]{2,1,0:T(8,128)(2,1)}, u32[]{:S(2)}, u32[]{:S(2)}) collective-permute-start(bf16[4,16,2304]{2,1,0:T(8,128)(2,1)S(1)} %get-tuple-element.49), channel_id=1, source_target_pairs={{0,136},{128,0},{8,128},{136,8},{1,137},{129,1},{9,129},{137,9},{2... | collective-permute-start | bytes 884744 | tf_op jit(solution)/shard_map/ppermute | solution.py:33
  117.8 16.8 %all-to-all-start.3 = ((f32[16,1,4608]{2,1,0:T(1,128)}), f32[16,1,4608]{2,1,0:T(1,128)S(1)}, u32[]{:S(2)}, u32[]{:S(2)}) async-start(f32[16,1,4608]{2,1,0:T(1,128)} %broadcast_in_dim.16), calls=%async_computation.3 | async-start | bytes 589824 | tf_op jit(solution)/shard_map/all_to_all | solution.py:42
  122.7 10.1 %collective-permute-start.25 = (bf16[16,2304]{1,0:T(8,128)(2,1)S(1)}, bf16[16,2304]{1,0:T(8,128)(2,1)S(1)}, u32[]{:S(2)}, u32[]{:S(2)}) collective-permute-start(bf16[16,2304]{1,0:T(8,128)(2,1)S(1)} %get-tuple-element.54), channel_id=1, source_target_pairs={{0,128},{128,8},{8,136},{136,0},{1,129},{129,9},{9,137},{137,1},{2... | collective-permute-start | bytes 221192 | tf_op jit(solution)/shard_map/ppermute | solution.py:33
  124.6 10.0 %collective-permute-start.27 = (bf16[16,2304]{1,0:T(8,128)(2,1)S(1)}, bf16[16,2304]{1,0:T(8,128)(2,1)S(1)}, u32[]{:S(2)}, u32[]{:S(2)}) collective-permute-start(bf16[16,2304]{1,0:T(8,128)(2,1)S(1)} %get-tuple-element.55), channel_id=1, source_target_pairs={{0,136},{128,0},{8,128},{136,8},{1,137},{129,1},{9,129},{137,9},{2... | collective-permute-start | bytes 221192 | tf_op jit(solution)/shard_map/ppermute | solution.py:33
  126.0 8.6 %collective-permute-start.26 = (bf16[16,2304]{1,0:T(8,128)(2,1)S(1)}, bf16[16,2304]{1,0:T(8,128)(2,1)S(1)}, u32[]{:S(2)}, u32[]{:S(2)}) collective-permute-start(bf16[16,2304]{1,0:T(8,128)(2,1)S(1)} %get-tuple-element.56), channel_id=1, source_target_pairs={{0,8},{128,136},{8,0},{136,128},{1,9},{129,137},{9,1},{137,129},{2... | collective-permute-start | bytes 221192 | tf_op jit(solution)/shard_map/ppermute | solution.py:33
  129.3 5.9 %collective-permute-start.31 = (bf16[16,2304]{1,0:T(8,128)(2,1)S(1)}, bf16[16,2304]{1,0:T(8,128)(2,1)S(1)}, u32[]{:S(2)}, u32[]{:S(2)}) collective-permute-start(bf16[16,2304]{1,0:T(8,128)(2,1)S(1)} %get-tuple-element.57), channel_id=1, source_target_pairs={{0,32},{32,64},{64,96},{96,0},{1,33},{33,65},{65,97},{97,1},{2,34}... | collective-permute-start | bytes 221192 | tf_op jit(solution)/shard_map/ppermute | solution.py:28
  140.0 14.2 %all-to-all-start.4 = ((bf16[8,4,4608]{2,1,0:T(4,128)(2,1)}), bf16[8,4,4608]{2,1,0:T(4,128)(2,1)S(1)}, u32[]{:S(2)}, u32[]{:S(2)}) async-start(bf16[8,4,4608]{2,1,0:T(4,128)(2,1)} %pad_maximum_fusion.2), calls=%async_computation.4 | async-start | bytes 589824 | tf_op jit(solution)/shard_map/all_to_all | solution.py:409
  (17 other events, 95.1 us)

commit v2 on v1

--- a/solution.py
+++ b/solution.py
@@ -14,23 +14,32 @@
 WIDTH = 4608
 HALF = WIDTH // 2
 TOKENS = 512
-NEAR = TOKENS // 2
 VOCAB_ROWS = 512
 PIECE = 16
 STEP = 768
 STEPS = WIDTH // STEP
 HALF_STEPS = HALF // STEP
 
-RING = (0, 2, 1, 3)
-
-
-def shift_y(block, step):
-    return lax.ppermute(block, "y", [(p, (p + step) % 4) for p in range(4)])
-
-
-def shift_x(block, step):
-    pairs = [(RING[p], RING[(p + step) % 4]) for p in range(4)]
-    return lax.ppermute(block, ("x_lo", "x_hi"), pairs)
+CROSS = ("x_lo", "y", "core", "x_hi")
+
+
+def cross_pairs(step, x_core):
+    index = lambda x, y, core: ((x % 2 * 4 + y) * 2 + core) * 2 + x // 2
+    pairs = []
+    for x in range(4):
+        for y in range(4):
+            for core in range(2):
+                to = ((x + step) % 4, y) if core == x_core else (x, (y + step) % 4)
+                pairs.append((index(x, y, core), index(*to, core)))
+    return pairs
+
+
+def shift_first(block, step):
+    return lax.ppermute(block, CROSS, cross_pairs(step, 0))
+
+
+def shift_second(block, step):
+    return lax.ppermute(block, CROSS, cross_pairs(step, 1))
 
 
 def swap_cores(block):
@@ -74,27 +83,30 @@
 
 
 def forward_kernel(place, targets, weight, *rest):
-    blocks = rest[:16]
-    gathered, capped_out, stats_out, weight_held, rows_held, logits, weight_sems, row_sems, out_sem = rest[16:]
+    blocks = rest[:8]
+    gathered, capped_out, stats_out, weight_held, rows_held, logits, weight_sems, row_sems, out_sem = rest[8:]
     core, y, x, position = place[0], place[1], place[2], place[3]
 
+    def half_columns(half):
+        return pl.ds(pl.multiple_of(half * HALF, HALF), HALF)
+
     def half_rows(half):
-        return rows_held.at[:, half * HALF : (half + 1) * HALF]
+        return rows_held.at[:, half_columns(half)]
 
     def weight_copy(j):
         columns = step_columns(j)
         return pltpu.make_async_copy(weight.at[:, columns], weight_held.at[:, columns], weight_sems.at[j])
 
-    def place_blocks(half):
+    def place_blocks(half, held):
         def pieces(inner, carry):
-            for far in range(2):
-                owner = core if far == 0 else 1 - core
-                for outer in range(4):
-                    up_y, up_x = (outer, inner) if half == 0 else (inner, outer)
+            for outer in range(4):
+                up_y = jnp.where(half == 0, outer, inner)
+                up_x = jnp.where(half == 0, inner, outer)
+                for owner in range(2):
                     row = piece_row(owner, lax.rem(y + up_y, 4), lax.rem(x + up_x, 4))
                     pltpu.make_async_copy(
-                        blocks[far * 8 + half * 4 + outer].at[inner],
-                        half_rows(half).at[pl.ds(row, PIECE), :],
+                        held[outer].at[inner, owner],
+                        rows_held.at[pl.ds(row, PIECE), half_columns(half)],
                         row_sems.at[half],
                     ).start()
             return carry
@@ -112,9 +124,9 @@
         )
 
     steps(lambda j: weight_copy(j).start(), 0, HALF_STEPS)
-    place_blocks(0)
+    place_blocks(core, blocks[:4])
     steps(lambda j: weight_copy(j).start(), HALF_STEPS, STEPS)
-    place_blocks(1)
+    place_blocks(1 - core, blocks[4:])
     logits[...] = jnp.zeros_like(logits)
     pltpu.make_async_copy(half_rows(0), half_rows(0), row_sems.at[0]).wait()
     steps(multiply, 0, HALF_STEPS)
@@ -156,7 +168,7 @@
             jax.ShapeDtypeStruct((VOCAB_ROWS, TOKENS), jnp.float32),
             jax.ShapeDtypeStruct((3, TOKENS), jnp.float32),
         ),
-        in_specs=[SCALARS, IN_VMEM, IN_HBM] + [ANYWHERE] * 16,
+        in_specs=[SCALARS, IN_VMEM, IN_HBM] + [ANYWHERE] * 8,
         out_specs=(IN_HBM, IN_VMEM, IN_VMEM),
         scratch_shapes=[
             pltpu.VMEM((VOCAB_ROWS, WIDTH), jnp.bfloat16),
@@ -181,14 +193,16 @@
     core, position = place[0], place[3]
 
     def arrival(j):
-        columns = step_columns(j)
-        return pltpu.make_async_copy(weight.at[:, columns], weight_held.at[:, columns], weight_sems.at[j])
+        columns = step_columns((1 - core) * HALF_STEPS + j)
+        return pltpu.make_async_copy(
+            weight.at[:, columns], weight_held.at[:, step_columns(j)], weight_sems.at[j]
+        )
 
     def leaving(j):
         columns = step_columns(j)
         return pltpu.make_async_copy(far_held.at[:, columns], far_out.at[:, columns], out_sems.at[j])
 
-    steps(lambda j: arrival(j).start())
+    steps(lambda j: arrival(j).start(), 0, HALF_STEPS)
     log_total = cap_value + jnp.log(totals[0:1, :])
     mean_logit = totals[1:2, :] / totals[0:1, :]
 
@@ -202,21 +216,20 @@
         ratio = values / cap_value
         grad = raw_grad * (1.0 - ratio * ratio)
         grad_out[rows, :] = grad.astype(jnp.bfloat16)
-        turned_out[:, :, :, rows] = grad.T.astype(jnp.bfloat16).reshape(8, 2, 32, 128)
+        turned_out[:, rows] = grad.T.astype(jnp.bfloat16)
 
     steps(gradient, 0, VOCAB_ROWS // 128)
 
     def multiply(j):
         arrival(j).wait()
         columns = step_columns(j)
-        rows = turned_out[:, 1 - core].reshape(NEAR, VOCAB_ROWS)
         far_held[:, columns] = jnp.dot(
-            rows, weight_held[:, columns], preferred_element_type=jnp.float32
+            turned_out[...], weight_held[:, columns], preferred_element_type=jnp.float32
         ).astype(jnp.bfloat16)
         leaving(j).start()
 
-    steps(multiply)
-    steps(lambda j: leaving(j).wait())
+    steps(multiply, 0, HALF_STEPS)
+    steps(lambda j: leaving(j).wait(), 0, HALF_STEPS)
 
 
 def far_gradient(place, targets, capped, totals, weight):
@@ -224,72 +237,65 @@
         far_kernel,
         out_shape=(
             jax.ShapeDtypeStruct((VOCAB_ROWS, TOKENS), jnp.bfloat16),
-            jax.ShapeDtypeStruct((8, 2, 32, VOCAB_ROWS), jnp.bfloat16),
-            jax.ShapeDtypeStruct((NEAR, WIDTH), jnp.bfloat16),
+            jax.ShapeDtypeStruct((TOKENS, VOCAB_ROWS), jnp.bfloat16),
+            jax.ShapeDtypeStruct((TOKENS, HALF), jnp.bfloat16),
         ),
         in_specs=[SCALARS, IN_VMEM, IN_VMEM, IN_VMEM, IN_HBM],
         out_specs=(IN_VMEM, IN_VMEM, ANYWHERE),
         scratch_shapes=[
-            pltpu.VMEM((VOCAB_ROWS, WIDTH), jnp.bfloat16),
-            pltpu.VMEM((NEAR, WIDTH), jnp.bfloat16),
-            pltpu.SemaphoreType.DMA((STEPS,)),
-            pltpu.SemaphoreType.DMA((STEPS,)),
+            pltpu.VMEM((VOCAB_ROWS, HALF), jnp.bfloat16),
+            pltpu.VMEM((TOKENS, HALF), jnp.bfloat16),
+            pltpu.SemaphoreType.DMA((HALF_STEPS,)),
+            pltpu.SemaphoreType.DMA((HALF_STEPS,)),
         ],
         compiler_params=pltpu.CompilerParams(vmem_limit_bytes=52 << 20),
         cost_estimate=pl.CostEstimate(
-            flops=2 * VOCAB_ROWS * NEAR * WIDTH, bytes_accessed=9 << 20, transcendentals=1 << 18
+            flops=VOCAB_ROWS * TOKENS * WIDTH, bytes_accessed=9 << 20, transcendentals=1 << 18
         ),
         name="far_gradient",
     )(place, targets, capped, totals, weight)
 
 
 def near_kernel(place, turned, weight, arrived, gathered, *rest):
-    sends, gain_out = rest[:8], rest[8]
-    weight_held, arrived_held, rows_held, first_held, second_held, in_sems, out_sems = rest[9:]
+    sends, gain_out = rest[:4], rest[4]
+    weight_held, arrived_held, rows_held, held, in_sems, out_sems = rest[5:]
     core, y, x = place[0], place[1], place[2]
 
     def arrivals(j):
-        columns = step_columns(j)
+        columns, own = step_columns(core * HALF_STEPS + j), step_columns(j)
         return [
-            pltpu.make_async_copy(weight.at[:, columns], weight_held.at[:, columns], in_sems.at[0, j]),
-            pltpu.make_async_copy(arrived.at[:, columns], arrived_held.at[:, columns], in_sems.at[1, j]),
-            pltpu.make_async_copy(
-                gathered.at[:, core, :, columns], rows_held.at[:, :, columns], in_sems.at[2, j]
-            ),
+            pltpu.make_async_copy(weight.at[:, columns], weight_held.at[:, own], in_sems.at[0, j]),
+            pltpu.make_async_copy(arrived.at[:, own], arrived_held.at[:, own], in_sems.at[1, j]),
+            pltpu.make_async_copy(gathered.at[:, columns], rows_held.at[:, own], in_sems.at[2, j]),
         ]
 
     def begin(j):
         for copy in arrivals(j):
             copy.start()
 
-    def multiply(half, held, j):
+    def multiply(j):
         for copy in arrivals(j):
             copy.wait()
         columns = step_columns(j)
-        rows = turned[:, core].reshape(NEAR, VOCAB_ROWS)
-        part = jnp.dot(rows, weight_held[:, columns], preferred_element_type=jnp.float32)
+        part = jnp.dot(turned[...], weight_held[:, columns], preferred_element_type=jnp.float32)
         part = part + arrived_held[:, columns].astype(jnp.float32)
         gain_out[:, columns] = jnp.sum(
-            part * rows_held[:, :, columns].reshape(NEAR, STEP).astype(jnp.float32), axis=0, keepdims=True
+            part * rows_held[:, columns].astype(jnp.float32), axis=0, keepdims=True
         )
         rounded = part.astype(jnp.bfloat16)
-        own = step_columns(j - half * HALF_STEPS)
         for to_y in range(4):
             for to_x in range(4):
                 up_y, up_x = lax.rem(to_y + 4 - y, 4), lax.rem(to_x + 4 - x, 4)
-                outer, inner = (up_y, up_x) if half == 0 else (up_x, up_y)
-                row = ((to_x % 2 * 4 + to_y) * 2 + to_x // 2) * PIECE
-                held[outer, inner, :, own] = rounded[row : row + PIECE]
-
-    steps(begin)
-    leaving = []
-    for half, held in ((0, first_held), (1, second_held)):
-        first = half * HALF_STEPS
-        steps(lambda j, half=half, held=held: multiply(half, held, j), first, first + HALF_STEPS)
-        for k in range(4):
-            copy = pltpu.make_async_copy(held.at[k], sends[half * 4 + k], out_sems.at[half * 4 + k])
-            copy.start()
-            leaving.append(copy)
+                outer, inner = jnp.where(core == 0, up_y, up_x), jnp.where(core == 0, up_x, up_y)
+                for owner in range(2):
+                    row = (((to_x % 2 * 4 + to_y) * 2 + owner) * 2 + to_x // 2) * PIECE
+                    held[outer, inner, owner, :, columns] = rounded[row : row + PIECE]
+
+    steps(begin, 0, HALF_STEPS)
+    steps(multiply, 0, HALF_STEPS)
+    leaving = [pltpu.make_async_copy(held.at[k], sends[k], out_sems.at[k]) for k in range(4)]
+    for copy in leaving:
+        copy.start()
     for copy in leaving:
         copy.wait()
 
@@ -297,26 +303,25 @@
 def near_gradient(place, turned, weight, arrived, gathered):
     outs = pl.pallas_call(
         near_kernel,
-        out_shape=[jax.ShapeDtypeStruct((4, PIECE, HALF), jnp.bfloat16)] * 8
-        + [jax.ShapeDtypeStruct((1, WIDTH), jnp.float32)],
+        out_shape=[jax.ShapeDtypeStruct((4, 2, PIECE, HALF), jnp.bfloat16)] * 4
+        + [jax.ShapeDtypeStruct((1, HALF), jnp.float32)],
         in_specs=[SCALARS, IN_VMEM, IN_HBM, ANYWHERE, IN_HBM],
-        out_specs=[ANYWHERE] * 8 + [IN_VMEM],
+        out_specs=[ANYWHERE] * 4 + [IN_VMEM],
         scratch_shapes=[
-            pltpu.VMEM((VOCAB_ROWS, WIDTH), jnp.bfloat16),
-            pltpu.VMEM((NEAR, WIDTH), jnp.bfloat16),
-            pltpu.VMEM((8, 32, WIDTH), jnp.bfloat16),
-            pltpu.VMEM((4, 4, PIECE, HALF), jnp.bfloat16),
-            pltpu.VMEM((4, 4, PIECE, HALF), jnp.bfloat16),
-            pltpu.SemaphoreType.DMA((3, STEPS)),
-            pltpu.SemaphoreType.DMA((8,)),
+            pltpu.VMEM((VOCAB_ROWS, HALF), jnp.bfloat16),
+            pltpu.VMEM((TOKENS, HALF), jnp.bfloat16),
+            pltpu.VMEM((TOKENS, HALF), jnp.bfloat16),
+            pltpu.VMEM((4, 4, 2, PIECE, HALF), jnp.bfloat16),
+            pltpu.SemaphoreType.DMA((3, HALF_STEPS)),
+            pltpu.SemaphoreType.DMA((4,)),
         ],
         compiler_params=pltpu.CompilerParams(vmem_limit_bytes=45 << 20),
         cost_estimate=pl.CostEstimate(
-            flops=2 * VOCAB_ROWS * NEAR * WIDTH, bytes_accessed=12 << 20, transcendentals=0
+            flops=VOCAB_ROWS * TOKENS * WIDTH, bytes_accessed=12 << 20, transcendentals=0
         ),
         name="near_gradient",
     )(place, turned, weight, arrived, gathered)
-    return outs[:4], outs[4:8], outs[8]
+    return outs[:4], outs[4]
 
 
 def weight_kernel(grad, gathered, out, rows_held, out_held, in_sems, out_sems):
@@ -372,45 +377,47 @@
     unit_rows = values * inverse
     normed = (unit_rows * norm_gain).astype(jnp.bfloat16)
 
-    line = gather_over(normed, "z", 8).reshape(PIECE, WIDTH)
-    first_row = jnp.stack(gather_ring(line[:, :HALF], shift_x))
-    second_row = jnp.stack(gather_ring(line[:, HALF:], shift_y))
-    near_blocks = gather_ring(first_row, shift_y) + gather_ring(second_row, shift_x)
-    arrived_blocks = lax.optimization_barrier(near_blocks[1:4] + near_blocks[5:])
-    near_blocks = [near_blocks[0], *arrived_blocks[:3], near_blocks[4], *arrived_blocks[3:]]
-    far_blocks = [swap_cores(block) for block in near_blocks]
-
-    gathered, capped, stats = forward(place, ids, weight, near_blocks + far_blocks)
+    def by_core(mine, other, axis):
+        return jnp.where(
+            core == 0, jnp.concatenate([mine, other], axis), jnp.concatenate([other, mine], axis)
+        )
+
+    mine = lax.dynamic_slice_in_dim(normed, core * HALF, HALF, 1)
+    other = swap_cores(lax.dynamic_slice_in_dim(normed, (1 - core) * HALF, HALF, 1))
+    line = gather_over(by_core(mine, other, 0), "z", 8)
+    line = line.reshape(8, 2, 2, HALF).transpose(1, 0, 2, 3).reshape(2, PIECE, HALF)
+    blocks = gather_ring(jnp.stack(gather_ring(line, shift_first)), shift_second)
+    blocks = blocks + [swap_cores(block) for block in blocks]
+
+    gathered, capped, stats = forward(place, ids, weight, blocks)
     stats = stats + swap_cores(stats)
     stats = sum_over(stats, PLANE, 16)
     stats = sum_over(stats, "z", 8)
 
     grad, turned, far_part = far_gradient(place, ids, capped, stats, weight)
     arrived = swap_cores(far_part)
-    first_sends, second_sends, gain_part = near_gradient(
-        place, turned, weight, arrived, gathered.reshape(8, 2, 32, WIDTH)
-    )
-    first_parts = send_ring(first_sends, shift_y)
-    second_parts = send_ring(second_sends, shift_x)
-    gain_part, first_parts[2] = lax.optimization_barrier((gain_part, first_parts[2]))
+    sends, gain_part = near_gradient(place, turned, weight, arrived, gathered)
+    parts = send_ring(sends, shift_second)
+    gain_part, parts[1] = lax.optimization_barrier((gain_part, parts[1]))
     gain_part = sum_over(gain_part, PLANE, 16)
-    gain_part = gain_part + swap_cores(gain_part)
-    first_half = total(first_parts).astype(jnp.bfloat16)
-    second_half = total(second_parts).astype(jnp.bfloat16)
-    first_line = total(send_ring([first_half[k] for k in range(4)], shift_x))
-    second_line = total(send_ring([second_half[k] for k in range(4)], shift_y))
-    line_part = jnp.concatenate([first_line, second_line], axis=1).astype(jnp.bfloat16)
+    half_sum = total(parts).astype(jnp.bfloat16)
+    line_part = total(send_ring([half_sum[k] for k in range(4)], shift_first)).astype(jnp.bfloat16)
+    line_part = line_part.reshape(2, 8, 2, HALF).transpose(1, 0, 2, 3).reshape(8, 4, HALF)
     gain_high = lax.reduce_precision(gain_part, 8, 7)
     gain_rows = jnp.concatenate([gain_high, gain_part - gain_high], axis=0).astype(jnp.bfloat16)
-    message = jnp.concatenate(
-        [line_part.reshape(8, 2, WIDTH), jnp.broadcast_to(gain_rows[None], (8, 2, WIDTH))], axis=1
-    )
+    message = jnp.concatenate([line_part, jnp.broadcast_to(gain_rows[None], (8, 2, HALF))], axis=1)
     message, grad = lax.optimization_barrier((message, grad))
     line_parts = lax.all_to_all(message, "z", 0, 0, tiled=True)
     grad_weight = weight_gradient(grad, gathered)
+    line_parts, grad_weight = lax.optimization_barrier((line_parts, grad_weight))
     line_sum = jnp.sum(line_parts.astype(jnp.float32), axis=0)
-    grad_normed = line_sum[:2]
-    grad_gain = (line_sum[2] + line_sum[3]) / norm_gain
+    gain_sum = line_sum[4:5] + line_sum[5:6]
+    first_core, second_core = line_sum[0:2], line_sum[2:4]
+    mine = jnp.concatenate([jnp.where(core == 0, first_core, second_core), gain_sum], axis=0)
+    theirs = jnp.concatenate([jnp.where(core == 0, second_core, first_core), gain_sum], axis=0)
+    whole = by_core(mine, swap_cores(theirs), 1)
+    grad_normed = whole[:2]
+    grad_gain = whole[2] / norm_gain
 
     total_exp, total_weighted, target_logit = stats
     log_total = cap_value + jnp.log(total_exp)

time: 157 us -> 157 us (level); the launches traced: 156 us -> 153 us
  starting transfers between devices: 55.5 us -> 31.5 us
  waiting for transfers between devices: 24.9 us -> 48.2 us
  other arithmetic: 8.12 us -> 6.08 us
    ppermute x24 -> x12, starting transfers between devices: 44.8 us -> 21.1 us  [the longest x6 11.1 us: shift_first(): return lax.ppermute(block, CROSS, cross_pairs(step, 0))]
    ppermute x24 -> x12, waiting for transfers between devices: 13.7 us -> 33.4 us  [the longest x6 26.4 us: shift_second(): return lax.ppermute(block, CROSS, cross_pairs(step, 1))]
    ppermute x11 -> x8, waiting for transfers between devices: 8.08 us -> 9.63 us  [swap_cores(): return lax.ppermute(block, 'core', [(0, 1), (1, 0)])]
  transfers between devices with their start and end apart: 37 -> 22, of which waited for: 16 -> 15; matrix products, arithmetic and copies ran while one was open for 3% -> 2% of each run, Pallas kernels for 4% -> 4%
where the time goes in v2:
time: 157 us; the launch traced here: 153 us
  waiting for transfers between devices  48.2 us (31%)
  blocking collectives  40.7 us (26%)
  starting transfers between devices  31.5 us (20%)
  Pallas kernels  24 us (15%)
  other arithmetic  6.08 us (4%)
  local copies, waits for them, and re-layouts  2.06 us (1%)
    all_to_all x3, blocking collectives, gather_over(): return lax.all_to_all(copies, axes, 0, 0, tiled=True)  40.7 us
    ppermute x6, waiting for transfers between devices, shift_second(): return lax.ppermute(block, CROSS, cross_pairs(step, 1))  26.4 us
    ppermute x6, starting transfers between devices, shift_first(): return lax.ppermute(block, CROSS, cross_pairs(step, 0))  11.1 us
    ppermute x6, starting transfers between devices, shift_second(): return lax.ppermute(block, CROSS, cross_pairs(step, 1))  9.96 us
    ppermute x8, waiting for transfers between devices, swap_cores(): return lax.ppermute(block, 'core', [(0, 1), (1, 0)])  9.63 us
    pallas_call x1, Pallas kernels, forward(): pl.pallas_call(forward_kernel, out_shape=(jax.ShapeDtypeStruct((TOKENS, W...  8.81 us
    ppermute x6, waiting for transfers between devices, shift_first(): return lax.ppermute(block, CROSS, cross_pairs(step, 0))  6.95 us
    pallas_call x1, Pallas kernels, weight_gradient(): pl.pallas_call(weight_kernel, out_shape=jax.ShapeDtypeStruct((VOCAB_ROWS,...  5.62 us
  transfers between devices with their start and end apart: 22, of which 15 were waited for; matrix products, arithmetic and copies ran while one was open for 2% of the time, Pallas kernels for 4%

profile of v2, /device:TPU:32, one launch (start us, length us, event | category | flops | bytes accessed | tf_op | source)
XLA Modules:
  0.0 153.5 jit_solution(5762405098068662317)
XLA Ops:
  3.7 16.7 %all_to_all.25 = bf16[8,4,2304]{2,1,0:T(4,128)(2,1)S(1)} all-to-all(bf16[8,4,2304]{2,1,0:T(4,128)(2,1)S(1)} %broadcast_in_dim.12), channel_id=1, replica_groups=mesh['x_lo'=2,'y'=4,'core'=2,'x_hi'=2,'z'=8] {'z'}, dimensions={0} | all-to-all | bytes 294912 | tf_op jit(solution)/shard_map/all_to_all | solution.py:51
  20.6 1.6 %collective-permute-start.3 = (bf16[2,16,2304]{2,1,0:T(8,128)(2,1)S(1)}, bf16[2,16,2304]{2,1,0:T(8,128)(2,1)S(1)}, u32[]{:S(2)}, u32[]{:S(2)}) collective-permute-start(bf16[2,16,2304]{2,1,0:T(8,128)(2,1)S(1)} %reshape.114), channel_id=1, source_target_pairs={{0,128},{16,48},{32,160},{48,80},{64,192},{80,112},{96,224},{112,1... | collective-permute-start | bytes 442376 | tf_op jit(solution)/shard_map/ppermute | solution.py:38
  22.2 2.7 %collective-permute-start.2 = (bf16[2,16,2304]{2,1,0:T(8,128)(2,1)S(1)}, bf16[2,16,2304]{2,1,0:T(8,128)(2,1)S(1)}, u32[]{:S(2)}, u32[]{:S(2)}) collective-permute-start(bf16[2,16,2304]{2,1,0:T(8,128)(2,1)S(1)} %reshape.114), channel_id=1, source_target_pairs={{0,8},{16,80},{32,40},{48,112},{64,72},{80,16},{96,104},{112,48},{... | collective-permute-start | bytes 442376 | tf_op jit(solution)/shard_map/ppermute | solution.py:38
  27.1 2.6 %collective-permute-done.2 = bf16[2,16,2304]{2,1,0:T(8,128)(2,1)S(1)} collective-permute-done((bf16[2,16,2304]{2,1,0:T(8,128)(2,1)S(1)}, bf16[2,16,2304]{2,1,0:T(8,128)(2,1)S(1)}, u32[]{:S(2)}, u32[]{:S(2)}) %collective-permute-start.2) | collective-permute-done | bytes 147488 | tf_op jit(solution)/shard_map/ppermute | solution.py:38
  30.1 1.7 %collective-permute-start.6 = (bf16[4,2,16,2304]{3,2,1,0:T(8,128)(2,1)S(1)}, bf16[4,2,16,2304]{3,2,1,0:T(8,128)(2,1)S(1)}, u32[]{:S(2)}, u32[]{:S(2)}) collective-permute-start(bf16[4,2,16,2304]{3,2,1,0:T(8,128)(2,1)S(1)} %pad_maximum_fusion.rest_0_), channel_id=1, source_target_pairs={{0,32},{16,144},{32,64},{48,176},{64,96},{80,208},{96,0},{112,240}... | collective-permute-start | bytes 1769480 | tf_op jit(solution)/shard_map/ppermute | solution.py:42
  31.8 2.9 %collective-permute-start.5 = (bf16[4,2,16,2304]{3,2,1,0:T(8,128)(2,1)S(1)}, bf16[4,2,16,2304]{3,2,1,0:T(8,128)(2,1)S(1)}, u32[]{:S(2)}, u32[]{:S(2)}) collective-permute-start(bf16[4,2,16,2304]{3,2,1,0:T(8,128)(2,1)S(1)} %pad_maximum_fusion.rest_0_), channel_id=1, source_target_pairs={{0,64},{16,24},{32,96},{48,56},{64,0},{80,88},{96,32},{112,120},{1... | collective-permute-start | bytes 1769480 | tf_op jit(solution)/shard_map/ppermute | solution.py:42
  36.1 5.3 %collective-permute-done.6.rest_3_ = bf16[4,2,16,2304]{3,2,1,0:T(8,128)(2,1)S(1)} collective-permute-done((bf16[4,2,16,2304]{3,2,1,0:T(8,128)(2,1)S(1)}, bf16[4,2,16,2304]{3,2,1,0:T(8,128)(2,1)S(1)}, u32[]{:S(2)}, u32[]{:S(2)}) %collective-permute-start.6) | collective-permute-done | bytes 589856 | tf_op jit(solution)/shard_map/ppermute | solution.py:42
  41.3 7.6 %collective-permute-done.5.rest_2_ = bf16[4,2,16,2304]{3,2,1,0:T(8,128)(2,1)S(1)} collective-permute-done((bf16[4,2,16,2304]{3,2,1,0:T(8,128)(2,1)S(1)}, bf16[4,2,16,2304]{3,2,1,0:T(8,128)(2,1)S(1)}, u32[]{:S(2)}, u32[]{:S(2)}) %collective-permute-start.5) | collective-permute-done | bytes 589856 | tf_op jit(solution)/shard_map/ppermute | solution.py:42
  49.5 2.3 %collective-permute-done.9.rest_6_ = bf16[4,2,16,2304]{3,2,1,0:T(8,128)(2,1)} collective-permute-done((bf16[4,2,16,2304]{3,2,1,0:T(8,128)(2,1)S(1)}, bf16[4,2,16,2304]{3,2,1,0:T(8,128)(2,1)}, u32[]{:S(2)}, u32[]{:S(2)}) %collective-permute-start.9) | collective-permute-done | bytes 589856 | tf_op jit(solution)/shard_map/ppermute | solution.py:46
  51.8 8.8 %forward.1 = (bf16[512,4608]{1,0:T(8,128)(2,1)}, f32[512,512]{1,0:T(8,128)}, f32[3,512]{1,0:T(4,128)S(1)}) custom-call(s32[4]{0:T(128)S(1)} %pad_add_fusion.place, s32[1,512]{1,0:T(1,128)S(1)} %bitcast.27, bf16[512,4608]{1,0:T(8,128)(2,1)} %weight.5, bf16[4,2,16,2304]{3,2,1,0:T(8,128)(2,1)S(1)} %pad_maximum_fusion.rest_0_, ...), custom_call_target="tpu_custom_call" | custom-call | flops 2415919104 | bytes 16777216 | tf_op jit(solution)/shard_map/forward/pallas_call | solution.py:164
  62.7 13.3 %all_to_all.26 = f32[16,3,512]{2,1,0:T(4,128)S(1)} all-to-all(f32[16,3,512]{2,1,0:T(4,128)S(1)} %broadcast_in_dim.13), channel_id=1, replica_groups=mesh['x_lo'=2,'y'=4,'core'=2,'x_hi'=2,'z'=8] {'x_lo','y','x_hi'}, dimensions={0} | all-to-all | bytes 196608 | tf_op jit(solution)/shard_map/all_to_all | solution.py:51
  76.1 10.8 %all_to_all.27 = f32[8,3,512]{2,1,0:T(4,128)S(1)} all-to-all(f32[8,3,512]{2,1,0:T(4,128)S(1)} %broadcast_in_dim.14), channel_id=1, replica_groups=mesh['x_lo'=2,'y'=4,'core'=2,'x_hi'=2,'z'=8] {'z'}, dimensions={0} | all-to-all | bytes 98304 | tf_op jit(solution)/shard_map/all_to_all | solution.py:51
  86.9 5.0 %far_gradient.1 = (bf16[512,512]{1,0:T(8,128)(2,1)S(1)}, bf16[512,512]{1,0:T(8,128)(2,1)S(1)}, bf16[512,2304]{1,0:T(8,128)(2,1)}) custom-call(s32[4]{0:T(128)S(1)} %pad_add_fusion.place, s32[1,512]{1,0:T(1,128)S(1)} %bitcast.28, f32[512,512]{1,0:T(8,128)} %get-tuple-element.22.capped, f32[3,512]{1,0:T(4,128)S(1)} %reduce_sum.58.totals, bf16[512,4608]{1,0:T(8,128)(2,1)} %weight.5), custom_call_target="tpu_custom_call" | custom-call | flops 1207959552 | bytes 9437184 | tf_op jit(solution)/shard_map/far_gradient/pallas_call | solution.py:236
  92.0 4.7 %collective-permute-done.12.arrived = bf16[512,2304]{1,0:T(8,128)(2,1)S(1)} collective-permute-done((bf16[512,2304]{1,0:T(8,128)(2,1)}, bf16[512,2304]{1,0:T(8,128)(2,1)S(1)}, u32[]{:S(2)}, u32[]{:S(2)}) %collective-permute-start.12) | collective-permute-done | bytes 2359328 | tf_op jit(solution)/shard_map/ppermute | solution.py:46
  96.8 4.5 %near_gradient.1 = (bf16[4,2,16,2304]{3,2,1,0:T(8,128)(2,1)S(1)}, bf16[4,2,16,2304]{3,2,1,0:T(8,128)(2,1)S(1)}, bf16[4,2,16,2304]{3,2,1,0:T(8,128)(2,1)S(1)}, bf...) custom-call(s32[4]{0:T(128)S(1)} %pad_add_fusion.place, bf16[512,512]{1,0:T(8,128)(2,1)S(1)} %get-tuple-element.23.turned, ...), custom_call_target="tpu_custom_call" | custom-call | flops 1207959552 | bytes 12582912 | tf_op jit(solution)/shard_map/near_gradient/pallas_call | solution.py:304
  102.0 2.2 %collective-permute-start.14 = (bf16[4,2,16,2304]{3,2,1,0:T(8,128)(2,1)S(1)}, bf16[4,2,16,2304]{3,2,1,0:T(8,128)(2,1)}, u32[]{:S(2)}, u32[]{:S(2)}) collective-permute-start(bf16[4,2,16,2304]{3,2,1,0:T(8,128)(2,1)S(1)} %get-tuple-element.30), channel_id=1, source_target_pairs={{0,64},{16,24},{32,96},{48,56},{64,0},{80,88},{96,32},{112,120},{1... | collective-permute-start | bytes 1769480 | tf_op jit(solution)/shard_map/ppermute | solution.py:42
  105.4 13.6 %collective-permute-done.13 = bf16[4,2,16,2304]{3,2,1,0:T(8,128)(2,1)S(1)} collective-permute-done((bf16[4,2,16,2304]{3,2,1,0:T(8,128)(2,1)S(1)}, bf16[4,2,16,2304]{3,2,1,0:T(8,128)(2,1)S(1)}, u32[]{:S(2)}, u32[]{:S(2)}) %collective-permute-start.13) | collective-permute-done | bytes 589856 | tf_op jit(solution)/shard_map/ppermute | solution.py:42
  119.7 3.5 %all-to-all-start.3 = ((f32[16,1,2304]{2,1,0:T(1,128)}), f32[16,1,2304]{2,1,0:T(1,128)S(1)}, u32[]{:S(2)}, u32[]{:S(2)}) async-start(f32[16,1,2304]{2,1,0:T(1,128)} %broadcast_in_dim.16), calls=%async_computation.3 | async-start | bytes 294912 | tf_op jit(solution)/shard_map/all_to_all | solution.py:51
  124.9 1.9 %collective-permute-start.16 = (bf16[2,16,2304]{2,1,0:T(8,128)(2,1)S(1)}, bf16[2,16,2304]{2,1,0:T(8,128)(2,1)S(1)}, u32[]{:S(2)}, u32[]{:S(2)}) collective-permute-start(bf16[2,16,2304]{2,1,0:T(8,128)(2,1)S(1)} %get-tuple-element.38), channel_id=1, source_target_pairs={{0,128},{16,48},{32,160},{48,80},{64,192},{80,112},{96,224},{112,1... | collective-permute-start | bytes 442376 | tf_op jit(solution)/shard_map/ppermute | solution.py:38
  128.2 2.1 %collective-permute-start.17 = (bf16[2,16,2304]{2,1,0:T(8,128)(2,1)S(1)}, bf16[2,16,2304]{2,1,0:T(8,128)(2,1)S(1)}, u32[]{:S(2)}, u32[]{:S(2)}) collective-permute-start(bf16[2,16,2304]{2,1,0:T(8,128)(2,1)S(1)} %get-tuple-element.40), channel_id=1, source_target_pairs={{0,8},{16,80},{32,40},{48,112},{64,72},{80,16},{96,104},{112,48},{... | collective-permute-start | bytes 442376 | tf_op jit(solution)/shard_map/ppermute | solution.py:38
  131.9 2.9 %collective-permute-done.17 = bf16[2,16,2304]{2,1,0:T(8,128)(2,1)S(1)} collective-permute-done((bf16[2,16,2304]{2,1,0:T(8,128)(2,1)S(1)}, bf16[2,16,2304]{2,1,0:T(8,128)(2,1)S(1)}, u32[]{:S(2)}, u32[]{:S(2)}) %collective-permute-start.17) | collective-permute-done | bytes 147488 | tf_op jit(solution)/shard_map/ppermute | solution.py:38
  135.8 4.8 %all-to-all-start.4 = ((bf16[8,6,2304]{2,1,0:T(8,128)(2,1)}), bf16[8,6,2304]{2,1,0:T(8,128)(2,1)S(1)}, u32[]{:S(2)}, u32[]{:S(2)}) async-start(bf16[8,6,2304]{2,1,0:T(8,128)(2,1)} %copy.28), calls=%async_computation.4 | async-start | bytes 589824 | tf_op jit(solution)/shard_map/all_to_all | solution.py:410
  140.6 5.6 %weight_gradient.1 = bf16[512,4608]{1,0:T(8,128)(2,1)} custom-call(bf16[512,512]{1,0:T(8,128)(2,1)S(1)} %get-tuple-element.35.grad, bf16[512,4608]{1,0:T(8,128)(2,1)} %get-tuple-element.25.gathered), custom_call_target="tpu_custom_call" | custom-call | flops 2415919104 | bytes 10485760 | tf_op jit(solution)/shard_map/weight_gradient/pallas_call | solution.py:350
  146.3 4.1 %all-to-all-done.4 = bf16[8,6,2304]{2,1,0:T(8,128)(2,1)S(1)} async-done(((bf16[8,6,2304]{2,1,0:T(8,128)(2,1)}), bf16[8,6,2304]{2,1,0:T(8,128)(2,1)S(1)}, u32[]{:S(2)}, u32[]{:S(2)}) %all-to-all-start.4) | async-done | bytes 221216 | tf_op jit(solution)/shard_map/all_to_all | solution.py:410
  (75 shorter events, 21.4 us)
Async XLA Ops:
  2.4 1.3 collective-permute-start
  20.4 31.4 %copy-start = (s32[512]{0:T(512)S(1)}, s32[512]{0:T(512)}, u32[]{:S(2)}) copy-start(s32[512]{0:T(512)} %param.7) | copy-start | bytes 6148
  20.6 6.4 %collective-permute-start.3 = (bf16[2,16,2304]{2,1,0:T(8,128)(2,1)S(1)}, bf16[2,16,2304]{2,1,0:T(8,128)(2,1)S(1)}, u32[]{:S(2)}, u32[]{:S(2)}) collective-permute-start(bf16[2,16,2304]{2,1,0:T(8,128)(2,1)S(1)} %reshape.114), channel_id=1, source_target_pairs={{0,128},{16,48},{32,160},{48,80},{64,192},{80,112},{96,224},{112,1... | collective-permute-start | bytes 442376 | tf_op jit(solution)/shard_map/ppermute | solution.py:38
  22.2 7.4 %collective-permute-start.2 = (bf16[2,16,2304]{2,1,0:T(8,128)(2,1)S(1)}, bf16[2,16,2304]{2,1,0:T(8,128)(2,1)S(1)}, u32[]{:S(2)}, u32[]{:S(2)}) collective-permute-start(bf16[2,16,2304]{2,1,0:T(8,128)(2,1)S(1)} %reshape.114), channel_id=1, source_target_pairs={{0,8},{16,80},{32,40},{48,112},{64,72},{80,16},{96,104},{112,48},{... | collective-permute-start | bytes 442376 | tf_op jit(solution)/shard_map/ppermute | solution.py:38
  24.9 5.1 %collective-permute-start.1 = (bf16[2,16,2304]{2,1,0:T(8,128)(2,1)S(1)}, bf16[2,16,2304]{2,1,0:T(8,128)(2,1)S(1)}, u32[]{:S(2)}, u32[]{:S(2)}) collective-permute-start(bf16[2,16,2304]{2,1,0:T(8,128)(2,1)S(1)} %reshape.114), channel_id=1, source_target_pairs={{0,136},{16,112},{32,168},{48,16},{64,200},{80,48},{96,232},{112,8... | collective-permute-start | bytes 442376 | tf_op jit(solution)/shard_map/ppermute | solution.py:38
  30.1 11.2 %collective-permute-start.6 = (bf16[4,2,16,2304]{3,2,1,0:T(8,128)(2,1)S(1)}, bf16[4,2,16,2304]{3,2,1,0:T(8,128)(2,1)S(1)}, u32[]{:S(2)}, u32[]{:S(2)}) collective-permute-start(bf16[4,2,16,2304]{3,2,1,0:T(8,128)(2,1)S(1)} %pad_maximum_fusion.rest_0_), channel_id=1, source_target_pairs={{0,32},{16,144},{32,64},{48,176},{64,96},{80,208},{96,0},{112,240}... | collective-permute-start | bytes 1769480 | tf_op jit(solution)/shard_map/ppermute | solution.py:42
  31.8 17.1 %collective-permute-start.5 = (bf16[4,2,16,2304]{3,2,1,0:T(8,128)(2,1)S(1)}, bf16[4,2,16,2304]{3,2,1,0:T(8,128)(2,1)S(1)}, u32[]{:S(2)}, u32[]{:S(2)}) collective-permute-start(bf16[4,2,16,2304]{3,2,1,0:T(8,128)(2,1)S(1)} %pad_maximum_fusion.rest_0_), channel_id=1, source_target_pairs={{0,64},{16,24},{32,96},{48,56},{64,0},{80,88},{96,32},{112,120},{1... | collective-permute-start | bytes 1769480 | tf_op jit(solution)/shard_map/ppermute | solution.py:42
  34.7 14.2 %collective-permute-start.4 = (bf16[4,2,16,2304]{3,2,1,0:T(8,128)(2,1)S(1)}, bf16[4,2,16,2304]{3,2,1,0:T(8,128)(2,1)S(1)}, u32[]{:S(2)}, u32[]{:S(2)}) collective-permute-start(bf16[4,2,16,2304]{3,2,1,0:T(8,128)(2,1)S(1)} %pad_maximum_fusion.rest_0_), channel_id=1, source_target_pairs={{0,96},{16,152},{32,0},{48,184},{64,32},{80,216},{96,64},{112,248}... | collective-permute-start | bytes 1769480 | tf_op jit(solution)/shard_map/ppermute | solution.py:42
  36.0 13.4 %collective-permute-start.7 = (bf16[4,2,16,2304]{3,2,1,0:T(8,128)(2,1)S(1)}, bf16[4,2,16,2304]{3,2,1,0:T(8,128)(2,1)S(1)}, u32[]{:S(2)}, u32[]{:S(2)}) collective-permute-start(bf16[4,2,16,2304]{3,2,1,0:T(8,128)(2,1)S(1)} %pad_maximum_fusion.rest_0_), channel_id=1, source_target_pairs={{0,16},{16,0},{1,17},{17,1},{2,18},{18,2},{3,19},{19,3},{4,20},{20... | collective-permute-start | bytes 1769480 | tf_op jit(solution)/shard_map/ppermute | solution.py:46
  41.3 8.2 %collective-permute-start.10 = (bf16[4,2,16,2304]{3,2,1,0:T(8,128)(2,1)S(1)}, bf16[4,2,16,2304]{3,2,1,0:T(8,128)(2,1)}, u32[]{:S(2)}, u32[]{:S(2)}) collective-permute-start(bf16[4,2,16,2304]{3,2,1,0:T(8,128)(2,1)S(1)} %collective-permute-done.6.rest_3_), channel_id=1, source_target_pairs={{0,16},{16,0},{1,17},{17,1},{2,18},{18,2},{3,19},{19,3},{4,20},{20... | collective-permute-start | bytes 1769480 | tf_op jit(solution)/shard_map/ppermute | solution.py:46
  48.9 2.9 %collective-permute-start.9 = (bf16[4,2,16,2304]{3,2,1,0:T(8,128)(2,1)S(1)}, bf16[4,2,16,2304]{3,2,1,0:T(8,128)(2,1)}, u32[]{:S(2)}, u32[]{:S(2)}) collective-permute-start(bf16[4,2,16,2304]{3,2,1,0:T(8,128)(2,1)S(1)} %collective-permute-done.5.rest_2_), channel_id=1, source_target_pairs={{0,16},{16,0},{1,17},{17,1},{2,18},{18,2},{3,19},{19,3},{4,20},{20... | collective-permute-start | bytes 1769480 | tf_op jit(solution)/shard_map/ppermute | solution.py:46
  48.9 2.9 %collective-permute-start.8 = (bf16[4,2,16,2304]{3,2,1,0:T(8,128)(2,1)S(1)}, bf16[4,2,16,2304]{3,2,1,0:T(8,128)(2,1)S(1)}, u32[]{:S(2)}, u32[]{:S(2)}) collective-permute-start(bf16[4,2,16,2304]{3,2,1,0:T(8,128)(2,1)S(1)} %collective-permute-done.4.rest_1_), channel_id=1, source_target_pairs={{0,16},{16,0},{1,17},{17,1},{2,18},{18,2},{3,19},{19,3},{4,20},{20... | collective-permute-start | bytes 1769480 | tf_op jit(solution)/shard_map/ppermute | solution.py:46
  60.6 2.1 %collective-permute-start.11 = (f32[3,512]{1,0:T(4,128)S(1)}, f32[3,512]{1,0:T(4,128)S(1)}, u32[]{:S(2)}, u32[]{:S(2)}) collective-permute-start(f32[3,512]{1,0:T(4,128)S(1)} %get-tuple-element.21), channel_id=1, source_target_pairs={{0,16},{16,0},{1,17},{17,1},{2,18},{18,2},{3,19},{19,3},{4,20},{20... | collective-permute-start | bytes 18440 | tf_op jit(solution)/shard_map/ppermute | solution.py:46
  91.9 4.8 %collective-permute-start.12 = (bf16[512,2304]{1,0:T(8,128)(2,1)}, bf16[512,2304]{1,0:T(8,128)(2,1)S(1)}, u32[]{:S(2)}, u32[]{:S(2)}) collective-permute-start(bf16[512,2304]{1,0:T(8,128)(2,1)} %get-tuple-element.24), channel_id=1, source_target_pairs={{0,16},{16,0},{1,17},{17,1},{2,18},{18,2},{3,19},{19,3},{4,20},{20... | collective-permute-start | bytes 7077896 | tf_op jit(solution)/shard_map/ppermute | solution.py:46
  101.3 17.7 %collective-permute-start.13 = (bf16[4,2,16,2304]{3,2,1,0:T(8,128)(2,1)S(1)}, bf16[4,2,16,2304]{3,2,1,0:T(8,128)(2,1)S(1)}, u32[]{:S(2)}, u32[]{:S(2)}) collective-permute-start(bf16[4,2,16,2304]{3,2,1,0:T(8,128)(2,1)S(1)} %get-tuple-element.28), channel_id=1, source_target_pairs={{0,32},{16,144},{32,64},{48,176},{64,96},{80,208},{96,0},{112,240}... | collective-permute-start | bytes 1769480 | tf_op jit(solution)/shard_map/ppermute | solution.py:42
  102.0 21.2 %collective-permute-start.14 = (bf16[4,2,16,2304]{3,2,1,0:T(8,128)(2,1)S(1)}, bf16[4,2,16,2304]{3,2,1,0:T(8,128)(2,1)}, u32[]{:S(2)}, u32[]{:S(2)}) collective-permute-start(bf16[4,2,16,2304]{3,2,1,0:T(8,128)(2,1)S(1)} %get-tuple-element.30), channel_id=1, source_target_pairs={{0,64},{16,24},{32,96},{48,56},{64,0},{80,88},{96,32},{112,120},{1... | collective-permute-start | bytes 1769480 | tf_op jit(solution)/shard_map/ppermute | solution.py:42
  104.2 19.1 %collective-permute-start.15 = (bf16[4,2,16,2304]{3,2,1,0:T(8,128)(2,1)S(1)}, bf16[4,2,16,2304]{3,2,1,0:T(8,128)(2,1)}, u32[]{:S(2)}, u32[]{:S(2)}) collective-permute-start(bf16[4,2,16,2304]{3,2,1,0:T(8,128)(2,1)S(1)} %get-tuple-element.31), channel_id=1, source_target_pairs={{0,96},{16,152},{32,0},{48,184},{64,32},{80,216},{96,64},{112,248}... | collective-permute-start | bytes 1769480 | tf_op jit(solution)/shard_map/ppermute | solution.py:42
  119.7 11.6 %all-to-all-start.3 = ((f32[16,1,2304]{2,1,0:T(1,128)}), f32[16,1,2304]{2,1,0:T(1,128)S(1)}, u32[]{:S(2)}, u32[]{:S(2)}) async-start(f32[16,1,2304]{2,1,0:T(1,128)} %broadcast_in_dim.16), calls=%async_computation.3 | async-start | bytes 294912 | tf_op jit(solution)/shard_map/all_to_all | solution.py:51
  124.9 6.7 %collective-permute-start.16 = (bf16[2,16,2304]{2,1,0:T(8,128)(2,1)S(1)}, bf16[2,16,2304]{2,1,0:T(8,128)(2,1)S(1)}, u32[]{:S(2)}, u32[]{:S(2)}) collective-permute-start(bf16[2,16,2304]{2,1,0:T(8,128)(2,1)S(1)} %get-tuple-element.38), channel_id=1, source_target_pairs={{0,128},{16,48},{32,160},{48,80},{64,192},{80,112},{96,224},{112,1... | collective-permute-start | bytes 442376 | tf_op jit(solution)/shard_map/ppermute | solution.py:38
  126.8 5.1 %collective-permute-start.18 = (bf16[2,16,2304]{2,1,0:T(8,128)(2,1)S(1)}, bf16[2,16,2304]{2,1,0:T(8,128)(2,1)S(1)}, u32[]{:S(2)}, u32[]{:S(2)}) collective-permute-start(bf16[2,16,2304]{2,1,0:T(8,128)(2,1)S(1)} %get-tuple-element.39), channel_id=1, source_target_pairs={{0,136},{16,112},{32,168},{48,16},{64,200},{80,48},{96,232},{112,8... | collective-permute-start | bytes 442376 | tf_op jit(solution)/shard_map/ppermute | solution.py:38
  128.2 6.6 %collective-permute-start.17 = (bf16[2,16,2304]{2,1,0:T(8,128)(2,1)S(1)}, bf16[2,16,2304]{2,1,0:T(8,128)(2,1)S(1)}, u32[]{:S(2)}, u32[]{:S(2)}) collective-permute-start(bf16[2,16,2304]{2,1,0:T(8,128)(2,1)S(1)} %get-tuple-element.40), channel_id=1, source_target_pairs={{0,8},{16,80},{32,40},{48,112},{64,72},{80,16},{96,104},{112,48},{... | collective-permute-start | bytes 442376 | tf_op jit(solution)/shard_map/ppermute | solution.py:38
  135.8 14.5 %all-to-all-start.4 = ((bf16[8,6,2304]{2,1,0:T(8,128)(2,1)}), bf16[8,6,2304]{2,1,0:T(8,128)(2,1)S(1)}, u32[]{:S(2)}, u32[]{:S(2)}) async-start(bf16[8,6,2304]{2,1,0:T(8,128)(2,1)} %copy.28), calls=%async_computation.4 | async-start | bytes 589824 | tf_op jit(solution)/shard_map/all_to_all | solution.py:410
  140.6 11.2 %copy-start.1 = (f32[4608]{0:T(1024)S(1)}, f32[4608]{0:T(1024)}, u32[]{:S(2)}) copy-start(f32[4608]{0:T(1024)} %param.5) | copy-start | bytes 55300
  150.5 1.3 collective-permute-start.19
  (1 other events, 11.2 us)

commit v3 on v2

--- a/solution.py
+++ b/solution.py
@@ -257,8 +257,8 @@
 
 
 def near_kernel(place, turned, weight, arrived, gathered, *rest):
-    sends, gain_out = rest[:4], rest[4]
-    weight_held, arrived_held, rows_held, held, in_sems, out_sems = rest[5:]
+    sends = rest[:4]
+    weight_held, arrived_held, rows_held, held, in_sems, out_sems = rest[4:]
     core, y, x = place[0], place[1], place[2]
 
     def arrivals(j):
@@ -279,9 +279,12 @@
         columns = step_columns(j)
         part = jnp.dot(turned[...], weight_held[:, columns], preferred_element_type=jnp.float32)
         part = part + arrived_held[:, columns].astype(jnp.float32)
-        gain_out[:, columns] = jnp.sum(
-            part * rows_held[:, columns].astype(jnp.float32), axis=0, keepdims=True
-        )
+        gain = jnp.sum(part * rows_held[:, columns].astype(jnp.float32), axis=0, keepdims=True)
+        high = gain.astype(jnp.bfloat16).astype(jnp.float32)
+        row = lax.broadcasted_iota(jnp.int32, (PIECE, STEP), 0)
+        gain_piece = jnp.where(row == 0, high, jnp.where(row == 1, gain - high, 0.0)).astype(jnp.bfloat16)
+        for k in range(4):
+            held[k, 8, :, columns] = gain_piece
         rounded = part.astype(jnp.bfloat16)
         for to_y in range(4):
             for to_x in range(4):
@@ -289,7 +292,7 @@
                 outer, inner = jnp.where(core == 0, up_y, up_x), jnp.where(core == 0, up_x, up_y)
                 for owner in range(2):
                     row = (((to_x % 2 * 4 + to_y) * 2 + owner) * 2 + to_x // 2) * PIECE
-                    held[outer, inner, owner, :, columns] = rounded[row : row + PIECE]
+                    held[outer, inner * 2 + owner, :, columns] = rounded[row : row + PIECE]
 
     steps(begin, 0, HALF_STEPS)
     steps(multiply, 0, HALF_STEPS)
@@ -301,17 +304,16 @@
 
 
 def near_gradient(place, turned, weight, arrived, gathered):
-    outs = pl.pallas_call(
+    return pl.pallas_call(
         near_kernel,
-        out_shape=[jax.ShapeDtypeStruct((4, 2, PIECE, HALF), jnp.bfloat16)] * 4
-        + [jax.ShapeDtypeStruct((1, HALF), jnp.float32)],
+        out_shape=[jax.ShapeDtypeStruct((9, PIECE, HALF), jnp.bfloat16)] * 4,
         in_specs=[SCALARS, IN_VMEM, IN_HBM, ANYWHERE, IN_HBM],
-        out_specs=[ANYWHERE] * 4 + [IN_VMEM],
+        out_specs=[ANYWHERE] * 4,
         scratch_shapes=[
             pltpu.VMEM((VOCAB_ROWS, HALF), jnp.bfloat16),
             pltpu.VMEM((TOKENS, HALF), jnp.bfloat16),
             pltpu.VMEM((TOKENS, HALF), jnp.bfloat16),
-            pltpu.VMEM((4, 4, 2, PIECE, HALF), jnp.bfloat16),
+            pltpu.VMEM((4, 9, PIECE, HALF), jnp.bfloat16),
             pltpu.SemaphoreType.DMA((3, HALF_STEPS)),
             pltpu.SemaphoreType.DMA((4,)),
         ],
@@ -321,7 +323,6 @@
         ),
         name="near_gradient",
     )(place, turned, weight, arrived, gathered)
-    return outs[:4], outs[4]
 
 
 def weight_kernel(grad, gathered, out, rows_held, out_held, in_sems, out_sems):
@@ -396,20 +397,27 @@
 
     grad, turned, far_part = far_gradient(place, ids, capped, stats, weight)
     arrived = swap_cores(far_part)
-    sends, gain_part = near_gradient(place, turned, weight, arrived, gathered)
+    sends = near_gradient(place, turned, weight, arrived, gathered)
+
+    def gain_rows(piece):
+        gain = piece[0:1] + piece[1:2]
+        high = lax.reduce_precision(gain, 8, 7)
+        return jnp.concatenate([high, gain - high], axis=0).astype(jnp.bfloat16)
+
     parts = send_ring(sends, shift_second)
-    gain_part, parts[1] = lax.optimization_barrier((gain_part, parts[1]))
-    gain_part = sum_over(gain_part, PLANE, 16)
-    half_sum = total(parts).astype(jnp.bfloat16)
-    line_part = total(send_ring([half_sum[k] for k in range(4)], shift_first)).astype(jnp.bfloat16)
+    grad, parts[1] = lax.optimization_barrier((grad, parts[1]))
+    grad_weight = weight_gradient(grad, gathered)
+    grad_weight, *parts = lax.optimization_barrier((grad_weight, *parts))
+    half_sum = total(parts)
+    half_rows = half_sum[:8].astype(jnp.bfloat16)
+    gain_piece = jnp.pad(gain_rows(half_sum[8]), ((0, PIECE - 2), (0, 0)))[None]
+    pieces = [jnp.concatenate([half_rows[2 * k : 2 * k + 2], gain_piece], axis=0) for k in range(4)]
+    line_sum = total(send_ring(pieces, shift_first))
+    line_part = line_sum[:2].astype(jnp.bfloat16)
     line_part = line_part.reshape(2, 8, 2, HALF).transpose(1, 0, 2, 3).reshape(8, 4, HALF)
-    gain_high = lax.reduce_precision(gain_part, 8, 7)
-    gain_rows = jnp.concatenate([gain_high, gain_part - gain_high], axis=0).astype(jnp.bfloat16)
-    message = jnp.concatenate([line_part, jnp.broadcast_to(gain_rows[None], (8, 2, HALF))], axis=1)
-    message, grad = lax.optimization_barrier((message, grad))
+    gain_pair = gain_rows(line_sum[2])
+    message = jnp.concatenate([line_part, jnp.broadcast_to(gain_pair[None], (8, 2, HALF))], axis=1)
     line_parts = lax.all_to_all(message, "z", 0, 0, tiled=True)
-    grad_weight = weight_gradient(grad, gathered)
-    line_parts, grad_weight = lax.optimization_barrier((line_parts, grad_weight))
     line_sum = jnp.sum(line_parts.astype(jnp.float32), axis=0)
     gain_sum = line_sum[4:5] + line_sum[5:6]
     first_core, second_core = line_sum[0:2], line_sum[2:4]

time: 157 us -> 160 us (1.019)
  waiting for transfers between devices: 48.2 us -> 57.7 us
  starting transfers between devices: 31.5 us -> 26.3 us
    all_to_all x1, waiting for transfers between devices: 4.11 us -> 9.73 us  [on_device(): line_parts = lax.all_to_all(message, 'z', 0, 0, tiled=True)]
    all_to_all x1 -> x0, starting transfers between devices: 3.52 us -> none  [gather_over(): return lax.all_to_all(copies, axes, 0, 0, tiled=True)]
    ppermute x6, waiting for transfers between devices: 6.95 us -> 10.4 us  [shift_first(): return lax.ppermute(block, CROSS, cross_pairs(step, 0))]
    ppermute x6, starting transfers between devices: 11.1 us -> 9.5 us  [shift_first(): return lax.ppermute(block, CROSS, cross_pairs(step, 0))]
    convert_element_type x2 -> x0, other arithmetic: 1.62 us -> none  [the longest x1 1.54 us: on_device(): half_sum = total(parts).astype(jnp.bfloat16)]
  transfers between devices with their start and end apart: 22 -> 21, of which waited for: 15 -> 14; matrix products, arithmetic and copies ran while one was open for 2% -> 0% of each run, Pallas kernels for 4% -> 4%
where the time goes in v3:
time: 160 us; the launch traced here: 157 us
  waiting for transfers between devices  57.7 us (36%)
  blocking collectives  40.7 us (25%)
  starting transfers between devices  26.3 us (16%)
  Pallas kernels  24.6 us (15%)
  other arithmetic  4.96 us (3%)
    all_to_all x3, blocking collectives, gather_over(): return lax.all_to_all(copies, axes, 0, 0, tiled=True)  40.7 us
    ppermute x6, waiting for transfers between devices, shift_second(): return lax.ppermute(block, CROSS, cross_pairs(step, 1))  28 us
    ppermute x6, waiting for transfers between devices, shift_first(): return lax.ppermute(block, CROSS, cross_pairs(step, 0))  10.4 us
    ppermute x6, starting transfers between devices, shift_second(): return lax.ppermute(block, CROSS, cross_pairs(step, 1))  9.97 us
    all_to_all x1, waiting for transfers between devices, on_device(): line_parts = lax.all_to_all(message, 'z', 0, 0, tiled=True)  9.73 us
    ppermute x8, waiting for transfers between devices, swap_cores(): return lax.ppermute(block, 'core', [(0, 1), (1, 0)])  9.63 us
    ppermute x6, starting transfers between devices, shift_first(): return lax.ppermute(block, CROSS, cross_pairs(step, 0))  9.5 us
    pallas_call x1, Pallas kernels, forward(): pl.pallas_call(forward_kernel, out_shape=(jax.ShapeDtypeStruct((TOKENS, W...  8.81 us
  transfers between devices with their start and end apart: 21, of which 14 were waited for; matrix products, arithmetic and copies ran while one was open for 0% of the time, Pallas kernels for 4%

profile of v3, /device:TPU:32, one launch (start us, length us, event | category | flops | bytes accessed | tf_op | source)
XLA Modules:
  0.0 156.7 jit_solution(5500817916105872700)
XLA Ops:
  3.8 16.7 %all_to_all.20 = bf16[8,4,2304]{2,1,0:T(4,128)(2,1)S(1)} all-to-all(bf16[8,4,2304]{2,1,0:T(4,128)(2,1)S(1)} %broadcast_in_dim.10), channel_id=1, replica_groups=mesh['x_lo'=2,'y'=4,'core'=2,'x_hi'=2,'z'=8] {'z'}, dimensions={0} | all-to-all | bytes 294912 | tf_op jit(solution)/shard_map/all_to_all | solution.py:51
  20.6 1.6 %collective-permute-start.3 = (bf16[2,16,2304]{2,1,0:T(8,128)(2,1)S(1)}, bf16[2,16,2304]{2,1,0:T(8,128)(2,1)S(1)}, u32[]{:S(2)}, u32[]{:S(2)}) collective-permute-start(bf16[2,16,2304]{2,1,0:T(8,128)(2,1)S(1)} %reshape.151), channel_id=1, source_target_pairs={{0,128},{16,48},{32,160},{48,80},{64,192},{80,112},{96,224},{112,1... | collective-permute-start | bytes 442376 | tf_op jit(solution)/shard_map/ppermute | solution.py:38
  22.2 2.7 %collective-permute-start.2 = (bf16[2,16,2304]{2,1,0:T(8,128)(2,1)S(1)}, bf16[2,16,2304]{2,1,0:T(8,128)(2,1)S(1)}, u32[]{:S(2)}, u32[]{:S(2)}) collective-permute-start(bf16[2,16,2304]{2,1,0:T(8,128)(2,1)S(1)} %reshape.151), channel_id=1, source_target_pairs={{0,8},{16,80},{32,40},{48,112},{64,72},{80,16},{96,104},{112,48},{... | collective-permute-start | bytes 442376 | tf_op jit(solution)/shard_map/ppermute | solution.py:38
  24.9 1.4 collective-permute-start.1
  27.1 2.6 %collective-permute-done.2 = bf16[2,16,2304]{2,1,0:T(8,128)(2,1)S(1)} collective-permute-done((bf16[2,16,2304]{2,1,0:T(8,128)(2,1)S(1)}, bf16[2,16,2304]{2,1,0:T(8,128)(2,1)S(1)}, u32[]{:S(2)}, u32[]{:S(2)}) %collective-permute-start.2) | collective-permute-done | bytes 147488 | tf_op jit(solution)/shard_map/ppermute | solution.py:38
  30.2 1.7 %collective-permute-start.6 = (bf16[4,2,16,2304]{3,2,1,0:T(8,128)(2,1)S(1)}, bf16[4,2,16,2304]{3,2,1,0:T(8,128)(2,1)S(1)}, u32[]{:S(2)}, u32[]{:S(2)}) collective-permute-start(bf16[4,2,16,2304]{3,2,1,0:T(8,128)(2,1)S(1)} %pad_maximum_fusion.rest_0_), channel_id=1, source_target_pairs={{0,32},{16,144},{32,64},{48,176},{64,96},{80,208},{96,0},{112,240}... | collective-permute-start | bytes 1769480 | tf_op jit(solution)/shard_map/ppermute | solution.py:42
  31.8 2.9 %collective-permute-start.5 = (bf16[4,2,16,2304]{3,2,1,0:T(8,128)(2,1)S(1)}, bf16[4,2,16,2304]{3,2,1,0:T(8,128)(2,1)S(1)}, u32[]{:S(2)}, u32[]{:S(2)}) collective-permute-start(bf16[4,2,16,2304]{3,2,1,0:T(8,128)(2,1)S(1)} %pad_maximum_fusion.rest_0_), channel_id=1, source_target_pairs={{0,64},{16,24},{32,96},{48,56},{64,0},{80,88},{96,32},{112,120},{1... | collective-permute-start | bytes 1769480 | tf_op jit(solution)/shard_map/ppermute | solution.py:42
  34.7 1.3 collective-permute-start.4
  36.1 5.3 %collective-permute-done.6.rest_3_ = bf16[4,2,16,2304]{3,2,1,0:T(8,128)(2,1)S(1)} collective-permute-done((bf16[4,2,16,2304]{3,2,1,0:T(8,128)(2,1)S(1)}, bf16[4,2,16,2304]{3,2,1,0:T(8,128)(2,1)S(1)}, u32[]{:S(2)}, u32[]{:S(2)}) %collective-permute-start.6) | collective-permute-done | bytes 589856 | tf_op jit(solution)/shard_map/ppermute | solution.py:42
  41.3 7.6 %collective-permute-done.5.rest_2_ = bf16[4,2,16,2304]{3,2,1,0:T(8,128)(2,1)S(1)} collective-permute-done((bf16[4,2,16,2304]{3,2,1,0:T(8,128)(2,1)S(1)}, bf16[4,2,16,2304]{3,2,1,0:T(8,128)(2,1)S(1)}, u32[]{:S(2)}, u32[]{:S(2)}) %collective-permute-start.5) | collective-permute-done | bytes 589856 | tf_op jit(solution)/shard_map/ppermute | solution.py:42
  49.5 2.3 %collective-permute-done.9.rest_6_ = bf16[4,2,16,2304]{3,2,1,0:T(8,128)(2,1)} collective-permute-done((bf16[4,2,16,2304]{3,2,1,0:T(8,128)(2,1)S(1)}, bf16[4,2,16,2304]{3,2,1,0:T(8,128)(2,1)}, u32[]{:S(2)}, u32[]{:S(2)}) %collective-permute-start.9) | collective-permute-done | bytes 589856 | tf_op jit(solution)/shard_map/ppermute | solution.py:46
  51.8 8.8 %forward.1 = (bf16[512,4608]{1,0:T(8,128)(2,1)}, f32[512,512]{1,0:T(8,128)}, f32[3,512]{1,0:T(4,128)S(1)}) custom-call(s32[4]{0:T(128)S(1)} %pad_add_fusion.place, s32[1,512]{1,0:T(1,128)S(1)} %bitcast.25, bf16[512,4608]{1,0:T(8,128)(2,1)} %weight.5, bf16[4,2,16,2304]{3,2,1,0:T(8,128)(2,1)S(1)} %pad_maximum_fusion.rest_0_, ...), custom_call_target="tpu_custom_call" | custom-call | flops 2415919104 | bytes 16777216 | tf_op jit(solution)/shard_map/forward/pallas_call | solution.py:164
  62.7 13.3 %all_to_all.21 = f32[16,3,512]{2,1,0:T(4,128)S(1)} all-to-all(f32[16,3,512]{2,1,0:T(4,128)S(1)} %broadcast_in_dim.11), channel_id=1, replica_groups=mesh['x_lo'=2,'y'=4,'core'=2,'x_hi'=2,'z'=8] {'x_lo','y','x_hi'}, dimensions={0} | all-to-all | bytes 196608 | tf_op jit(solution)/shard_map/all_to_all | solution.py:51
  76.1 10.8 %all_to_all.22 = f32[8,3,512]{2,1,0:T(4,128)S(1)} all-to-all(f32[8,3,512]{2,1,0:T(4,128)S(1)} %broadcast_in_dim.12), channel_id=1, replica_groups=mesh['x_lo'=2,'y'=4,'core'=2,'x_hi'=2,'z'=8] {'z'}, dimensions={0} | all-to-all | bytes 98304 | tf_op jit(solution)/shard_map/all_to_all | solution.py:51
  86.9 5.0 %far_gradient.1 = (bf16[512,512]{1,0:T(8,128)(2,1)S(1)}, bf16[512,512]{1,0:T(8,128)(2,1)S(1)}, bf16[512,2304]{1,0:T(8,128)(2,1)}) custom-call(s32[4]{0:T(128)S(1)} %pad_add_fusion.place, s32[1,512]{1,0:T(1,128)S(1)} %bitcast.26, f32[512,512]{1,0:T(8,128)} %get-tuple-element.22.capped, f32[3,512]{1,0:T(4,128)S(1)} %reduce_sum.47.totals, bf16[512,4608]{1,0:T(8,128)(2,1)} %weight.5), custom_call_target="tpu_custom_call" | custom-call | flops 1207959552 | bytes 9437184 | tf_op jit(solution)/shard_map/far_gradient/pallas_call | solution.py:236
  92.0 4.7 %collective-permute-done.12.arrived = bf16[512,2304]{1,0:T(8,128)(2,1)S(1)} collective-permute-done((bf16[512,2304]{1,0:T(8,128)(2,1)}, bf16[512,2304]{1,0:T(8,128)(2,1)S(1)}, u32[]{:S(2)}, u32[]{:S(2)}) %collective-permute-start.12) | collective-permute-done | bytes 2359328 | tf_op jit(solution)/shard_map/ppermute | solution.py:46
  96.8 5.2 %near_gradient.1 = (bf16[9,16,2304]{2,1,0:T(8,128)(2,1)S(1)}, bf16[9,16,2304]{2,1,0:T(8,128)(2,1)S(1)}, bf16[9,16,2304]{2,1,0:T(8,128)(2,1)S(1)}, bf16[9,16,2304]{2,1,0:T(8,128)(2,1)S(1)}) custom-call(s32[4]{0:T(128)S(1)} %pad_add_fusion.place, bf16[512,512]{1,0:T(8,128)(2,1)S(1)} %get-tuple-element.24.turned, bf16[512,4608]{1,0:T(8,128)(2,1)} %weight.5, ...), custom_call_target="tpu_custom_call" | custom-call | flops 1207959552 | bytes 12582912 | tf_op jit(solution)/shard_map/near_gradient/pallas_call | solution.py:307
  102.7 2.2 %collective-permute-start.14 = (bf16[9,16,2304]{2,1,0:T(8,128)(2,1)S(1)}, bf16[9,16,2304]{2,1,0:T(8,128)(2,1)S(1)}, u32[]{:S(2)}, u32[]{:S(2)}) collective-permute-start(bf16[9,16,2304]{2,1,0:T(8,128)(2,1)S(1)} %get-tuple-element.31), channel_id=1, source_target_pairs={{0,64},{16,24},{32,96},{48,56},{64,0},{80,88},{96,32},{112,120},{1... | collective-permute-start | bytes 1990664 | tf_op jit(solution)/shard_map/ppermute | solution.py:42
  106.0 15.2 %collective-permute-done.13 = bf16[9,16,2304]{2,1,0:T(8,128)(2,1)S(1)} collective-permute-done((bf16[9,16,2304]{2,1,0:T(8,128)(2,1)S(1)}, bf16[9,16,2304]{2,1,0:T(8,128)(2,1)S(1)}, u32[]{:S(2)}, u32[]{:S(2)}) %collective-permute-start.13) | collective-permute-done | bytes 663584 | tf_op jit(solution)/shard_map/ppermute | solution.py:42
  121.2 5.6 %weight_gradient.1 = bf16[512,4608]{1,0:T(8,128)(2,1)} custom-call(bf16[512,512]{1,0:T(8,128)(2,1)S(1)} %get-tuple-element.28.grad, bf16[512,4608]{1,0:T(8,128)(2,1)} %get-tuple-element.26.gathered), custom_call_target="tpu_custom_call" | custom-call | flops 2415919104 | bytes 10485760 | tf_op jit(solution)/shard_map/weight_gradient/pallas_call | solution.py:351
  128.1 2.2 %collective-permute-start.17 = (bf16[3,16,2304]{2,1,0:T(8,128)(2,1)S(1)}, bf16[3,16,2304]{2,1,0:T(8,128)(2,1)S(1)}, u32[]{:S(2)}, u32[]{:S(2)}) collective-permute-start(bf16[3,16,2304]{2,1,0:T(8,128)(2,1)S(1)} %get-tuple-element.51), channel_id=1, source_target_pairs={{0,8},{16,80},{32,40},{48,112},{64,72},{80,16},{96,104},{112,48},{... | collective-permute-start | bytes 663560 | tf_op jit(solution)/shard_map/ppermute | solution.py:38
  131.2 5.8 %collective-permute-done.16 = bf16[3,16,2304]{2,1,0:T(8,128)(2,1)S(1)} collective-permute-done((bf16[3,16,2304]{2,1,0:T(8,128)(2,1)S(1)}, bf16[3,16,2304]{2,1,0:T(8,128)(2,1)S(1)}, u32[]{:S(2)}, u32[]{:S(2)}) %collective-permute-start.16) | collective-permute-done | bytes 221216 | tf_op jit(solution)/shard_map/ppermute | solution.py:38
  139.1 4.8 %all-to-all-start.3 = ((bf16[8,6,2304]{2,1,0:T(8,128)(2,1)}), bf16[8,6,2304]{2,1,0:T(8,128)(2,1)S(1)}, u32[]{:S(2)}, u32[]{:S(2)}) async-start(bf16[8,6,2304]{2,1,0:T(8,128)(2,1)} %copy.27), calls=%async_computation.3 | async-start | bytes 589824 | tf_op jit(solution)/shard_map/all_to_all | solution.py:420
  143.9 9.7 %all-to-all-done.3 = bf16[8,6,2304]{2,1,0:T(8,128)(2,1)S(1)} async-done(((bf16[8,6,2304]{2,1,0:T(8,128)(2,1)}), bf16[8,6,2304]{2,1,0:T(8,128)(2,1)S(1)}, u32[]{:S(2)}, u32[]{:S(2)}) %all-to-all-start.3) | async-done | bytes 221216 | tf_op jit(solution)/shard_map/all_to_all | solution.py:420
  (76 shorter events, 16.5 us)
Async XLA Ops:
  2.4 1.3 collective-permute-start
  3.7 48.0 %copy-start = (s32[512]{0:T(512)S(1)}, s32[512]{0:T(512)}, u32[]{:S(2)}) copy-start(s32[512]{0:T(512)} %param.7) | copy-start | bytes 6148
  20.6 6.4 %collective-permute-start.3 = (bf16[2,16,2304]{2,1,0:T(8,128)(2,1)S(1)}, bf16[2,16,2304]{2,1,0:T(8,128)(2,1)S(1)}, u32[]{:S(2)}, u32[]{:S(2)}) collective-permute-start(bf16[2,16,2304]{2,1,0:T(8,128)(2,1)S(1)} %reshape.151), channel_id=1, source_target_pairs={{0,128},{16,48},{32,160},{48,80},{64,192},{80,112},{96,224},{112,1... | collective-permute-start | bytes 442376 | tf_op jit(solution)/shard_map/ppermute | solution.py:38
  22.2 7.4 %collective-permute-start.2 = (bf16[2,16,2304]{2,1,0:T(8,128)(2,1)S(1)}, bf16[2,16,2304]{2,1,0:T(8,128)(2,1)S(1)}, u32[]{:S(2)}, u32[]{:S(2)}) collective-permute-start(bf16[2,16,2304]{2,1,0:T(8,128)(2,1)S(1)} %reshape.151), channel_id=1, source_target_pairs={{0,8},{16,80},{32,40},{48,112},{64,72},{80,16},{96,104},{112,48},{... | collective-permute-start | bytes 442376 | tf_op jit(solution)/shard_map/ppermute | solution.py:38
  24.9 5.1 %collective-permute-start.1 = (bf16[2,16,2304]{2,1,0:T(8,128)(2,1)S(1)}, bf16[2,16,2304]{2,1,0:T(8,128)(2,1)S(1)}, u32[]{:S(2)}, u32[]{:S(2)}) collective-permute-start(bf16[2,16,2304]{2,1,0:T(8,128)(2,1)S(1)} %reshape.151), channel_id=1, source_target_pairs={{0,136},{16,112},{32,168},{48,16},{64,200},{80,48},{96,232},{112,8... | collective-permute-start | bytes 442376 | tf_op jit(solution)/shard_map/ppermute | solution.py:38
  30.2 11.2 %collective-permute-start.6 = (bf16[4,2,16,2304]{3,2,1,0:T(8,128)(2,1)S(1)}, bf16[4,2,16,2304]{3,2,1,0:T(8,128)(2,1)S(1)}, u32[]{:S(2)}, u32[]{:S(2)}) collective-permute-start(bf16[4,2,16,2304]{3,2,1,0:T(8,128)(2,1)S(1)} %pad_maximum_fusion.rest_0_), channel_id=1, source_target_pairs={{0,32},{16,144},{32,64},{48,176},{64,96},{80,208},{96,0},{112,240}... | collective-permute-start | bytes 1769480 | tf_op jit(solution)/shard_map/ppermute | solution.py:42
  31.8 17.1 %collective-permute-start.5 = (bf16[4,2,16,2304]{3,2,1,0:T(8,128)(2,1)S(1)}, bf16[4,2,16,2304]{3,2,1,0:T(8,128)(2,1)S(1)}, u32[]{:S(2)}, u32[]{:S(2)}) collective-permute-start(bf16[4,2,16,2304]{3,2,1,0:T(8,128)(2,1)S(1)} %pad_maximum_fusion.rest_0_), channel_id=1, source_target_pairs={{0,64},{16,24},{32,96},{48,56},{64,0},{80,88},{96,32},{112,120},{1... | collective-permute-start | bytes 1769480 | tf_op jit(solution)/shard_map/ppermute | solution.py:42
  34.7 14.2 %collective-permute-start.4 = (bf16[4,2,16,2304]{3,2,1,0:T(8,128)(2,1)S(1)}, bf16[4,2,16,2304]{3,2,1,0:T(8,128)(2,1)S(1)}, u32[]{:S(2)}, u32[]{:S(2)}) collective-permute-start(bf16[4,2,16,2304]{3,2,1,0:T(8,128)(2,1)S(1)} %pad_maximum_fusion.rest_0_), channel_id=1, source_target_pairs={{0,96},{16,152},{32,0},{48,184},{64,32},{80,216},{96,64},{112,248}... | collective-permute-start | bytes 1769480 | tf_op jit(solution)/shard_map/ppermute | solution.py:42
  36.1 13.4 %collective-permute-start.7 = (bf16[4,2,16,2304]{3,2,1,0:T(8,128)(2,1)S(1)}, bf16[4,2,16,2304]{3,2,1,0:T(8,128)(2,1)S(1)}, u32[]{:S(2)}, u32[]{:S(2)}) collective-permute-start(bf16[4,2,16,2304]{3,2,1,0:T(8,128)(2,1)S(1)} %pad_maximum_fusion.rest_0_), channel_id=1, source_target_pairs={{0,16},{16,0},{1,17},{17,1},{2,18},{18,2},{3,19},{19,3},{4,20},{20... | collective-permute-start | bytes 1769480 | tf_op jit(solution)/shard_map/ppermute | solution.py:46
  41.3 8.2 %collective-permute-start.10 = (bf16[4,2,16,2304]{3,2,1,0:T(8,128)(2,1)S(1)}, bf16[4,2,16,2304]{3,2,1,0:T(8,128)(2,1)}, u32[]{:S(2)}, u32[]{:S(2)}) collective-permute-start(bf16[4,2,16,2304]{3,2,1,0:T(8,128)(2,1)S(1)} %collective-permute-done.6.rest_3_), channel_id=1, source_target_pairs={{0,16},{16,0},{1,17},{17,1},{2,18},{18,2},{3,19},{19,3},{4,20},{20... | collective-permute-start | bytes 1769480 | tf_op jit(solution)/shard_map/ppermute | solution.py:46
  48.9 2.9 %collective-permute-start.9 = (bf16[4,2,16,2304]{3,2,1,0:T(8,128)(2,1)S(1)}, bf16[4,2,16,2304]{3,2,1,0:T(8,128)(2,1)}, u32[]{:S(2)}, u32[]{:S(2)}) collective-permute-start(bf16[4,2,16,2304]{3,2,1,0:T(8,128)(2,1)S(1)} %collective-permute-done.5.rest_2_), channel_id=1, source_target_pairs={{0,16},{16,0},{1,17},{17,1},{2,18},{18,2},{3,19},{19,3},{4,20},{20... | collective-permute-start | bytes 1769480 | tf_op jit(solution)/shard_map/ppermute | solution.py:46
  48.9 2.9 %collective-permute-start.8 = (bf16[4,2,16,2304]{3,2,1,0:T(8,128)(2,1)S(1)}, bf16[4,2,16,2304]{3,2,1,0:T(8,128)(2,1)S(1)}, u32[]{:S(2)}, u32[]{:S(2)}) collective-permute-start(bf16[4,2,16,2304]{3,2,1,0:T(8,128)(2,1)S(1)} %collective-permute-done.4.rest_1_), channel_id=1, source_target_pairs={{0,16},{16,0},{1,17},{17,1},{2,18},{18,2},{3,19},{19,3},{4,20},{20... | collective-permute-start | bytes 1769480 | tf_op jit(solution)/shard_map/ppermute | solution.py:46
  60.6 2.1 %collective-permute-start.11 = (f32[3,512]{1,0:T(4,128)S(1)}, f32[3,512]{1,0:T(4,128)S(1)}, u32[]{:S(2)}, u32[]{:S(2)}) collective-permute-start(f32[3,512]{1,0:T(4,128)S(1)} %get-tuple-element.21), channel_id=1, source_target_pairs={{0,16},{16,0},{1,17},{17,1},{2,18},{18,2},{3,19},{19,3},{4,20},{20... | collective-permute-start | bytes 18440 | tf_op jit(solution)/shard_map/ppermute | solution.py:46
  91.9 4.8 %collective-permute-start.12 = (bf16[512,2304]{1,0:T(8,128)(2,1)}, bf16[512,2304]{1,0:T(8,128)(2,1)S(1)}, u32[]{:S(2)}, u32[]{:S(2)}) collective-permute-start(bf16[512,2304]{1,0:T(8,128)(2,1)} %get-tuple-element.25), channel_id=1, source_target_pairs={{0,16},{16,0},{1,17},{17,1},{2,18},{18,2},{3,19},{19,3},{4,20},{20... | collective-permute-start | bytes 7077896 | tf_op jit(solution)/shard_map/ppermute | solution.py:46
  102.0 19.3 %collective-permute-start.13 = (bf16[9,16,2304]{2,1,0:T(8,128)(2,1)S(1)}, bf16[9,16,2304]{2,1,0:T(8,128)(2,1)S(1)}, u32[]{:S(2)}, u32[]{:S(2)}) collective-permute-start(bf16[9,16,2304]{2,1,0:T(8,128)(2,1)S(1)} %get-tuple-element.27), channel_id=1, source_target_pairs={{0,32},{16,144},{32,64},{48,176},{64,96},{80,208},{96,0},{112,240}... | collective-permute-start | bytes 1990664 | tf_op jit(solution)/shard_map/ppermute | solution.py:42
  102.7 24.1 %collective-permute-start.14 = (bf16[9,16,2304]{2,1,0:T(8,128)(2,1)S(1)}, bf16[9,16,2304]{2,1,0:T(8,128)(2,1)S(1)}, u32[]{:S(2)}, u32[]{:S(2)}) collective-permute-start(bf16[9,16,2304]{2,1,0:T(8,128)(2,1)S(1)} %get-tuple-element.31), channel_id=1, source_target_pairs={{0,64},{16,24},{32,96},{48,56},{64,0},{80,88},{96,32},{112,120},{1... | collective-permute-start | bytes 1990664 | tf_op jit(solution)/shard_map/ppermute | solution.py:42
  104.9 22.0 %collective-permute-start.15 = (bf16[9,16,2304]{2,1,0:T(8,128)(2,1)S(1)}, bf16[9,16,2304]{2,1,0:T(8,128)(2,1)S(1)}, u32[]{:S(2)}, u32[]{:S(2)}) collective-permute-start(bf16[9,16,2304]{2,1,0:T(8,128)(2,1)S(1)} %get-tuple-element.32), channel_id=1, source_target_pairs={{0,96},{16,152},{32,0},{48,184},{64,32},{80,216},{96,64},{112,248}... | collective-permute-start | bytes 1990664 | tf_op jit(solution)/shard_map/ppermute | solution.py:42
  127.4 9.6 %collective-permute-start.16 = (bf16[3,16,2304]{2,1,0:T(8,128)(2,1)S(1)}, bf16[3,16,2304]{2,1,0:T(8,128)(2,1)S(1)}, u32[]{:S(2)}, u32[]{:S(2)}) collective-permute-start(bf16[3,16,2304]{2,1,0:T(8,128)(2,1)S(1)} %get-tuple-element.50), channel_id=1, source_target_pairs={{0,128},{16,48},{32,160},{48,80},{64,192},{80,112},{96,224},{112,1... | collective-permute-start | bytes 663560 | tf_op jit(solution)/shard_map/ppermute | solution.py:38
  128.1 8.9 %collective-permute-start.17 = (bf16[3,16,2304]{2,1,0:T(8,128)(2,1)S(1)}, bf16[3,16,2304]{2,1,0:T(8,128)(2,1)S(1)}, u32[]{:S(2)}, u32[]{:S(2)}) collective-permute-start(bf16[3,16,2304]{2,1,0:T(8,128)(2,1)S(1)} %get-tuple-element.51), channel_id=1, source_target_pairs={{0,8},{16,80},{32,40},{48,112},{64,72},{80,16},{96,104},{112,48},{... | collective-permute-start | bytes 663560 | tf_op jit(solution)/shard_map/ppermute | solution.py:38
  130.2 7.7 %collective-permute-start.18 = (bf16[3,16,2304]{2,1,0:T(8,128)(2,1)S(1)}, bf16[3,16,2304]{2,1,0:T(8,128)(2,1)S(1)}, u32[]{:S(2)}, u32[]{:S(2)}) collective-permute-start(bf16[3,16,2304]{2,1,0:T(8,128)(2,1)S(1)} %get-tuple-element.52), channel_id=1, source_target_pairs={{0,136},{16,112},{32,168},{48,16},{64,200},{80,48},{96,232},{112,8... | collective-permute-start | bytes 663560 | tf_op jit(solution)/shard_map/ppermute | solution.py:38
  138.2 16.9 %copy-start.1 = (f32[4608]{0:T(1024)S(1)}, f32[4608]{0:T(1024)}, u32[]{:S(2)}) copy-start(f32[4608]{0:T(1024)} %param.5) | copy-start | bytes 55300
  138.2 16.9 %copy-start.2 = (bf16[2,4608]{1,0:T(2,128)(2,1)S(1)}, bf16[2,4608]{1,0:T(2,128)(2,1)}, u32[]{:S(2)}) copy-start(bf16[2,4608]{1,0:T(2,128)(2,1)} %param.4) | copy-start | bytes 55300
  139.1 14.5 %all-to-all-start.3 = ((bf16[8,6,2304]{2,1,0:T(8,128)(2,1)}), bf16[8,6,2304]{2,1,0:T(8,128)(2,1)S(1)}, u32[]{:S(2)}, u32[]{:S(2)}) async-start(bf16[8,6,2304]{2,1,0:T(8,128)(2,1)} %copy.27), calls=%async_computation.3 | async-start | bytes 589824 | tf_op jit(solution)/shard_map/all_to_all | solution.py:420
  153.7 1.3 collective-permute-start.19

commit v4 on v3

--- a/solution.py
+++ b/solution.py
@@ -378,22 +378,15 @@
     unit_rows = values * inverse
     normed = (unit_rows * norm_gain).astype(jnp.bfloat16)
 
-    def by_core(mine, other, axis):
-        return jnp.where(
-            core == 0, jnp.concatenate([mine, other], axis), jnp.concatenate([other, mine], axis)
-        )
-
-    mine = lax.dynamic_slice_in_dim(normed, core * HALF, HALF, 1)
-    other = swap_cores(lax.dynamic_slice_in_dim(normed, (1 - core) * HALF, HALF, 1))
-    line = gather_over(by_core(mine, other, 0), "z", 8)
-    line = line.reshape(8, 2, 2, HALF).transpose(1, 0, 2, 3).reshape(2, PIECE, HALF)
+    halves = normed.reshape(2, 2, HALF).transpose(1, 0, 2)
+    halves = jnp.broadcast_to(halves[:, None], (2, 8, 2, HALF)).reshape(16, 2, HALF)
+    line = lax.all_to_all(halves, ("core", "z"), 0, 0, tiled=True).reshape(2, PIECE, HALF)
     blocks = gather_ring(jnp.stack(gather_ring(line, shift_first)), shift_second)
     blocks = blocks + [swap_cores(block) for block in blocks]
 
     gathered, capped, stats = forward(place, ids, weight, blocks)
-    stats = stats + swap_cores(stats)
     stats = sum_over(stats, PLANE, 16)
-    stats = sum_over(stats, "z", 8)
+    stats = sum_over(stats, ("core", "z"), 16)
 
     grad, turned, far_part = far_gradient(place, ids, capped, stats, weight)
     arrived = swap_cores(far_part)
@@ -414,18 +407,14 @@
     pieces = [jnp.concatenate([half_rows[2 * k : 2 * k + 2], gain_piece], axis=0) for k in range(4)]
     line_sum = total(send_ring(pieces, shift_first))
     line_part = line_sum[:2].astype(jnp.bfloat16)
-    line_part = line_part.reshape(2, 8, 2, HALF).transpose(1, 0, 2, 3).reshape(8, 4, HALF)
     gain_pair = gain_rows(line_sum[2])
-    message = jnp.concatenate([line_part, jnp.broadcast_to(gain_pair[None], (8, 2, HALF))], axis=1)
-    line_parts = lax.all_to_all(message, "z", 0, 0, tiled=True)
-    line_sum = jnp.sum(line_parts.astype(jnp.float32), axis=0)
-    gain_sum = line_sum[4:5] + line_sum[5:6]
-    first_core, second_core = line_sum[0:2], line_sum[2:4]
-    mine = jnp.concatenate([jnp.where(core == 0, first_core, second_core), gain_sum], axis=0)
-    theirs = jnp.concatenate([jnp.where(core == 0, second_core, first_core), gain_sum], axis=0)
-    whole = by_core(mine, swap_cores(theirs), 1)
-    grad_normed = whole[:2]
-    grad_gain = whole[2] / norm_gain
+    message = jnp.concatenate(
+        [line_part.reshape(16, 2, HALF), jnp.broadcast_to(gain_pair[None], (16, 2, HALF))], axis=1
+    )
+    line_parts = lax.all_to_all(message, ("core", "z"), 0, 0, tiled=True)
+    sums = jnp.sum(line_parts.astype(jnp.float32).reshape(2, 8, 4, HALF), axis=1)
+    grad_normed = jnp.concatenate([sums[0, :2], sums[1, :2]], axis=1)
+    grad_gain = (sums[:, 2] + sums[:, 3]).reshape(WIDTH) / norm_gain
 
     total_exp, total_weighted, target_logit = stats
     log_total = cap_value + jnp.log(total_exp)

time: 160 us -> 155 us (0.969); the launches traced: 157 us -> 154 us
  starting transfers between devices: 26.3 us -> 23.7 us
  blocking collectives: 40.7 us -> 42.4 us
    all_to_all x0 -> x1, blocking collectives: none -> 16.9 us  [on_device(): lax.all_to_all(halves, ('core', 'z'), 0, 0, tiled=True)]
    all_to_all x3 -> x2, blocking collectives: 40.7 us -> 25.5 us  [gather_over(): return lax.all_to_all(copies, axes, 0, 0, tiled=True)]
    ppermute x8 -> x5, waiting for transfers between devices: 9.63 us -> 7.04 us  [swap_cores(): return lax.ppermute(block, 'core', [(0, 1), (1, 0)])]
  transfers between devices with their start and end apart: 21 -> 18, of which waited for: 14 -> 11; matrix products, arithmetic and copies ran while one was open for 0% -> 0% of each run, Pallas kernels for 4% -> 4%
where the time goes in v4:
time: 155 us; the launch traced here: 154 us
  waiting for transfers between devices  56.4 us (36%)
  blocking collectives  42.4 us (27%)
  Pallas kernels  24.7 us (16%)
  starting transfers between devices  23.7 us (15%)
  other arithmetic  6.01 us (4%)
    ppermute x6, waiting for transfers between devices, shift_second(): return lax.ppermute(block, CROSS, cross_pairs(step, 1))  28 us
    all_to_all x2, blocking collectives, gather_over(): return lax.all_to_all(copies, axes, 0, 0, tiled=True)  25.5 us
    all_to_all x1, blocking collectives, on_device(): lax.all_to_all(halves, ('core', 'z'), 0, 0, tiled=True)  16.9 us
    all_to_all x1, waiting for transfers between devices, on_device(): line_parts = lax.all_to_all(message, ('core', 'z'), 0, 0, tiled=True)  11 us
    ppermute x6, waiting for transfers between devices, shift_first(): return lax.ppermute(block, CROSS, cross_pairs(step, 0))  10.3 us
    ppermute x6, starting transfers between devices, shift_second(): return lax.ppermute(block, CROSS, cross_pairs(step, 1))  9.78 us
    ppermute x6, starting transfers between devices, shift_first(): return lax.ppermute(block, CROSS, cross_pairs(step, 0))  9.6 us
    pallas_call x1, Pallas kernels, forward(): pl.pallas_call(forward_kernel, out_shape=(jax.ShapeDtypeStruct((TOKENS, W...  8.83 us
  transfers between devices with their start and end apart: 18, of which 11 were waited for; matrix products, arithmetic and copies ran while one was open for 0% of the time, Pallas kernels for 4%

profile of v4, /device:TPU:32, one launch (start us, length us, event | category | flops | bytes accessed | tf_op | source)
XLA Modules:
  0.0 154.5 jit_solution(6247464621515063598)
XLA Ops:
  2.5 16.9 %all_to_all.20 = bf16[16,2,2304]{2,1,0:T(2,128)(2,1)S(1)} all-to-all(bf16[16,2,2304]{2,1,0:T(2,128)(2,1)S(1)} %bitcast.30), channel_id=1, replica_groups=mesh['x_lo'=2,'y'=4,'core'=2,'x_hi'=2,'z'=8] {'core','z'}, dimensions={0} | all-to-all | bytes 294912 | tf_op jit(solution)/shard_map/all_to_all | solution.py:383
  19.5 1.6 %collective-permute-start.2 = (bf16[2,16,2304]{2,1,0:T(8,128)(2,1)S(1)}, bf16[2,16,2304]{2,1,0:T(8,128)(2,1)S(1)}, u32[]{:S(2)}, u32[]{:S(2)}) collective-permute-start(bf16[2,16,2304]{2,1,0:T(8,128)(2,1)S(1)} %reshape.134), channel_id=1, source_target_pairs={{0,128},{16,48},{32,160},{48,80},{64,192},{80,112},{96,224},{112,1... | collective-permute-start | bytes 442376 | tf_op jit(solution)/shard_map/ppermute | solution.py:38
  21.1 2.7 %collective-permute-start.1 = (bf16[2,16,2304]{2,1,0:T(8,128)(2,1)S(1)}, bf16[2,16,2304]{2,1,0:T(8,128)(2,1)S(1)}, u32[]{:S(2)}, u32[]{:S(2)}) collective-permute-start(bf16[2,16,2304]{2,1,0:T(8,128)(2,1)S(1)} %reshape.134), channel_id=1, source_target_pairs={{0,8},{16,80},{32,40},{48,112},{64,72},{80,16},{96,104},{112,48},{... | collective-permute-start | bytes 442376 | tf_op jit(solution)/shard_map/ppermute | solution.py:38
  23.8 1.4 collective-permute-start
  25.9 2.6 %collective-permute-done.1 = bf16[2,16,2304]{2,1,0:T(8,128)(2,1)S(1)} collective-permute-done((bf16[2,16,2304]{2,1,0:T(8,128)(2,1)S(1)}, bf16[2,16,2304]{2,1,0:T(8,128)(2,1)S(1)}, u32[]{:S(2)}, u32[]{:S(2)}) %collective-permute-start.1) | collective-permute-done | bytes 147488 | tf_op jit(solution)/shard_map/ppermute | solution.py:38
  29.0 1.7 %collective-permute-start.5 = (bf16[4,2,16,2304]{3,2,1,0:T(8,128)(2,1)S(1)}, bf16[4,2,16,2304]{3,2,1,0:T(8,128)(2,1)S(1)}, u32[]{:S(2)}, u32[]{:S(2)}) collective-permute-start(bf16[4,2,16,2304]{3,2,1,0:T(8,128)(2,1)S(1)} %pad_maximum_fusion.rest_0_), channel_id=1, source_target_pairs={{0,32},{16,144},{32,64},{48,176},{64,96},{80,208},{96,0},{112,240}... | collective-permute-start | bytes 1769480 | tf_op jit(solution)/shard_map/ppermute | solution.py:42
  30.7 2.9 %collective-permute-start.4 = (bf16[4,2,16,2304]{3,2,1,0:T(8,128)(2,1)S(1)}, bf16[4,2,16,2304]{3,2,1,0:T(8,128)(2,1)S(1)}, u32[]{:S(2)}, u32[]{:S(2)}) collective-permute-start(bf16[4,2,16,2304]{3,2,1,0:T(8,128)(2,1)S(1)} %pad_maximum_fusion.rest_0_), channel_id=1, source_target_pairs={{0,64},{16,24},{32,96},{48,56},{64,0},{80,88},{96,32},{112,120},{1... | collective-permute-start | bytes 1769480 | tf_op jit(solution)/shard_map/ppermute | solution.py:42
  33.6 1.3 collective-permute-start.3
  34.9 5.3 %collective-permute-done.5.rest_3_ = bf16[4,2,16,2304]{3,2,1,0:T(8,128)(2,1)S(1)} collective-permute-done((bf16[4,2,16,2304]{3,2,1,0:T(8,128)(2,1)S(1)}, bf16[4,2,16,2304]{3,2,1,0:T(8,128)(2,1)S(1)}, u32[]{:S(2)}, u32[]{:S(2)}) %collective-permute-start.5) | collective-permute-done | bytes 589856 | tf_op jit(solution)/shard_map/ppermute | solution.py:42
  40.2 7.6 %collective-permute-done.4.rest_2_ = bf16[4,2,16,2304]{3,2,1,0:T(8,128)(2,1)S(1)} collective-permute-done((bf16[4,2,16,2304]{3,2,1,0:T(8,128)(2,1)S(1)}, bf16[4,2,16,2304]{3,2,1,0:T(8,128)(2,1)S(1)}, u32[]{:S(2)}, u32[]{:S(2)}) %collective-permute-start.4) | collective-permute-done | bytes 589856 | tf_op jit(solution)/shard_map/ppermute | solution.py:42
  48.3 2.3 %collective-permute-done.8.rest_6_ = bf16[4,2,16,2304]{3,2,1,0:T(8,128)(2,1)} collective-permute-done((bf16[4,2,16,2304]{3,2,1,0:T(8,128)(2,1)S(1)}, bf16[4,2,16,2304]{3,2,1,0:T(8,128)(2,1)}, u32[]{:S(2)}, u32[]{:S(2)}) %collective-permute-start.8) | collective-permute-done | bytes 589856 | tf_op jit(solution)/shard_map/ppermute | solution.py:46
  50.6 8.8 %forward.1 = (bf16[512,4608]{1,0:T(8,128)(2,1)}, f32[512,512]{1,0:T(8,128)}, f32[3,512]{1,0:T(4,128)S(1)}) custom-call(s32[4]{0:T(128)S(1)} %pad_add_fusion.place, s32[1,512]{1,0:T(1,128)S(1)} %bitcast.28, bf16[512,4608]{1,0:T(8,128)(2,1)} %weight.5, bf16[4,2,16,2304]{3,2,1,0:T(8,128)(2,1)S(1)} %pad_maximum_fusion.rest_0_, ...), custom_call_target="tpu_custom_call" | custom-call | flops 2415919104 | bytes 16777216 | tf_op jit(solution)/shard_map/forward/pallas_call | solution.py:164
  59.5 13.8 %all_to_all.21 = f32[16,3,512]{2,1,0:T(4,128)S(1)} all-to-all(f32[16,3,512]{2,1,0:T(4,128)S(1)} %broadcast_in_dim.11), channel_id=1, replica_groups=mesh['x_lo'=2,'y'=4,'core'=2,'x_hi'=2,'z'=8] {'x_lo','y','x_hi'}, dimensions={0} | all-to-all | bytes 196608 | tf_op jit(solution)/shard_map/all_to_all | solution.py:51
  73.4 11.6 %all_to_all.22 = f32[16,3,512]{2,1,0:T(4,128)S(1)} all-to-all(f32[16,3,512]{2,1,0:T(4,128)S(1)} %broadcast_in_dim.12), channel_id=1, replica_groups=mesh['x_lo'=2,'y'=4,'core'=2,'x_hi'=2,'z'=8] {'core','z'}, dimensions={0} | all-to-all | bytes 196608 | tf_op jit(solution)/shard_map/all_to_all | solution.py:51
  85.1 5.0 %far_gradient.1 = (bf16[512,512]{1,0:T(8,128)(2,1)S(1)}, bf16[512,512]{1,0:T(8,128)(2,1)S(1)}, bf16[512,2304]{1,0:T(8,128)(2,1)}) custom-call(s32[4]{0:T(128)S(1)} %pad_add_fusion.place, s32[1,512]{1,0:T(1,128)S(1)} %bitcast.29, f32[512,512]{1,0:T(8,128)} %get-tuple-element.22.capped, f32[3,512]{1,0:T(4,128)S(1)} %reduce_sum.47.totals, bf16[512,4608]{1,0:T(8,128)(2,1)} %weight.5), custom_call_target="tpu_custom_call" | custom-call | flops 1207959552 | bytes 9437184 | tf_op jit(solution)/shard_map/far_gradient/pallas_call | solution.py:236
  90.2 4.7 %collective-permute-done.10.arrived = bf16[512,2304]{1,0:T(8,128)(2,1)S(1)} collective-permute-done((bf16[512,2304]{1,0:T(8,128)(2,1)}, bf16[512,2304]{1,0:T(8,128)(2,1)S(1)}, u32[]{:S(2)}, u32[]{:S(2)}) %collective-permute-start.10) | collective-permute-done | bytes 2359328 | tf_op jit(solution)/shard_map/ppermute | solution.py:46
  95.0 5.2 %near_gradient.1 = (bf16[9,16,2304]{2,1,0:T(8,128)(2,1)S(1)}, bf16[9,16,2304]{2,1,0:T(8,128)(2,1)S(1)}, bf16[9,16,2304]{2,1,0:T(8,128)(2,1)S(1)}, bf16[9,16,2304]{2,1,0:T(8,128)(2,1)S(1)}) custom-call(s32[4]{0:T(128)S(1)} %pad_add_fusion.place, bf16[512,512]{1,0:T(8,128)(2,1)S(1)} %get-tuple-element.24.turned, bf16[512,4608]{1,0:T(8,128)(2,1)} %weight.5, ...), custom_call_target="tpu_custom_call" | custom-call | flops 1207959552 | bytes 12582912 | tf_op jit(solution)/shard_map/near_gradient/pallas_call | solution.py:307
  100.6 2.2 %collective-permute-start.12 = (bf16[9,16,2304]{2,1,0:T(8,128)(2,1)S(1)}, bf16[9,16,2304]{2,1,0:T(8,128)(2,1)S(1)}, u32[]{:S(2)}, u32[]{:S(2)}) collective-permute-start(bf16[9,16,2304]{2,1,0:T(8,128)(2,1)S(1)} %get-tuple-element.31), channel_id=1, source_target_pairs={{0,64},{16,24},{32,96},{48,56},{64,0},{80,88},{96,32},{112,120},{1... | collective-permute-start | bytes 1990664 | tf_op jit(solution)/shard_map/ppermute | solution.py:42
  104.0 15.2 %collective-permute-done.11 = bf16[9,16,2304]{2,1,0:T(8,128)(2,1)S(1)} collective-permute-done((bf16[9,16,2304]{2,1,0:T(8,128)(2,1)S(1)}, bf16[9,16,2304]{2,1,0:T(8,128)(2,1)S(1)}, u32[]{:S(2)}, u32[]{:S(2)}) %collective-permute-start.11) | collective-permute-done | bytes 663584 | tf_op jit(solution)/shard_map/ppermute | solution.py:42
  119.2 5.6 %weight_gradient.1 = bf16[512,4608]{1,0:T(8,128)(2,1)} custom-call(bf16[512,512]{1,0:T(8,128)(2,1)S(1)} %get-tuple-element.28.grad, bf16[512,4608]{1,0:T(8,128)(2,1)} %get-tuple-element.26.gathered), custom_call_target="tpu_custom_call" | custom-call | flops 2415919104 | bytes 10485760 | tf_op jit(solution)/shard_map/weight_gradient/pallas_call | solution.py:351
  126.1 2.2 %collective-permute-start.15 = (bf16[3,16,2304]{2,1,0:T(8,128)(2,1)S(1)}, bf16[3,16,2304]{2,1,0:T(8,128)(2,1)S(1)}, u32[]{:S(2)}, u32[]{:S(2)}) collective-permute-start(bf16[3,16,2304]{2,1,0:T(8,128)(2,1)S(1)} %get-tuple-element.51), channel_id=1, source_target_pairs={{0,8},{16,80},{32,40},{48,112},{64,72},{80,16},{96,104},{112,48},{... | collective-permute-start | bytes 663560 | tf_op jit(solution)/shard_map/ppermute | solution.py:38
  129.3 5.7 %collective-permute-done.14 = bf16[3,16,2304]{2,1,0:T(8,128)(2,1)S(1)} collective-permute-done((bf16[3,16,2304]{2,1,0:T(8,128)(2,1)S(1)}, bf16[3,16,2304]{2,1,0:T(8,128)(2,1)S(1)}, u32[]{:S(2)}, u32[]{:S(2)}) %collective-permute-start.14) | collective-permute-done | bytes 221216 | tf_op jit(solution)/shard_map/ppermute | solution.py:38
  137.3 3.7 %all-to-all-start.3 = ((bf16[16,4,2304]{2,1,0:T(4,128)(2,1)}), bf16[16,4,2304]{2,1,0:T(4,128)(2,1)S(1)}, u32[]{:S(2)}, u32[]{:S(2)}) async-start(bf16[16,4,2304]{2,1,0:T(4,128)(2,1)} %pad_maximum_fusion.5), calls=%async_computation.3 | async-start | bytes 589824 | tf_op jit(solution)/shard_map/all_to_all | solution.py:414
  141.6 11.0 %all-to-all-done.3 = bf16[16,4,2304]{2,1,0:T(4,128)(2,1)S(1)} async-done(((bf16[16,4,2304]{2,1,0:T(4,128)(2,1)}), bf16[16,4,2304]{2,1,0:T(4,128)(2,1)S(1)}, u32[]{:S(2)}, u32[]{:S(2)}) %all-to-all-start.3) | async-done | bytes 294944 | tf_op jit(solution)/shard_map/all_to_all | solution.py:414
  (63 shorter events, 12.4 us)
Async XLA Ops:
  0.6 50.0 %copy-start = (s32[512]{0:T(512)S(1)}, s32[512]{0:T(512)}, u32[]{:S(2)}) copy-start(s32[512]{0:T(512)} %param.7) | copy-start | bytes 6148
  19.5 6.4 %collective-permute-start.2 = (bf16[2,16,2304]{2,1,0:T(8,128)(2,1)S(1)}, bf16[2,16,2304]{2,1,0:T(8,128)(2,1)S(1)}, u32[]{:S(2)}, u32[]{:S(2)}) collective-permute-start(bf16[2,16,2304]{2,1,0:T(8,128)(2,1)S(1)} %reshape.134), channel_id=1, source_target_pairs={{0,128},{16,48},{32,160},{48,80},{64,192},{80,112},{96,224},{112,1... | collective-permute-start | bytes 442376 | tf_op jit(solution)/shard_map/ppermute | solution.py:38
  21.1 7.4 %collective-permute-start.1 = (bf16[2,16,2304]{2,1,0:T(8,128)(2,1)S(1)}, bf16[2,16,2304]{2,1,0:T(8,128)(2,1)S(1)}, u32[]{:S(2)}, u32[]{:S(2)}) collective-permute-start(bf16[2,16,2304]{2,1,0:T(8,128)(2,1)S(1)} %reshape.134), channel_id=1, source_target_pairs={{0,8},{16,80},{32,40},{48,112},{64,72},{80,16},{96,104},{112,48},{... | collective-permute-start | bytes 442376 | tf_op jit(solution)/shard_map/ppermute | solution.py:38
  23.8 5.1 %collective-permute-start = (bf16[2,16,2304]{2,1,0:T(8,128)(2,1)S(1)}, bf16[2,16,2304]{2,1,0:T(8,128)(2,1)S(1)}, u32[]{:S(2)}, u32[]{:S(2)}) collective-permute-start(bf16[2,16,2304]{2,1,0:T(8,128)(2,1)S(1)} %reshape.134), channel_id=1, source_target_pairs={{0,136},{16,112},{32,168},{48,16},{64,200},{80,48},{96,232},{112,8... | collective-permute-start | bytes 442376 | tf_op jit(solution)/shard_map/ppermute | solution.py:38
  29.0 11.2 %collective-permute-start.5 = (bf16[4,2,16,2304]{3,2,1,0:T(8,128)(2,1)S(1)}, bf16[4,2,16,2304]{3,2,1,0:T(8,128)(2,1)S(1)}, u32[]{:S(2)}, u32[]{:S(2)}) collective-permute-start(bf16[4,2,16,2304]{3,2,1,0:T(8,128)(2,1)S(1)} %pad_maximum_fusion.rest_0_), channel_id=1, source_target_pairs={{0,32},{16,144},{32,64},{48,176},{64,96},{80,208},{96,0},{112,240}... | collective-permute-start | bytes 1769480 | tf_op jit(solution)/shard_map/ppermute | solution.py:42
  30.7 17.1 %collective-permute-start.4 = (bf16[4,2,16,2304]{3,2,1,0:T(8,128)(2,1)S(1)}, bf16[4,2,16,2304]{3,2,1,0:T(8,128)(2,1)S(1)}, u32[]{:S(2)}, u32[]{:S(2)}) collective-permute-start(bf16[4,2,16,2304]{3,2,1,0:T(8,128)(2,1)S(1)} %pad_maximum_fusion.rest_0_), channel_id=1, source_target_pairs={{0,64},{16,24},{32,96},{48,56},{64,0},{80,88},{96,32},{112,120},{1... | collective-permute-start | bytes 1769480 | tf_op jit(solution)/shard_map/ppermute | solution.py:42
  33.6 14.2 %collective-permute-start.3 = (bf16[4,2,16,2304]{3,2,1,0:T(8,128)(2,1)S(1)}, bf16[4,2,16,2304]{3,2,1,0:T(8,128)(2,1)S(1)}, u32[]{:S(2)}, u32[]{:S(2)}) collective-permute-start(bf16[4,2,16,2304]{3,2,1,0:T(8,128)(2,1)S(1)} %pad_maximum_fusion.rest_0_), channel_id=1, source_target_pairs={{0,96},{16,152},{32,0},{48,184},{64,32},{80,216},{96,64},{112,248}... | collective-permute-start | bytes 1769480 | tf_op jit(solution)/shard_map/ppermute | solution.py:42
  34.9 13.4 %collective-permute-start.6 = (bf16[4,2,16,2304]{3,2,1,0:T(8,128)(2,1)S(1)}, bf16[4,2,16,2304]{3,2,1,0:T(8,128)(2,1)S(1)}, u32[]{:S(2)}, u32[]{:S(2)}) collective-permute-start(bf16[4,2,16,2304]{3,2,1,0:T(8,128)(2,1)S(1)} %pad_maximum_fusion.rest_0_), channel_id=1, source_target_pairs={{0,16},{16,0},{1,17},{17,1},{2,18},{18,2},{3,19},{19,3},{4,20},{20... | collective-permute-start | bytes 1769480 | tf_op jit(solution)/shard_map/ppermute | solution.py:46
  40.2 8.2 %collective-permute-start.9 = (bf16[4,2,16,2304]{3,2,1,0:T(8,128)(2,1)S(1)}, bf16[4,2,16,2304]{3,2,1,0:T(8,128)(2,1)}, u32[]{:S(2)}, u32[]{:S(2)}) collective-permute-start(bf16[4,2,16,2304]{3,2,1,0:T(8,128)(2,1)S(1)} %collective-permute-done.5.rest_3_), channel_id=1, source_target_pairs={{0,16},{16,0},{1,17},{17,1},{2,18},{18,2},{3,19},{19,3},{4,20},{20... | collective-permute-start | bytes 1769480 | tf_op jit(solution)/shard_map/ppermute | solution.py:46
  47.7 2.9 %collective-permute-start.8 = (bf16[4,2,16,2304]{3,2,1,0:T(8,128)(2,1)S(1)}, bf16[4,2,16,2304]{3,2,1,0:T(8,128)(2,1)}, u32[]{:S(2)}, u32[]{:S(2)}) collective-permute-start(bf16[4,2,16,2304]{3,2,1,0:T(8,128)(2,1)S(1)} %collective-permute-done.4.rest_2_), channel_id=1, source_target_pairs={{0,16},{16,0},{1,17},{17,1},{2,18},{18,2},{3,19},{19,3},{4,20},{20... | collective-permute-start | bytes 1769480 | tf_op jit(solution)/shard_map/ppermute | solution.py:46
  47.7 2.9 %collective-permute-start.7 = (bf16[4,2,16,2304]{3,2,1,0:T(8,128)(2,1)S(1)}, bf16[4,2,16,2304]{3,2,1,0:T(8,128)(2,1)S(1)}, u32[]{:S(2)}, u32[]{:S(2)}) collective-permute-start(bf16[4,2,16,2304]{3,2,1,0:T(8,128)(2,1)S(1)} %collective-permute-done.3.rest_1_), channel_id=1, source_target_pairs={{0,16},{16,0},{1,17},{17,1},{2,18},{18,2},{3,19},{19,3},{4,20},{20... | collective-permute-start | bytes 1769480 | tf_op jit(solution)/shard_map/ppermute | solution.py:46
  90.1 4.8 %collective-permute-start.10 = (bf16[512,2304]{1,0:T(8,128)(2,1)}, bf16[512,2304]{1,0:T(8,128)(2,1)S(1)}, u32[]{:S(2)}, u32[]{:S(2)}) collective-permute-start(bf16[512,2304]{1,0:T(8,128)(2,1)} %get-tuple-element.25), channel_id=1, source_target_pairs={{0,16},{16,0},{1,17},{17,1},{2,18},{18,2},{3,19},{19,3},{4,20},{20... | collective-permute-start | bytes 7077896 | tf_op jit(solution)/shard_map/ppermute | solution.py:46
  100.1 19.1 %collective-permute-start.11 = (bf16[9,16,2304]{2,1,0:T(8,128)(2,1)S(1)}, bf16[9,16,2304]{2,1,0:T(8,128)(2,1)S(1)}, u32[]{:S(2)}, u32[]{:S(2)}) collective-permute-start(bf16[9,16,2304]{2,1,0:T(8,128)(2,1)S(1)} %get-tuple-element.27), channel_id=1, source_target_pairs={{0,32},{16,144},{32,64},{48,176},{64,96},{80,208},{96,0},{112,240}... | collective-permute-start | bytes 1990664 | tf_op jit(solution)/shard_map/ppermute | solution.py:42
  100.6 24.2 %collective-permute-start.12 = (bf16[9,16,2304]{2,1,0:T(8,128)(2,1)S(1)}, bf16[9,16,2304]{2,1,0:T(8,128)(2,1)S(1)}, u32[]{:S(2)}, u32[]{:S(2)}) collective-permute-start(bf16[9,16,2304]{2,1,0:T(8,128)(2,1)S(1)} %get-tuple-element.31), channel_id=1, source_target_pairs={{0,64},{16,24},{32,96},{48,56},{64,0},{80,88},{96,32},{112,120},{1... | collective-permute-start | bytes 1990664 | tf_op jit(solution)/shard_map/ppermute | solution.py:42
  102.9 22.0 %collective-permute-start.13 = (bf16[9,16,2304]{2,1,0:T(8,128)(2,1)S(1)}, bf16[9,16,2304]{2,1,0:T(8,128)(2,1)S(1)}, u32[]{:S(2)}, u32[]{:S(2)}) collective-permute-start(bf16[9,16,2304]{2,1,0:T(8,128)(2,1)S(1)} %get-tuple-element.32), channel_id=1, source_target_pairs={{0,96},{16,152},{32,0},{48,184},{64,32},{80,216},{96,64},{112,248}... | collective-permute-start | bytes 1990664 | tf_op jit(solution)/shard_map/ppermute | solution.py:42
  125.4 9.6 %collective-permute-start.14 = (bf16[3,16,2304]{2,1,0:T(8,128)(2,1)S(1)}, bf16[3,16,2304]{2,1,0:T(8,128)(2,1)S(1)}, u32[]{:S(2)}, u32[]{:S(2)}) collective-permute-start(bf16[3,16,2304]{2,1,0:T(8,128)(2,1)S(1)} %get-tuple-element.50), channel_id=1, source_target_pairs={{0,128},{16,48},{32,160},{48,80},{64,192},{80,112},{96,224},{112,1... | collective-permute-start | bytes 663560 | tf_op jit(solution)/shard_map/ppermute | solution.py:38
  126.1 8.9 %collective-permute-start.15 = (bf16[3,16,2304]{2,1,0:T(8,128)(2,1)S(1)}, bf16[3,16,2304]{2,1,0:T(8,128)(2,1)S(1)}, u32[]{:S(2)}, u32[]{:S(2)}) collective-permute-start(bf16[3,16,2304]{2,1,0:T(8,128)(2,1)S(1)} %get-tuple-element.51), channel_id=1, source_target_pairs={{0,8},{16,80},{32,40},{48,112},{64,72},{80,16},{96,104},{112,48},{... | collective-permute-start | bytes 663560 | tf_op jit(solution)/shard_map/ppermute | solution.py:38
  128.3 7.6 %collective-permute-start.16 = (bf16[3,16,2304]{2,1,0:T(8,128)(2,1)S(1)}, bf16[3,16,2304]{2,1,0:T(8,128)(2,1)S(1)}, u32[]{:S(2)}, u32[]{:S(2)}) collective-permute-start(bf16[3,16,2304]{2,1,0:T(8,128)(2,1)S(1)} %get-tuple-element.52), channel_id=1, source_target_pairs={{0,136},{16,112},{32,168},{48,16},{64,200},{80,48},{96,232},{112,8... | collective-permute-start | bytes 663560 | tf_op jit(solution)/shard_map/ppermute | solution.py:38
  136.0 16.9 %copy-start.1 = (f32[4608]{0:T(1024)S(1)}, f32[4608]{0:T(1024)}, u32[]{:S(2)}) copy-start(f32[4608]{0:T(1024)} %param.5) | copy-start | bytes 55300
  136.1 16.9 %copy-start.2 = (bf16[2,4608]{1,0:T(2,128)(2,1)S(1)}, bf16[2,4608]{1,0:T(2,128)(2,1)}, u32[]{:S(2)}) copy-start(bf16[2,4608]{1,0:T(2,128)(2,1)} %param.4) | copy-start | bytes 55300
  137.3 15.3 %all-to-all-start.3 = ((bf16[16,4,2304]{2,1,0:T(4,128)(2,1)}), bf16[16,4,2304]{2,1,0:T(4,128)(2,1)S(1)}, u32[]{:S(2)}, u32[]{:S(2)}) async-start(bf16[16,4,2304]{2,1,0:T(4,128)(2,1)} %pad_maximum_fusion.5), calls=%async_computation.3 | async-start | bytes 589824 | tf_op jit(solution)/shard_map/all_to_all | solution.py:414

commit v5 on v4

--- a/solution.py
+++ b/solution.py
@@ -78,8 +78,8 @@
     return pl.ds(pl.multiple_of(step * STEP, STEP), STEP)
 
 
-def steps(body, first=0, last=STEPS):
-    lax.fori_loop(first, last, lambda j, carry: (body(j), carry)[1], 0)
+def steps(body, first=0, last=STEPS, unroll=False):
+    lax.fori_loop(first, last, lambda j, carry: (body(j), carry)[1], 0, unroll=unroll)
 
 
 def forward_kernel(place, targets, weight, *rest):
@@ -129,11 +129,11 @@
     place_blocks(1 - core, blocks[4:])
     logits[...] = jnp.zeros_like(logits)
     pltpu.make_async_copy(half_rows(0), half_rows(0), row_sems.at[0]).wait()
-    steps(multiply, 0, HALF_STEPS)
+    steps(multiply, 0, HALF_STEPS, True)
     pltpu.make_async_copy(half_rows(1), half_rows(1), row_sems.at[1]).wait()
     out_copy = pltpu.make_async_copy(rows_held, gathered, out_sem)
     out_copy.start()
-    steps(multiply, HALF_STEPS, STEPS)
+    steps(multiply, HALF_STEPS, STEPS, True)
 
     def finish(k, carry):
         rows = pl.ds(pl.multiple_of(k * 64, 64), 64)
@@ -228,7 +228,7 @@
         ).astype(jnp.bfloat16)
         leaving(j).start()
 
-    steps(multiply, 0, HALF_STEPS)
+    steps(multiply, 0, HALF_STEPS, True)
     steps(lambda j: leaving(j).wait(), 0, HALF_STEPS)
 
 
@@ -295,7 +295,7 @@
                     held[outer, inner * 2 + owner, :, columns] = rounded[row : row + PIECE]
 
     steps(begin, 0, HALF_STEPS)
-    steps(multiply, 0, HALF_STEPS)
+    steps(multiply, 0, HALF_STEPS, True)
     leaving = [pltpu.make_async_copy(held.at[k], sends[k], out_sems.at[k]) for k in range(4)]
     for copy in leaving:
         copy.start()
@@ -397,8 +397,9 @@
         high = lax.reduce_precision(gain, 8, 7)
         return jnp.concatenate([high, gain - high], axis=0).astype(jnp.bfloat16)
 
-    parts = send_ring(sends, shift_second)
-    grad, parts[1] = lax.optimization_barrier((grad, parts[1]))
+    own, *others = sends
+    grad, own = lax.optimization_barrier((grad, own))
+    parts = send_ring([own, *others], shift_second)
     grad_weight = weight_gradient(grad, gathered)
     grad_weight, *parts = lax.optimization_barrier((grad_weight, *parts))
     half_sum = total(parts)

time: 155 us -> 150 us (0.968)
  waiting for transfers between devices: 56.4 us -> 51.6 us
    ppermute x6, waiting for transfers between devices: 28 us -> 23.3 us  [shift_second(): return lax.ppermute(block, CROSS, cross_pairs(step, 1))]
  transfers between devices with their start and end apart: 18 -> 18, of which waited for: 11 -> 12; matrix products, arithmetic and copies ran while one was open for 0% -> 0% of each run, Pallas kernels for 4% -> 4%
where the time goes in v5:
time: 150 us
  waiting for transfers between devices  51.6 us (34%)
  blocking collectives  42.4 us (28%)
  Pallas kernels  24.5 us (16%)
  starting transfers between devices  23.9 us (16%)
  other arithmetic  6 us (4%)
    all_to_all x2, blocking collectives, gather_over(): return lax.all_to_all(copies, axes, 0, 0, tiled=True)  25.5 us
    ppermute x6, waiting for transfers between devices, shift_second(): return lax.ppermute(block, CROSS, cross_pairs(step, 1))  23.3 us
    all_to_all x1, blocking collectives, on_device(): lax.all_to_all(halves, ('core', 'z'), 0, 0, tiled=True)  16.9 us
    all_to_all x1, waiting for transfers between devices, on_device(): line_parts = lax.all_to_all(message, ('core', 'z'), 0, 0, tiled=True)  11 us
    ppermute x6, waiting for transfers between devices, shift_first(): return lax.ppermute(block, CROSS, cross_pairs(step, 0))  10.3 us
    ppermute x6, starting transfers between devices, shift_second(): return lax.ppermute(block, CROSS, cross_pairs(step, 1))  9.78 us
    ppermute x6, starting transfers between devices, shift_first(): return lax.ppermute(block, CROSS, cross_pairs(step, 0))  9.62 us
    pallas_call x1, Pallas kernels, forward(): pl.pallas_call(forward_kernel, out_shape=(jax.ShapeDtypeStruct((TOKENS, W...  8.24 us
  transfers between devices with their start and end apart: 18, of which 12 were waited for; matrix products, arithmetic and copies ran while one was open for 0% of the time, Pallas kernels for 4%

profile of v5, /device:TPU:32, one launch (start us, length us, event | category | flops | bytes accessed | tf_op | source)
XLA Modules:
  0.0 149.8 jit_solution(13882005812002521601)
XLA Ops:
  2.5 16.9 %all_to_all.20 = bf16[16,2,2304]{2,1,0:T(2,128)(2,1)S(1)} all-to-all(bf16[16,2,2304]{2,1,0:T(2,128)(2,1)S(1)} %bitcast.30), channel_id=1, replica_groups=mesh['x_lo'=2,'y'=4,'core'=2,'x_hi'=2,'z'=8] {'core','z'}, dimensions={0} | all-to-all | bytes 294912 | tf_op jit(solution)/shard_map/all_to_all | solution.py:383
  19.5 1.6 %collective-permute-start.2 = (bf16[2,16,2304]{2,1,0:T(8,128)(2,1)S(1)}, bf16[2,16,2304]{2,1,0:T(8,128)(2,1)S(1)}, u32[]{:S(2)}, u32[]{:S(2)}) collective-permute-start(bf16[2,16,2304]{2,1,0:T(8,128)(2,1)S(1)} %reshape.134), channel_id=1, source_target_pairs={{0,128},{16,48},{32,160},{48,80},{64,192},{80,112},{96,224},{112,1... | collective-permute-start | bytes 442376 | tf_op jit(solution)/shard_map/ppermute | solution.py:38
  21.1 2.7 %collective-permute-start.1 = (bf16[2,16,2304]{2,1,0:T(8,128)(2,1)S(1)}, bf16[2,16,2304]{2,1,0:T(8,128)(2,1)S(1)}, u32[]{:S(2)}, u32[]{:S(2)}) collective-permute-start(bf16[2,16,2304]{2,1,0:T(8,128)(2,1)S(1)} %reshape.134), channel_id=1, source_target_pairs={{0,8},{16,80},{32,40},{48,112},{64,72},{80,16},{96,104},{112,48},{... | collective-permute-start | bytes 442376 | tf_op jit(solution)/shard_map/ppermute | solution.py:38
  23.8 1.4 collective-permute-start
  25.9 2.6 %collective-permute-done.1 = bf16[2,16,2304]{2,1,0:T(8,128)(2,1)S(1)} collective-permute-done((bf16[2,16,2304]{2,1,0:T(8,128)(2,1)S(1)}, bf16[2,16,2304]{2,1,0:T(8,128)(2,1)S(1)}, u32[]{:S(2)}, u32[]{:S(2)}) %collective-permute-start.1) | collective-permute-done | bytes 147488 | tf_op jit(solution)/shard_map/ppermute | solution.py:38
  29.0 1.7 %collective-permute-start.5 = (bf16[4,2,16,2304]{3,2,1,0:T(8,128)(2,1)S(1)}, bf16[4,2,16,2304]{3,2,1,0:T(8,128)(2,1)S(1)}, u32[]{:S(2)}, u32[]{:S(2)}) collective-permute-start(bf16[4,2,16,2304]{3,2,1,0:T(8,128)(2,1)S(1)} %pad_maximum_fusion.rest_0_), channel_id=1, source_target_pairs={{0,32},{16,144},{32,64},{48,176},{64,96},{80,208},{96,0},{112,240}... | collective-permute-start | bytes 1769480 | tf_op jit(solution)/shard_map/ppermute | solution.py:42
  30.7 2.9 %collective-permute-start.4 = (bf16[4,2,16,2304]{3,2,1,0:T(8,128)(2,1)S(1)}, bf16[4,2,16,2304]{3,2,1,0:T(8,128)(2,1)S(1)}, u32[]{:S(2)}, u32[]{:S(2)}) collective-permute-start(bf16[4,2,16,2304]{3,2,1,0:T(8,128)(2,1)S(1)} %pad_maximum_fusion.rest_0_), channel_id=1, source_target_pairs={{0,64},{16,24},{32,96},{48,56},{64,0},{80,88},{96,32},{112,120},{1... | collective-permute-start | bytes 1769480 | tf_op jit(solution)/shard_map/ppermute | solution.py:42
  33.6 1.3 collective-permute-start.3
  34.9 5.3 %collective-permute-done.5.rest_3_ = bf16[4,2,16,2304]{3,2,1,0:T(8,128)(2,1)S(1)} collective-permute-done((bf16[4,2,16,2304]{3,2,1,0:T(8,128)(2,1)S(1)}, bf16[4,2,16,2304]{3,2,1,0:T(8,128)(2,1)S(1)}, u32[]{:S(2)}, u32[]{:S(2)}) %collective-permute-start.5) | collective-permute-done | bytes 589856 | tf_op jit(solution)/shard_map/ppermute | solution.py:42
  40.2 7.6 %collective-permute-done.4.rest_2_ = bf16[4,2,16,2304]{3,2,1,0:T(8,128)(2,1)S(1)} collective-permute-done((bf16[4,2,16,2304]{3,2,1,0:T(8,128)(2,1)S(1)}, bf16[4,2,16,2304]{3,2,1,0:T(8,128)(2,1)S(1)}, u32[]{:S(2)}, u32[]{:S(2)}) %collective-permute-start.4) | collective-permute-done | bytes 589856 | tf_op jit(solution)/shard_map/ppermute | solution.py:42
  48.3 2.3 %collective-permute-done.8.rest_6_ = bf16[4,2,16,2304]{3,2,1,0:T(8,128)(2,1)} collective-permute-done((bf16[4,2,16,2304]{3,2,1,0:T(8,128)(2,1)S(1)}, bf16[4,2,16,2304]{3,2,1,0:T(8,128)(2,1)}, u32[]{:S(2)}, u32[]{:S(2)}) %collective-permute-start.8) | collective-permute-done | bytes 589856 | tf_op jit(solution)/shard_map/ppermute | solution.py:46
  50.6 8.2 %forward.1 = (bf16[512,4608]{1,0:T(8,128)(2,1)}, f32[512,512]{1,0:T(8,128)}, f32[3,512]{1,0:T(4,128)S(1)}) custom-call(s32[4]{0:T(128)S(1)} %pad_add_fusion.place, s32[1,512]{1,0:T(1,128)S(1)} %bitcast.28, bf16[512,4608]{1,0:T(8,128)(2,1)} %weight.5, bf16[4,2,16,2304]{3,2,1,0:T(8,128)(2,1)S(1)} %pad_maximum_fusion.rest_0_, ...), custom_call_target="tpu_custom_call" | custom-call | flops 2415919104 | bytes 16777216 | tf_op jit(solution)/shard_map/forward/pallas_call | solution.py:164
  58.9 13.8 %all_to_all.21 = f32[16,3,512]{2,1,0:T(4,128)S(1)} all-to-all(f32[16,3,512]{2,1,0:T(4,128)S(1)} %broadcast_in_dim.11), channel_id=1, replica_groups=mesh['x_lo'=2,'y'=4,'core'=2,'x_hi'=2,'z'=8] {'x_lo','y','x_hi'}, dimensions={0} | all-to-all | bytes 196608 | tf_op jit(solution)/shard_map/all_to_all | solution.py:51
  72.8 11.6 %all_to_all.22 = f32[16,3,512]{2,1,0:T(4,128)S(1)} all-to-all(f32[16,3,512]{2,1,0:T(4,128)S(1)} %broadcast_in_dim.12), channel_id=1, replica_groups=mesh['x_lo'=2,'y'=4,'core'=2,'x_hi'=2,'z'=8] {'core','z'}, dimensions={0} | all-to-all | bytes 196608 | tf_op jit(solution)/shard_map/all_to_all | solution.py:51
  84.5 5.3 %far_gradient.1 = (bf16[512,512]{1,0:T(8,128)(2,1)S(1)}, bf16[512,512]{1,0:T(8,128)(2,1)S(1)}, bf16[512,2304]{1,0:T(8,128)(2,1)}) custom-call(s32[4]{0:T(128)S(1)} %pad_add_fusion.place, s32[1,512]{1,0:T(1,128)S(1)} %bitcast.29, f32[512,512]{1,0:T(8,128)} %get-tuple-element.22.capped, f32[3,512]{1,0:T(4,128)S(1)} %reduce_sum.47.totals, bf16[512,4608]{1,0:T(8,128)(2,1)} %weight.5), custom_call_target="tpu_custom_call" | custom-call | flops 1207959552 | bytes 9437184 | tf_op jit(solution)/shard_map/far_gradient/pallas_call | solution.py:236
  90.1 4.7 %collective-permute-done.10.arrived = bf16[512,2304]{1,0:T(8,128)(2,1)S(1)} collective-permute-done((bf16[512,2304]{1,0:T(8,128)(2,1)}, bf16[512,2304]{1,0:T(8,128)(2,1)S(1)}, u32[]{:S(2)}, u32[]{:S(2)}) %collective-permute-start.10) | collective-permute-done | bytes 2359328 | tf_op jit(solution)/shard_map/ppermute | solution.py:46
  94.8 5.4 %near_gradient.1 = (bf16[9,16,2304]{2,1,0:T(8,128)(2,1)S(1)}, bf16[9,16,2304]{2,1,0:T(8,128)(2,1)S(1)}, bf16[9,16,2304]{2,1,0:T(8,128)(2,1)S(1)}, bf16[9,16,2304]{2,1,0:T(8,128)(2,1)S(1)}) custom-call(s32[4]{0:T(128)S(1)} %pad_add_fusion.place, bf16[512,512]{1,0:T(8,128)(2,1)S(1)} %get-tuple-element.24.turned, bf16[512,4608]{1,0:T(8,128)(2,1)} %weight.5, ...), custom_call_target="tpu_custom_call" | custom-call | flops 1207959552 | bytes 12582912 | tf_op jit(solution)/shard_map/near_gradient/pallas_call | solution.py:307
  100.6 2.2 %collective-permute-start.12 = (bf16[9,16,2304]{2,1,0:T(8,128)(2,1)S(1)}, bf16[9,16,2304]{2,1,0:T(8,128)(2,1)S(1)}, u32[]{:S(2)}, u32[]{:S(2)}) collective-permute-start(bf16[9,16,2304]{2,1,0:T(8,128)(2,1)S(1)} %get-tuple-element.31), channel_id=1, source_target_pairs={{0,64},{16,24},{32,96},{48,56},{64,0},{80,88},{96,32},{112,120},{1... | collective-permute-start | bytes 1990664 | tf_op jit(solution)/shard_map/ppermute | solution.py:42
  104.0 5.6 %weight_gradient.1 = bf16[512,4608]{1,0:T(8,128)(2,1)} custom-call(bf16[512,512]{1,0:T(8,128)(2,1)S(1)} %get-tuple-element.28.grad, bf16[512,4608]{1,0:T(8,128)(2,1)} %get-tuple-element.26.gathered), custom_call_target="tpu_custom_call" | custom-call | flops 2415919104 | bytes 10485760 | tf_op jit(solution)/shard_map/weight_gradient/pallas_call | solution.py:351
  109.7 9.6 %collective-permute-done.11 = bf16[9,16,2304]{2,1,0:T(8,128)(2,1)S(1)} collective-permute-done((bf16[9,16,2304]{2,1,0:T(8,128)(2,1)S(1)}, bf16[9,16,2304]{2,1,0:T(8,128)(2,1)S(1)}, u32[]{:S(2)}, u32[]{:S(2)}) %collective-permute-start.11) | collective-permute-done | bytes 663584 | tf_op jit(solution)/shard_map/ppermute | solution.py:42
  121.3 2.2 %collective-permute-start.15 = (bf16[3,16,2304]{2,1,0:T(8,128)(2,1)S(1)}, bf16[3,16,2304]{2,1,0:T(8,128)(2,1)S(1)}, u32[]{:S(2)}, u32[]{:S(2)}) collective-permute-start(bf16[3,16,2304]{2,1,0:T(8,128)(2,1)S(1)} %get-tuple-element.51), channel_id=1, source_target_pairs={{0,8},{16,80},{32,40},{48,112},{64,72},{80,16},{96,104},{112,48},{... | collective-permute-start | bytes 663560 | tf_op jit(solution)/shard_map/ppermute | solution.py:38
  124.6 5.7 %collective-permute-done.14 = bf16[3,16,2304]{2,1,0:T(8,128)(2,1)S(1)} collective-permute-done((bf16[3,16,2304]{2,1,0:T(8,128)(2,1)S(1)}, bf16[3,16,2304]{2,1,0:T(8,128)(2,1)S(1)}, u32[]{:S(2)}, u32[]{:S(2)}) %collective-permute-start.14) | collective-permute-done | bytes 221216 | tf_op jit(solution)/shard_map/ppermute | solution.py:38
  132.6 3.7 %all-to-all-start.3 = ((bf16[16,4,2304]{2,1,0:T(4,128)(2,1)}), bf16[16,4,2304]{2,1,0:T(4,128)(2,1)S(1)}, u32[]{:S(2)}, u32[]{:S(2)}) async-start(bf16[16,4,2304]{2,1,0:T(4,128)(2,1)} %pad_maximum_fusion.5), calls=%async_computation.3 | async-start | bytes 589824 | tf_op jit(solution)/shard_map/all_to_all | solution.py:415
  136.9 11.0 %all-to-all-done.3 = bf16[16,4,2304]{2,1,0:T(4,128)(2,1)S(1)} async-done(((bf16[16,4,2304]{2,1,0:T(4,128)(2,1)}), bf16[16,4,2304]{2,1,0:T(4,128)(2,1)S(1)}, u32[]{:S(2)}, u32[]{:S(2)}) %all-to-all-start.3) | async-done | bytes 294944 | tf_op jit(solution)/shard_map/all_to_all | solution.py:415
  (63 shorter events, 13.5 us)
Async XLA Ops:
  0.6 50.0 %copy-start = (s32[512]{0:T(512)S(1)}, s32[512]{0:T(512)}, u32[]{:S(2)}) copy-start(s32[512]{0:T(512)} %param.7) | copy-start | bytes 6148
  19.5 6.4 %collective-permute-start.2 = (bf16[2,16,2304]{2,1,0:T(8,128)(2,1)S(1)}, bf16[2,16,2304]{2,1,0:T(8,128)(2,1)S(1)}, u32[]{:S(2)}, u32[]{:S(2)}) collective-permute-start(bf16[2,16,2304]{2,1,0:T(8,128)(2,1)S(1)} %reshape.134), channel_id=1, source_target_pairs={{0,128},{16,48},{32,160},{48,80},{64,192},{80,112},{96,224},{112,1... | collective-permute-start | bytes 442376 | tf_op jit(solution)/shard_map/ppermute | solution.py:38
  21.1 7.4 %collective-permute-start.1 = (bf16[2,16,2304]{2,1,0:T(8,128)(2,1)S(1)}, bf16[2,16,2304]{2,1,0:T(8,128)(2,1)S(1)}, u32[]{:S(2)}, u32[]{:S(2)}) collective-permute-start(bf16[2,16,2304]{2,1,0:T(8,128)(2,1)S(1)} %reshape.134), channel_id=1, source_target_pairs={{0,8},{16,80},{32,40},{48,112},{64,72},{80,16},{96,104},{112,48},{... | collective-permute-start | bytes 442376 | tf_op jit(solution)/shard_map/ppermute | solution.py:38
  23.8 5.1 %collective-permute-start = (bf16[2,16,2304]{2,1,0:T(8,128)(2,1)S(1)}, bf16[2,16,2304]{2,1,0:T(8,128)(2,1)S(1)}, u32[]{:S(2)}, u32[]{:S(2)}) collective-permute-start(bf16[2,16,2304]{2,1,0:T(8,128)(2,1)S(1)} %reshape.134), channel_id=1, source_target_pairs={{0,136},{16,112},{32,168},{48,16},{64,200},{80,48},{96,232},{112,8... | collective-permute-start | bytes 442376 | tf_op jit(solution)/shard_map/ppermute | solution.py:38
  29.0 11.2 %collective-permute-start.5 = (bf16[4,2,16,2304]{3,2,1,0:T(8,128)(2,1)S(1)}, bf16[4,2,16,2304]{3,2,1,0:T(8,128)(2,1)S(1)}, u32[]{:S(2)}, u32[]{:S(2)}) collective-permute-start(bf16[4,2,16,2304]{3,2,1,0:T(8,128)(2,1)S(1)} %pad_maximum_fusion.rest_0_), channel_id=1, source_target_pairs={{0,32},{16,144},{32,64},{48,176},{64,96},{80,208},{96,0},{112,240}... | collective-permute-start | bytes 1769480 | tf_op jit(solution)/shard_map/ppermute | solution.py:42
  30.7 17.1 %collective-permute-start.4 = (bf16[4,2,16,2304]{3,2,1,0:T(8,128)(2,1)S(1)}, bf16[4,2,16,2304]{3,2,1,0:T(8,128)(2,1)S(1)}, u32[]{:S(2)}, u32[]{:S(2)}) collective-permute-start(bf16[4,2,16,2304]{3,2,1,0:T(8,128)(2,1)S(1)} %pad_maximum_fusion.rest_0_), channel_id=1, source_target_pairs={{0,64},{16,24},{32,96},{48,56},{64,0},{80,88},{96,32},{112,120},{1... | collective-permute-start | bytes 1769480 | tf_op jit(solution)/shard_map/ppermute | solution.py:42
  33.6 14.2 %collective-permute-start.3 = (bf16[4,2,16,2304]{3,2,1,0:T(8,128)(2,1)S(1)}, bf16[4,2,16,2304]{3,2,1,0:T(8,128)(2,1)S(1)}, u32[]{:S(2)}, u32[]{:S(2)}) collective-permute-start(bf16[4,2,16,2304]{3,2,1,0:T(8,128)(2,1)S(1)} %pad_maximum_fusion.rest_0_), channel_id=1, source_target_pairs={{0,96},{16,152},{32,0},{48,184},{64,32},{80,216},{96,64},{112,248}... | collective-permute-start | bytes 1769480 | tf_op jit(solution)/shard_map/ppermute | solution.py:42
  34.9 13.4 %collective-permute-start.6 = (bf16[4,2,16,2304]{3,2,1,0:T(8,128)(2,1)S(1)}, bf16[4,2,16,2304]{3,2,1,0:T(8,128)(2,1)S(1)}, u32[]{:S(2)}, u32[]{:S(2)}) collective-permute-start(bf16[4,2,16,2304]{3,2,1,0:T(8,128)(2,1)S(1)} %pad_maximum_fusion.rest_0_), channel_id=1, source_target_pairs={{0,16},{16,0},{1,17},{17,1},{2,18},{18,2},{3,19},{19,3},{4,20},{20... | collective-permute-start | bytes 1769480 | tf_op jit(solution)/shard_map/ppermute | solution.py:46
  40.2 8.2 %collective-permute-start.9 = (bf16[4,2,16,2304]{3,2,1,0:T(8,128)(2,1)S(1)}, bf16[4,2,16,2304]{3,2,1,0:T(8,128)(2,1)}, u32[]{:S(2)}, u32[]{:S(2)}) collective-permute-start(bf16[4,2,16,2304]{3,2,1,0:T(8,128)(2,1)S(1)} %collective-permute-done.5.rest_3_), channel_id=1, source_target_pairs={{0,16},{16,0},{1,17},{17,1},{2,18},{18,2},{3,19},{19,3},{4,20},{20... | collective-permute-start | bytes 1769480 | tf_op jit(solution)/shard_map/ppermute | solution.py:46
  47.7 2.9 %collective-permute-start.8 = (bf16[4,2,16,2304]{3,2,1,0:T(8,128)(2,1)S(1)}, bf16[4,2,16,2304]{3,2,1,0:T(8,128)(2,1)}, u32[]{:S(2)}, u32[]{:S(2)}) collective-permute-start(bf16[4,2,16,2304]{3,2,1,0:T(8,128)(2,1)S(1)} %collective-permute-done.4.rest_2_), channel_id=1, source_target_pairs={{0,16},{16,0},{1,17},{17,1},{2,18},{18,2},{3,19},{19,3},{4,20},{20... | collective-permute-start | bytes 1769480 | tf_op jit(solution)/shard_map/ppermute | solution.py:46
  47.7 2.9 %collective-permute-start.7 = (bf16[4,2,16,2304]{3,2,1,0:T(8,128)(2,1)S(1)}, bf16[4,2,16,2304]{3,2,1,0:T(8,128)(2,1)S(1)}, u32[]{:S(2)}, u32[]{:S(2)}) collective-permute-start(bf16[4,2,16,2304]{3,2,1,0:T(8,128)(2,1)S(1)} %collective-permute-done.3.rest_1_), channel_id=1, source_target_pairs={{0,16},{16,0},{1,17},{17,1},{2,18},{18,2},{3,19},{19,3},{4,20},{20... | collective-permute-start | bytes 1769480 | tf_op jit(solution)/shard_map/ppermute | solution.py:46
  89.8 5.0 %collective-permute-start.10 = (bf16[512,2304]{1,0:T(8,128)(2,1)}, bf16[512,2304]{1,0:T(8,128)(2,1)S(1)}, u32[]{:S(2)}, u32[]{:S(2)}) collective-permute-start(bf16[512,2304]{1,0:T(8,128)(2,1)} %get-tuple-element.25), channel_id=1, source_target_pairs={{0,16},{16,0},{1,17},{17,1},{2,18},{18,2},{3,19},{19,3},{4,20},{20... | collective-permute-start | bytes 7077896 | tf_op jit(solution)/shard_map/ppermute | solution.py:46
  100.2 19.1 %collective-permute-start.11 = (bf16[9,16,2304]{2,1,0:T(8,128)(2,1)S(1)}, bf16[9,16,2304]{2,1,0:T(8,128)(2,1)S(1)}, u32[]{:S(2)}, u32[]{:S(2)}) collective-permute-start(bf16[9,16,2304]{2,1,0:T(8,128)(2,1)S(1)} %get-tuple-element.30), channel_id=1, source_target_pairs={{0,32},{16,144},{32,64},{48,176},{64,96},{80,208},{96,0},{112,240}... | collective-permute-start | bytes 1990664 | tf_op jit(solution)/shard_map/ppermute | solution.py:42
  100.6 18.6 %collective-permute-start.12 = (bf16[9,16,2304]{2,1,0:T(8,128)(2,1)S(1)}, bf16[9,16,2304]{2,1,0:T(8,128)(2,1)S(1)}, u32[]{:S(2)}, u32[]{:S(2)}) collective-permute-start(bf16[9,16,2304]{2,1,0:T(8,128)(2,1)S(1)} %get-tuple-element.31), channel_id=1, source_target_pairs={{0,64},{16,24},{32,96},{48,56},{64,0},{80,88},{96,32},{112,120},{1... | collective-permute-start | bytes 1990664 | tf_op jit(solution)/shard_map/ppermute | solution.py:42
  102.9 17.3 %collective-permute-start.13 = (bf16[9,16,2304]{2,1,0:T(8,128)(2,1)S(1)}, bf16[9,16,2304]{2,1,0:T(8,128)(2,1)S(1)}, u32[]{:S(2)}, u32[]{:S(2)}) collective-permute-start(bf16[9,16,2304]{2,1,0:T(8,128)(2,1)S(1)} %get-tuple-element.32), channel_id=1, source_target_pairs={{0,96},{16,152},{32,0},{48,184},{64,32},{80,216},{96,64},{112,248}... | collective-permute-start | bytes 1990664 | tf_op jit(solution)/shard_map/ppermute | solution.py:42
  120.7 9.6 %collective-permute-start.14 = (bf16[3,16,2304]{2,1,0:T(8,128)(2,1)S(1)}, bf16[3,16,2304]{2,1,0:T(8,128)(2,1)S(1)}, u32[]{:S(2)}, u32[]{:S(2)}) collective-permute-start(bf16[3,16,2304]{2,1,0:T(8,128)(2,1)S(1)} %get-tuple-element.50), channel_id=1, source_target_pairs={{0,128},{16,48},{32,160},{48,80},{64,192},{80,112},{96,224},{112,1... | collective-permute-start | bytes 663560 | tf_op jit(solution)/shard_map/ppermute | solution.py:38
  121.3 8.9 %collective-permute-start.15 = (bf16[3,16,2304]{2,1,0:T(8,128)(2,1)S(1)}, bf16[3,16,2304]{2,1,0:T(8,128)(2,1)S(1)}, u32[]{:S(2)}, u32[]{:S(2)}) collective-permute-start(bf16[3,16,2304]{2,1,0:T(8,128)(2,1)S(1)} %get-tuple-element.51), channel_id=1, source_target_pairs={{0,8},{16,80},{32,40},{48,112},{64,72},{80,16},{96,104},{112,48},{... | collective-permute-start | bytes 663560 | tf_op jit(solution)/shard_map/ppermute | solution.py:38
  123.6 7.6 %collective-permute-start.16 = (bf16[3,16,2304]{2,1,0:T(8,128)(2,1)S(1)}, bf16[3,16,2304]{2,1,0:T(8,128)(2,1)S(1)}, u32[]{:S(2)}, u32[]{:S(2)}) collective-permute-start(bf16[3,16,2304]{2,1,0:T(8,128)(2,1)S(1)} %get-tuple-element.52), channel_id=1, source_target_pairs={{0,136},{16,112},{32,168},{48,16},{64,200},{80,48},{96,232},{112,8... | collective-permute-start | bytes 663560 | tf_op jit(solution)/shard_map/ppermute | solution.py:38
  131.3 16.9 %copy-start.1 = (f32[4608]{0:T(1024)S(1)}, f32[4608]{0:T(1024)}, u32[]{:S(2)}) copy-start(f32[4608]{0:T(1024)} %param.5) | copy-start | bytes 55300
  131.3 16.9 %copy-start.2 = (bf16[2,4608]{1,0:T(2,128)(2,1)S(1)}, bf16[2,4608]{1,0:T(2,128)(2,1)}, u32[]{:S(2)}) copy-start(bf16[2,4608]{1,0:T(2,128)(2,1)} %param.4) | copy-start | bytes 55300
  132.6 15.3 %all-to-all-start.3 = ((bf16[16,4,2304]{2,1,0:T(4,128)(2,1)}), bf16[16,4,2304]{2,1,0:T(4,128)(2,1)S(1)}, u32[]{:S(2)}, u32[]{:S(2)}) async-start(bf16[16,4,2304]{2,1,0:T(4,128)(2,1)} %pad_maximum_fusion.5), calls=%async_computation.3 | async-start | bytes 589824 | tf_op jit(solution)/shard_map/all_to_all | solution.py:415

commit v6 on v5

--- a/solution.py
+++ b/solution.py
@@ -16,7 +16,7 @@
 TOKENS = 512
 VOCAB_ROWS = 512
 PIECE = 16
-STEP = 768
+STEP = 2304
 STEPS = WIDTH // STEP
 HALF_STEPS = HALF // STEP
 

time: 150 us -> 151 us (level)
  no operation moved by 1% of the time
where the time goes in v6:
time: 151 us; the launch traced here: 150 us
  waiting for transfers between devices  51.3 us (34%)
  blocking collectives  42.4 us (28%)
  Pallas kernels  25.3 us (17%)
  starting transfers between devices  23.9 us (16%)
  other arithmetic  6 us (4%)
    all_to_all x2, blocking collectives, gather_over(): return lax.all_to_all(copies, axes, 0, 0, tiled=True)  25.5 us
    ppermute x6, waiting for transfers between devices, shift_second(): return lax.ppermute(block, CROSS, cross_pairs(step, 1))  23 us
    all_to_all x1, blocking collectives, on_device(): lax.all_to_all(halves, ('core', 'z'), 0, 0, tiled=True)  16.9 us
    all_to_all x1, waiting for transfers between devices, on_device(): line_parts = lax.all_to_all(message, ('core', 'z'), 0, 0, tiled=True)  11 us
    ppermute x6, waiting for transfers between devices, shift_first(): return lax.ppermute(block, CROSS, cross_pairs(step, 0))  10.2 us
    ppermute x6, starting transfers between devices, shift_second(): return lax.ppermute(block, CROSS, cross_pairs(step, 1))  9.78 us
    ppermute x6, starting transfers between devices, shift_first(): return lax.ppermute(block, CROSS, cross_pairs(step, 0))  9.63 us
    pallas_call x1, Pallas kernels, forward(): pl.pallas_call(forward_kernel, out_shape=(jax.ShapeDtypeStruct((TOKENS, W...  7.93 us
  transfers between devices with their start and end apart: 18, of which 12 were waited for; matrix products, arithmetic and copies ran while one was open for 0% of the time, Pallas kernels for 4%

profile of v6, /device:TPU:32, one launch (start us, length us, event | category | flops | bytes accessed | tf_op | source)
XLA Modules:
  0.0 150.3 jit_solution(6051024015303396849)
XLA Ops:
  2.5 16.9 %all_to_all.20 = bf16[16,2,2304]{2,1,0:T(2,128)(2,1)S(1)} all-to-all(bf16[16,2,2304]{2,1,0:T(2,128)(2,1)S(1)} %bitcast.30), channel_id=1, replica_groups=mesh['x_lo'=2,'y'=4,'core'=2,'x_hi'=2,'z'=8] {'core','z'}, dimensions={0} | all-to-all | bytes 294912 | tf_op jit(solution)/shard_map/all_to_all | solution.py:383
  19.5 1.6 %collective-permute-start.2 = (bf16[2,16,2304]{2,1,0:T(8,128)(2,1)S(1)}, bf16[2,16,2304]{2,1,0:T(8,128)(2,1)S(1)}, u32[]{:S(2)}, u32[]{:S(2)}) collective-permute-start(bf16[2,16,2304]{2,1,0:T(8,128)(2,1)S(1)} %reshape.134), channel_id=1, source_target_pairs={{0,128},{16,48},{32,160},{48,80},{64,192},{80,112},{96,224},{112,1... | collective-permute-start | bytes 442376 | tf_op jit(solution)/shard_map/ppermute | solution.py:38
  21.1 2.7 %collective-permute-start.1 = (bf16[2,16,2304]{2,1,0:T(8,128)(2,1)S(1)}, bf16[2,16,2304]{2,1,0:T(8,128)(2,1)S(1)}, u32[]{:S(2)}, u32[]{:S(2)}) collective-permute-start(bf16[2,16,2304]{2,1,0:T(8,128)(2,1)S(1)} %reshape.134), channel_id=1, source_target_pairs={{0,8},{16,80},{32,40},{48,112},{64,72},{80,16},{96,104},{112,48},{... | collective-permute-start | bytes 442376 | tf_op jit(solution)/shard_map/ppermute | solution.py:38
  23.8 1.4 collective-permute-start
  25.9 2.6 %collective-permute-done.1 = bf16[2,16,2304]{2,1,0:T(8,128)(2,1)S(1)} collective-permute-done((bf16[2,16,2304]{2,1,0:T(8,128)(2,1)S(1)}, bf16[2,16,2304]{2,1,0:T(8,128)(2,1)S(1)}, u32[]{:S(2)}, u32[]{:S(2)}) %collective-permute-start.1) | collective-permute-done | bytes 147488 | tf_op jit(solution)/shard_map/ppermute | solution.py:38
  29.0 1.7 %collective-permute-start.5 = (bf16[4,2,16,2304]{3,2,1,0:T(8,128)(2,1)S(1)}, bf16[4,2,16,2304]{3,2,1,0:T(8,128)(2,1)S(1)}, u32[]{:S(2)}, u32[]{:S(2)}) collective-permute-start(bf16[4,2,16,2304]{3,2,1,0:T(8,128)(2,1)S(1)} %pad_maximum_fusion.rest_0_), channel_id=1, source_target_pairs={{0,32},{16,144},{32,64},{48,176},{64,96},{80,208},{96,0},{112,240}... | collective-permute-start | bytes 1769480 | tf_op jit(solution)/shard_map/ppermute | solution.py:42
  30.7 2.9 %collective-permute-start.4 = (bf16[4,2,16,2304]{3,2,1,0:T(8,128)(2,1)S(1)}, bf16[4,2,16,2304]{3,2,1,0:T(8,128)(2,1)S(1)}, u32[]{:S(2)}, u32[]{:S(2)}) collective-permute-start(bf16[4,2,16,2304]{3,2,1,0:T(8,128)(2,1)S(1)} %pad_maximum_fusion.rest_0_), channel_id=1, source_target_pairs={{0,64},{16,24},{32,96},{48,56},{64,0},{80,88},{96,32},{112,120},{1... | collective-permute-start | bytes 1769480 | tf_op jit(solution)/shard_map/ppermute | solution.py:42
  33.6 1.3 collective-permute-start.3
  34.9 5.3 %collective-permute-done.5.rest_3_ = bf16[4,2,16,2304]{3,2,1,0:T(8,128)(2,1)S(1)} collective-permute-done((bf16[4,2,16,2304]{3,2,1,0:T(8,128)(2,1)S(1)}, bf16[4,2,16,2304]{3,2,1,0:T(8,128)(2,1)S(1)}, u32[]{:S(2)}, u32[]{:S(2)}) %collective-permute-start.5) | collective-permute-done | bytes 589856 | tf_op jit(solution)/shard_map/ppermute | solution.py:42
  40.2 7.6 %collective-permute-done.4.rest_2_ = bf16[4,2,16,2304]{3,2,1,0:T(8,128)(2,1)S(1)} collective-permute-done((bf16[4,2,16,2304]{3,2,1,0:T(8,128)(2,1)S(1)}, bf16[4,2,16,2304]{3,2,1,0:T(8,128)(2,1)S(1)}, u32[]{:S(2)}, u32[]{:S(2)}) %collective-permute-start.4) | collective-permute-done | bytes 589856 | tf_op jit(solution)/shard_map/ppermute | solution.py:42
  48.3 2.3 %collective-permute-done.8.rest_6_ = bf16[4,2,16,2304]{3,2,1,0:T(8,128)(2,1)} collective-permute-done((bf16[4,2,16,2304]{3,2,1,0:T(8,128)(2,1)S(1)}, bf16[4,2,16,2304]{3,2,1,0:T(8,128)(2,1)}, u32[]{:S(2)}, u32[]{:S(2)}) %collective-permute-start.8) | collective-permute-done | bytes 589856 | tf_op jit(solution)/shard_map/ppermute | solution.py:46
  50.6 7.9 %forward.1 = (bf16[512,4608]{1,0:T(8,128)(2,1)}, f32[512,512]{1,0:T(8,128)}, f32[3,512]{1,0:T(4,128)S(1)}) custom-call(s32[4]{0:T(128)S(1)} %pad_add_fusion.place, s32[1,512]{1,0:T(1,128)S(1)} %bitcast.28, bf16[512,4608]{1,0:T(8,128)(2,1)} %weight.5, bf16[4,2,16,2304]{3,2,1,0:T(8,128)(2,1)S(1)} %pad_maximum_fusion.rest_0_, ...), custom_call_target="tpu_custom_call" | custom-call | flops 2415919104 | bytes 16777216 | tf_op jit(solution)/shard_map/forward/pallas_call | solution.py:164
  58.6 13.8 %all_to_all.21 = f32[16,3,512]{2,1,0:T(4,128)S(1)} all-to-all(f32[16,3,512]{2,1,0:T(4,128)S(1)} %broadcast_in_dim.11), channel_id=1, replica_groups=mesh['x_lo'=2,'y'=4,'core'=2,'x_hi'=2,'z'=8] {'x_lo','y','x_hi'}, dimensions={0} | all-to-all | bytes 196608 | tf_op jit(solution)/shard_map/all_to_all | solution.py:51
  72.5 11.6 %all_to_all.22 = f32[16,3,512]{2,1,0:T(4,128)S(1)} all-to-all(f32[16,3,512]{2,1,0:T(4,128)S(1)} %broadcast_in_dim.12), channel_id=1, replica_groups=mesh['x_lo'=2,'y'=4,'core'=2,'x_hi'=2,'z'=8] {'core','z'}, dimensions={0} | all-to-all | bytes 196608 | tf_op jit(solution)/shard_map/all_to_all | solution.py:51
  84.2 5.7 %far_gradient.1 = (bf16[512,512]{1,0:T(8,128)(2,1)S(1)}, bf16[512,512]{1,0:T(8,128)(2,1)S(1)}, bf16[512,2304]{1,0:T(8,128)(2,1)}) custom-call(s32[4]{0:T(128)S(1)} %pad_add_fusion.place, s32[1,512]{1,0:T(1,128)S(1)} %bitcast.29, f32[512,512]{1,0:T(8,128)} %get-tuple-element.22.capped, f32[3,512]{1,0:T(4,128)S(1)} %reduce_sum.47.totals, bf16[512,4608]{1,0:T(8,128)(2,1)} %weight.5), custom_call_target="tpu_custom_call" | custom-call | flops 1207959552 | bytes 9437184 | tf_op jit(solution)/shard_map/far_gradient/pallas_call | solution.py:236
  90.2 4.7 %collective-permute-done.10.arrived = bf16[512,2304]{1,0:T(8,128)(2,1)S(1)} collective-permute-done((bf16[512,2304]{1,0:T(8,128)(2,1)}, bf16[512,2304]{1,0:T(8,128)(2,1)S(1)}, u32[]{:S(2)}, u32[]{:S(2)}) %collective-permute-start.10) | collective-permute-done | bytes 2359328 | tf_op jit(solution)/shard_map/ppermute | solution.py:46
  94.9 5.8 %near_gradient.1 = (bf16[9,16,2304]{2,1,0:T(8,128)(2,1)S(1)}, bf16[9,16,2304]{2,1,0:T(8,128)(2,1)S(1)}, bf16[9,16,2304]{2,1,0:T(8,128)(2,1)S(1)}, bf16[9,16,2304]{2,1,0:T(8,128)(2,1)S(1)}) custom-call(s32[4]{0:T(128)S(1)} %pad_add_fusion.place, bf16[512,512]{1,0:T(8,128)(2,1)S(1)} %get-tuple-element.24.turned, bf16[512,4608]{1,0:T(8,128)(2,1)} %weight.5, ...), custom_call_target="tpu_custom_call" | custom-call | flops 1207959552 | bytes 12582912 | tf_op jit(solution)/shard_map/near_gradient/pallas_call | solution.py:307
  101.2 2.2 %collective-permute-start.12 = (bf16[9,16,2304]{2,1,0:T(8,128)(2,1)S(1)}, bf16[9,16,2304]{2,1,0:T(8,128)(2,1)S(1)}, u32[]{:S(2)}, u32[]{:S(2)}) collective-permute-start(bf16[9,16,2304]{2,1,0:T(8,128)(2,1)S(1)} %get-tuple-element.31), channel_id=1, source_target_pairs={{0,64},{16,24},{32,96},{48,56},{64,0},{80,88},{96,32},{112,120},{1... | collective-permute-start | bytes 1990664 | tf_op jit(solution)/shard_map/ppermute | solution.py:42
  104.6 5.9 %weight_gradient.1 = bf16[512,4608]{1,0:T(8,128)(2,1)} custom-call(bf16[512,512]{1,0:T(8,128)(2,1)S(1)} %get-tuple-element.28.grad, bf16[512,4608]{1,0:T(8,128)(2,1)} %get-tuple-element.26.gathered), custom_call_target="tpu_custom_call" | custom-call | flops 2415919104 | bytes 10485760 | tf_op jit(solution)/shard_map/weight_gradient/pallas_call | solution.py:351
  110.5 9.3 %collective-permute-done.11 = bf16[9,16,2304]{2,1,0:T(8,128)(2,1)S(1)} collective-permute-done((bf16[9,16,2304]{2,1,0:T(8,128)(2,1)S(1)}, bf16[9,16,2304]{2,1,0:T(8,128)(2,1)S(1)}, u32[]{:S(2)}, u32[]{:S(2)}) %collective-permute-start.11) | collective-permute-done | bytes 663584 | tf_op jit(solution)/shard_map/ppermute | solution.py:42
  121.9 2.2 %collective-permute-start.15 = (bf16[3,16,2304]{2,1,0:T(8,128)(2,1)S(1)}, bf16[3,16,2304]{2,1,0:T(8,128)(2,1)S(1)}, u32[]{:S(2)}, u32[]{:S(2)}) collective-permute-start(bf16[3,16,2304]{2,1,0:T(8,128)(2,1)S(1)} %get-tuple-element.51), channel_id=1, source_target_pairs={{0,8},{16,80},{32,40},{48,112},{64,72},{80,16},{96,104},{112,48},{... | collective-permute-start | bytes 663560 | tf_op jit(solution)/shard_map/ppermute | solution.py:38
  125.1 5.7 %collective-permute-done.14 = bf16[3,16,2304]{2,1,0:T(8,128)(2,1)S(1)} collective-permute-done((bf16[3,16,2304]{2,1,0:T(8,128)(2,1)S(1)}, bf16[3,16,2304]{2,1,0:T(8,128)(2,1)S(1)}, u32[]{:S(2)}, u32[]{:S(2)}) %collective-permute-start.14) | collective-permute-done | bytes 221216 | tf_op jit(solution)/shard_map/ppermute | solution.py:38
  133.2 3.7 %all-to-all-start.3 = ((bf16[16,4,2304]{2,1,0:T(4,128)(2,1)}), bf16[16,4,2304]{2,1,0:T(4,128)(2,1)S(1)}, u32[]{:S(2)}, u32[]{:S(2)}) async-start(bf16[16,4,2304]{2,1,0:T(4,128)(2,1)} %pad_maximum_fusion.5), calls=%async_computation.3 | async-start | bytes 589824 | tf_op jit(solution)/shard_map/all_to_all | solution.py:415
  137.4 11.0 %all-to-all-done.3 = bf16[16,4,2304]{2,1,0:T(4,128)(2,1)S(1)} async-done(((bf16[16,4,2304]{2,1,0:T(4,128)(2,1)}), bf16[16,4,2304]{2,1,0:T(4,128)(2,1)S(1)}, u32[]{:S(2)}, u32[]{:S(2)}) %all-to-all-start.3) | async-done | bytes 294944 | tf_op jit(solution)/shard_map/all_to_all | solution.py:415
  (63 shorter events, 13.5 us)
Async XLA Ops:
  0.6 50.0 %copy-start = (s32[512]{0:T(512)S(1)}, s32[512]{0:T(512)}, u32[]{:S(2)}) copy-start(s32[512]{0:T(512)} %param.7) | copy-start | bytes 6148
  19.5 6.4 %collective-permute-start.2 = (bf16[2,16,2304]{2,1,0:T(8,128)(2,1)S(1)}, bf16[2,16,2304]{2,1,0:T(8,128)(2,1)S(1)}, u32[]{:S(2)}, u32[]{:S(2)}) collective-permute-start(bf16[2,16,2304]{2,1,0:T(8,128)(2,1)S(1)} %reshape.134), channel_id=1, source_target_pairs={{0,128},{16,48},{32,160},{48,80},{64,192},{80,112},{96,224},{112,1... | collective-permute-start | bytes 442376 | tf_op jit(solution)/shard_map/ppermute | solution.py:38
  21.1 7.4 %collective-permute-start.1 = (bf16[2,16,2304]{2,1,0:T(8,128)(2,1)S(1)}, bf16[2,16,2304]{2,1,0:T(8,128)(2,1)S(1)}, u32[]{:S(2)}, u32[]{:S(2)}) collective-permute-start(bf16[2,16,2304]{2,1,0:T(8,128)(2,1)S(1)} %reshape.134), channel_id=1, source_target_pairs={{0,8},{16,80},{32,40},{48,112},{64,72},{80,16},{96,104},{112,48},{... | collective-permute-start | bytes 442376 | tf_op jit(solution)/shard_map/ppermute | solution.py:38
  23.8 5.1 %collective-permute-start = (bf16[2,16,2304]{2,1,0:T(8,128)(2,1)S(1)}, bf16[2,16,2304]{2,1,0:T(8,128)(2,1)S(1)}, u32[]{:S(2)}, u32[]{:S(2)}) collective-permute-start(bf16[2,16,2304]{2,1,0:T(8,128)(2,1)S(1)} %reshape.134), channel_id=1, source_target_pairs={{0,136},{16,112},{32,168},{48,16},{64,200},{80,48},{96,232},{112,8... | collective-permute-start | bytes 442376 | tf_op jit(solution)/shard_map/ppermute | solution.py:38
  29.0 11.2 %collective-permute-start.5 = (bf16[4,2,16,2304]{3,2,1,0:T(8,128)(2,1)S(1)}, bf16[4,2,16,2304]{3,2,1,0:T(8,128)(2,1)S(1)}, u32[]{:S(2)}, u32[]{:S(2)}) collective-permute-start(bf16[4,2,16,2304]{3,2,1,0:T(8,128)(2,1)S(1)} %pad_maximum_fusion.rest_0_), channel_id=1, source_target_pairs={{0,32},{16,144},{32,64},{48,176},{64,96},{80,208},{96,0},{112,240}... | collective-permute-start | bytes 1769480 | tf_op jit(solution)/shard_map/ppermute | solution.py:42
  30.7 17.1 %collective-permute-start.4 = (bf16[4,2,16,2304]{3,2,1,0:T(8,128)(2,1)S(1)}, bf16[4,2,16,2304]{3,2,1,0:T(8,128)(2,1)S(1)}, u32[]{:S(2)}, u32[]{:S(2)}) collective-permute-start(bf16[4,2,16,2304]{3,2,1,0:T(8,128)(2,1)S(1)} %pad_maximum_fusion.rest_0_), channel_id=1, source_target_pairs={{0,64},{16,24},{32,96},{48,56},{64,0},{80,88},{96,32},{112,120},{1... | collective-permute-start | bytes 1769480 | tf_op jit(solution)/shard_map/ppermute | solution.py:42
  33.6 14.2 %collective-permute-start.3 = (bf16[4,2,16,2304]{3,2,1,0:T(8,128)(2,1)S(1)}, bf16[4,2,16,2304]{3,2,1,0:T(8,128)(2,1)S(1)}, u32[]{:S(2)}, u32[]{:S(2)}) collective-permute-start(bf16[4,2,16,2304]{3,2,1,0:T(8,128)(2,1)S(1)} %pad_maximum_fusion.rest_0_), channel_id=1, source_target_pairs={{0,96},{16,152},{32,0},{48,184},{64,32},{80,216},{96,64},{112,248}... | collective-permute-start | bytes 1769480 | tf_op jit(solution)/shard_map/ppermute | solution.py:42
  34.9 13.4 %collective-permute-start.6 = (bf16[4,2,16,2304]{3,2,1,0:T(8,128)(2,1)S(1)}, bf16[4,2,16,2304]{3,2,1,0:T(8,128)(2,1)S(1)}, u32[]{:S(2)}, u32[]{:S(2)}) collective-permute-start(bf16[4,2,16,2304]{3,2,1,0:T(8,128)(2,1)S(1)} %pad_maximum_fusion.rest_0_), channel_id=1, source_target_pairs={{0,16},{16,0},{1,17},{17,1},{2,18},{18,2},{3,19},{19,3},{4,20},{20... | collective-permute-start | bytes 1769480 | tf_op jit(solution)/shard_map/ppermute | solution.py:46
  40.2 8.2 %collective-permute-start.9 = (bf16[4,2,16,2304]{3,2,1,0:T(8,128)(2,1)S(1)}, bf16[4,2,16,2304]{3,2,1,0:T(8,128)(2,1)}, u32[]{:S(2)}, u32[]{:S(2)}) collective-permute-start(bf16[4,2,16,2304]{3,2,1,0:T(8,128)(2,1)S(1)} %collective-permute-done.5.rest_3_), channel_id=1, source_target_pairs={{0,16},{16,0},{1,17},{17,1},{2,18},{18,2},{3,19},{19,3},{4,20},{20... | collective-permute-start | bytes 1769480 | tf_op jit(solution)/shard_map/ppermute | solution.py:46
  47.7 2.9 %collective-permute-start.8 = (bf16[4,2,16,2304]{3,2,1,0:T(8,128)(2,1)S(1)}, bf16[4,2,16,2304]{3,2,1,0:T(8,128)(2,1)}, u32[]{:S(2)}, u32[]{:S(2)}) collective-permute-start(bf16[4,2,16,2304]{3,2,1,0:T(8,128)(2,1)S(1)} %collective-permute-done.4.rest_2_), channel_id=1, source_target_pairs={{0,16},{16,0},{1,17},{17,1},{2,18},{18,2},{3,19},{19,3},{4,20},{20... | collective-permute-start | bytes 1769480 | tf_op jit(solution)/shard_map/ppermute | solution.py:46
  47.7 2.9 %collective-permute-start.7 = (bf16[4,2,16,2304]{3,2,1,0:T(8,128)(2,1)S(1)}, bf16[4,2,16,2304]{3,2,1,0:T(8,128)(2,1)S(1)}, u32[]{:S(2)}, u32[]{:S(2)}) collective-permute-start(bf16[4,2,16,2304]{3,2,1,0:T(8,128)(2,1)S(1)} %collective-permute-done.3.rest_1_), channel_id=1, source_target_pairs={{0,16},{16,0},{1,17},{17,1},{2,18},{18,2},{3,19},{19,3},{4,20},{20... | collective-permute-start | bytes 1769480 | tf_op jit(solution)/shard_map/ppermute | solution.py:46
  89.9 5.0 %collective-permute-start.10 = (bf16[512,2304]{1,0:T(8,128)(2,1)}, bf16[512,2304]{1,0:T(8,128)(2,1)S(1)}, u32[]{:S(2)}, u32[]{:S(2)}) collective-permute-start(bf16[512,2304]{1,0:T(8,128)(2,1)} %get-tuple-element.25), channel_id=1, source_target_pairs={{0,16},{16,0},{1,17},{17,1},{2,18},{18,2},{3,19},{19,3},{4,20},{20... | collective-permute-start | bytes 7077896 | tf_op jit(solution)/shard_map/ppermute | solution.py:46
  100.7 19.1 %collective-permute-start.11 = (bf16[9,16,2304]{2,1,0:T(8,128)(2,1)S(1)}, bf16[9,16,2304]{2,1,0:T(8,128)(2,1)S(1)}, u32[]{:S(2)}, u32[]{:S(2)}) collective-permute-start(bf16[9,16,2304]{2,1,0:T(8,128)(2,1)S(1)} %get-tuple-element.30), channel_id=1, source_target_pairs={{0,32},{16,144},{32,64},{48,176},{64,96},{80,208},{96,0},{112,240}... | collective-permute-start | bytes 1990664 | tf_op jit(solution)/shard_map/ppermute | solution.py:42
  101.2 18.6 %collective-permute-start.12 = (bf16[9,16,2304]{2,1,0:T(8,128)(2,1)S(1)}, bf16[9,16,2304]{2,1,0:T(8,128)(2,1)S(1)}, u32[]{:S(2)}, u32[]{:S(2)}) collective-permute-start(bf16[9,16,2304]{2,1,0:T(8,128)(2,1)S(1)} %get-tuple-element.31), channel_id=1, source_target_pairs={{0,64},{16,24},{32,96},{48,56},{64,0},{80,88},{96,32},{112,120},{1... | collective-permute-start | bytes 1990664 | tf_op jit(solution)/shard_map/ppermute | solution.py:42
  103.4 17.3 %collective-permute-start.13 = (bf16[9,16,2304]{2,1,0:T(8,128)(2,1)S(1)}, bf16[9,16,2304]{2,1,0:T(8,128)(2,1)S(1)}, u32[]{:S(2)}, u32[]{:S(2)}) collective-permute-start(bf16[9,16,2304]{2,1,0:T(8,128)(2,1)S(1)} %get-tuple-element.32), channel_id=1, source_target_pairs={{0,96},{16,152},{32,0},{48,184},{64,32},{80,216},{96,64},{112,248}... | collective-permute-start | bytes 1990664 | tf_op jit(solution)/shard_map/ppermute | solution.py:42
  121.3 9.6 %collective-permute-start.14 = (bf16[3,16,2304]{2,1,0:T(8,128)(2,1)S(1)}, bf16[3,16,2304]{2,1,0:T(8,128)(2,1)S(1)}, u32[]{:S(2)}, u32[]{:S(2)}) collective-permute-start(bf16[3,16,2304]{2,1,0:T(8,128)(2,1)S(1)} %get-tuple-element.50), channel_id=1, source_target_pairs={{0,128},{16,48},{32,160},{48,80},{64,192},{80,112},{96,224},{112,1... | collective-permute-start | bytes 663560 | tf_op jit(solution)/shard_map/ppermute | solution.py:38
  121.9 9.0 %collective-permute-start.15 = (bf16[3,16,2304]{2,1,0:T(8,128)(2,1)S(1)}, bf16[3,16,2304]{2,1,0:T(8,128)(2,1)S(1)}, u32[]{:S(2)}, u32[]{:S(2)}) collective-permute-start(bf16[3,16,2304]{2,1,0:T(8,128)(2,1)S(1)} %get-tuple-element.51), channel_id=1, source_target_pairs={{0,8},{16,80},{32,40},{48,112},{64,72},{80,16},{96,104},{112,48},{... | collective-permute-start | bytes 663560 | tf_op jit(solution)/shard_map/ppermute | solution.py:38
  124.1 7.6 %collective-permute-start.16 = (bf16[3,16,2304]{2,1,0:T(8,128)(2,1)S(1)}, bf16[3,16,2304]{2,1,0:T(8,128)(2,1)S(1)}, u32[]{:S(2)}, u32[]{:S(2)}) collective-permute-start(bf16[3,16,2304]{2,1,0:T(8,128)(2,1)S(1)} %get-tuple-element.52), channel_id=1, source_target_pairs={{0,136},{16,112},{32,168},{48,16},{64,200},{80,48},{96,232},{112,8... | collective-permute-start | bytes 663560 | tf_op jit(solution)/shard_map/ppermute | solution.py:38
  131.9 16.8 %copy-start.1 = (f32[4608]{0:T(1024)S(1)}, f32[4608]{0:T(1024)}, u32[]{:S(2)}) copy-start(f32[4608]{0:T(1024)} %param.5) | copy-start | bytes 55300
  131.9 16.8 %copy-start.2 = (bf16[2,4608]{1,0:T(2,128)(2,1)S(1)}, bf16[2,4608]{1,0:T(2,128)(2,1)}, u32[]{:S(2)}) copy-start(bf16[2,4608]{1,0:T(2,128)(2,1)} %param.4) | copy-start | bytes 55300
  133.2 15.3 %all-to-all-start.3 = ((bf16[16,4,2304]{2,1,0:T(4,128)(2,1)}), bf16[16,4,2304]{2,1,0:T(4,128)(2,1)S(1)}, u32[]{:S(2)}, u32[]{:S(2)}) async-start(bf16[16,4,2304]{2,1,0:T(4,128)(2,1)} %pad_maximum_fusion.5), calls=%async_computation.3 | async-start | bytes 589824 | tf_op jit(solution)/shard_map/all_to_all | solution.py:415

commit v7 on v4

--- a/solution.py
+++ b/solution.py
@@ -94,7 +94,7 @@
         return rows_held.at[:, half_columns(half)]
 
     def weight_copy(j):
-        columns = step_columns(j)
+        columns = half_columns(j)
         return pltpu.make_async_copy(weight.at[:, columns], weight_held.at[:, columns], weight_sems.at[j])
 
     def place_blocks(half, held):
@@ -115,7 +115,7 @@
 
     def multiply(j):
         weight_copy(j).wait()
-        columns = step_columns(j)
+        columns = half_columns(j)
         logits[...] += lax.dot_general(
             weight_held[:, columns],
             rows_held[:, columns],
@@ -123,17 +123,17 @@
             preferred_element_type=jnp.float32,
         )
 
-    steps(lambda j: weight_copy(j).start(), 0, HALF_STEPS)
+    steps(lambda j: weight_copy(j).start(), 0, 1)
     place_blocks(core, blocks[:4])
-    steps(lambda j: weight_copy(j).start(), HALF_STEPS, STEPS)
+    steps(lambda j: weight_copy(j).start(), 1, 2)
     place_blocks(1 - core, blocks[4:])
     logits[...] = jnp.zeros_like(logits)
     pltpu.make_async_copy(half_rows(0), half_rows(0), row_sems.at[0]).wait()
-    steps(multiply, 0, HALF_STEPS)
+    steps(multiply, 0, 1)
     pltpu.make_async_copy(half_rows(1), half_rows(1), row_sems.at[1]).wait()
     out_copy = pltpu.make_async_copy(rows_held, gathered, out_sem)
     out_copy.start()
-    steps(multiply, HALF_STEPS, STEPS)
+    steps(multiply, 1, 2)
 
     def finish(k, carry):
         rows = pl.ds(pl.multiple_of(k * 64, 64), 64)
@@ -397,8 +397,9 @@
         high = lax.reduce_precision(gain, 8, 7)
         return jnp.concatenate([high, gain - high], axis=0).astype(jnp.bfloat16)
 
-    parts = send_ring(sends, shift_second)
-    grad, parts[1] = lax.optimization_barrier((grad, parts[1]))
+    own, *others = sends
+    grad, own = lax.optimization_barrier((grad, own))
+    parts = send_ring([own, *others], shift_second)
     grad_weight = weight_gradient(grad, gathered)
     grad_weight, *parts = lax.optimization_barrier((grad_weight, *parts))
     half_sum = total(parts)

time: 155 us -> 150 us (0.968)
  waiting for transfers between devices: 56.4 us -> 51.6 us
    ppermute x6, waiting for transfers between devices: 28 us -> 23.3 us  [shift_second(): return lax.ppermute(block, CROSS, cross_pairs(step, 1))]
  transfers between devices with their start and end apart: 18 -> 18, of which waited for: 11 -> 12; matrix products, arithmetic and copies ran while one was open for 0% -> 0% of each run, Pallas kernels for 4% -> 4%
where the time goes in v7:
time: 150 us; the launch traced here: 149 us
  waiting for transfers between devices  51.6 us (34%)
  blocking collectives  42.4 us (28%)
  starting transfers between devices  23.9 us (16%)
  Pallas kernels  23.8 us (16%)
  other arithmetic  6 us (4%)
    all_to_all x2, blocking collectives, gather_over(): return lax.all_to_all(copies, axes, 0, 0, tiled=True)  25.5 us
    ppermute x6, waiting for transfers between devices, shift_second(): return lax.ppermute(block, CROSS, cross_pairs(step, 1))  23.3 us
    all_to_all x1, blocking collectives, on_device(): lax.all_to_all(halves, ('core', 'z'), 0, 0, tiled=True)  16.9 us
    all_to_all x1, waiting for transfers between devices, on_device(): line_parts = lax.all_to_all(message, ('core', 'z'), 0, 0, tiled=True)  11 us
    ppermute x6, waiting for transfers between devices, shift_first(): return lax.ppermute(block, CROSS, cross_pairs(step, 0))  10.2 us
    ppermute x6, starting transfers between devices, shift_second(): return lax.ppermute(block, CROSS, cross_pairs(step, 1))  9.95 us
    ppermute x6, starting transfers between devices, shift_first(): return lax.ppermute(block, CROSS, cross_pairs(step, 0))  9.63 us
    pallas_call x1, Pallas kernels, forward(): pl.pallas_call(forward_kernel, out_shape=(jax.ShapeDtypeStruct((TOKENS, W...  7.96 us
  transfers between devices with their start and end apart: 18, of which 12 were waited for; matrix products, arithmetic and copies ran while one was open for 0% of the time, Pallas kernels for 4%

profile of v7, /device:TPU:32, one launch (start us, length us, event | category | flops | bytes accessed | tf_op | source)
XLA Modules:
  0.0 149.1 jit_solution(1447982529176926073)
XLA Ops:
  2.5 16.9 %all_to_all.20 = bf16[16,2,2304]{2,1,0:T(2,128)(2,1)S(1)} all-to-all(bf16[16,2,2304]{2,1,0:T(2,128)(2,1)S(1)} %bitcast.30), channel_id=1, replica_groups=mesh['x_lo'=2,'y'=4,'core'=2,'x_hi'=2,'z'=8] {'core','z'}, dimensions={0} | all-to-all | bytes 294912 | tf_op jit(solution)/shard_map/all_to_all | solution.py:383
  19.5 1.6 %collective-permute-start.2 = (bf16[2,16,2304]{2,1,0:T(8,128)(2,1)S(1)}, bf16[2,16,2304]{2,1,0:T(8,128)(2,1)S(1)}, u32[]{:S(2)}, u32[]{:S(2)}) collective-permute-start(bf16[2,16,2304]{2,1,0:T(8,128)(2,1)S(1)} %reshape.134), channel_id=1, source_target_pairs={{0,128},{16,48},{32,160},{48,80},{64,192},{80,112},{96,224},{112,1... | collective-permute-start | bytes 442376 | tf_op jit(solution)/shard_map/ppermute | solution.py:38
  21.1 2.7 %collective-permute-start.1 = (bf16[2,16,2304]{2,1,0:T(8,128)(2,1)S(1)}, bf16[2,16,2304]{2,1,0:T(8,128)(2,1)S(1)}, u32[]{:S(2)}, u32[]{:S(2)}) collective-permute-start(bf16[2,16,2304]{2,1,0:T(8,128)(2,1)S(1)} %reshape.134), channel_id=1, source_target_pairs={{0,8},{16,80},{32,40},{48,112},{64,72},{80,16},{96,104},{112,48},{... | collective-permute-start | bytes 442376 | tf_op jit(solution)/shard_map/ppermute | solution.py:38
  23.8 1.4 collective-permute-start
  25.9 2.6 %collective-permute-done.1 = bf16[2,16,2304]{2,1,0:T(8,128)(2,1)S(1)} collective-permute-done((bf16[2,16,2304]{2,1,0:T(8,128)(2,1)S(1)}, bf16[2,16,2304]{2,1,0:T(8,128)(2,1)S(1)}, u32[]{:S(2)}, u32[]{:S(2)}) %collective-permute-start.1) | collective-permute-done | bytes 147488 | tf_op jit(solution)/shard_map/ppermute | solution.py:38
  29.0 1.7 %collective-permute-start.5 = (bf16[4,2,16,2304]{3,2,1,0:T(8,128)(2,1)S(1)}, bf16[4,2,16,2304]{3,2,1,0:T(8,128)(2,1)S(1)}, u32[]{:S(2)}, u32[]{:S(2)}) collective-permute-start(bf16[4,2,16,2304]{3,2,1,0:T(8,128)(2,1)S(1)} %pad_maximum_fusion.rest_0_), channel_id=1, source_target_pairs={{0,32},{16,144},{32,64},{48,176},{64,96},{80,208},{96,0},{112,240}... | collective-permute-start | bytes 1769480 | tf_op jit(solution)/shard_map/ppermute | solution.py:42
  30.7 2.9 %collective-permute-start.4 = (bf16[4,2,16,2304]{3,2,1,0:T(8,128)(2,1)S(1)}, bf16[4,2,16,2304]{3,2,1,0:T(8,128)(2,1)S(1)}, u32[]{:S(2)}, u32[]{:S(2)}) collective-permute-start(bf16[4,2,16,2304]{3,2,1,0:T(8,128)(2,1)S(1)} %pad_maximum_fusion.rest_0_), channel_id=1, source_target_pairs={{0,64},{16,24},{32,96},{48,56},{64,0},{80,88},{96,32},{112,120},{1... | collective-permute-start | bytes 1769480 | tf_op jit(solution)/shard_map/ppermute | solution.py:42
  33.6 1.3 collective-permute-start.3
  34.9 5.3 %collective-permute-done.5.rest_3_ = bf16[4,2,16,2304]{3,2,1,0:T(8,128)(2,1)S(1)} collective-permute-done((bf16[4,2,16,2304]{3,2,1,0:T(8,128)(2,1)S(1)}, bf16[4,2,16,2304]{3,2,1,0:T(8,128)(2,1)S(1)}, u32[]{:S(2)}, u32[]{:S(2)}) %collective-permute-start.5) | collective-permute-done | bytes 589856 | tf_op jit(solution)/shard_map/ppermute | solution.py:42
  40.2 7.6 %collective-permute-done.4.rest_2_ = bf16[4,2,16,2304]{3,2,1,0:T(8,128)(2,1)S(1)} collective-permute-done((bf16[4,2,16,2304]{3,2,1,0:T(8,128)(2,1)S(1)}, bf16[4,2,16,2304]{3,2,1,0:T(8,128)(2,1)S(1)}, u32[]{:S(2)}, u32[]{:S(2)}) %collective-permute-start.4) | collective-permute-done | bytes 589856 | tf_op jit(solution)/shard_map/ppermute | solution.py:42
  48.3 2.3 %collective-permute-done.8.rest_6_ = bf16[4,2,16,2304]{3,2,1,0:T(8,128)(2,1)} collective-permute-done((bf16[4,2,16,2304]{3,2,1,0:T(8,128)(2,1)S(1)}, bf16[4,2,16,2304]{3,2,1,0:T(8,128)(2,1)}, u32[]{:S(2)}, u32[]{:S(2)}) %collective-permute-start.8) | collective-permute-done | bytes 589856 | tf_op jit(solution)/shard_map/ppermute | solution.py:46
  50.6 8.0 %forward.1 = (bf16[512,4608]{1,0:T(8,128)(2,1)}, f32[512,512]{1,0:T(8,128)}, f32[3,512]{1,0:T(4,128)S(1)}) custom-call(s32[4]{0:T(128)S(1)} %pad_add_fusion.place, s32[1,512]{1,0:T(1,128)S(1)} %bitcast.28, bf16[512,4608]{1,0:T(8,128)(2,1)} %weight.5, bf16[4,2,16,2304]{3,2,1,0:T(8,128)(2,1)S(1)} %pad_maximum_fusion.rest_0_, ...), custom_call_target="tpu_custom_call" | custom-call | flops 2415919104 | bytes 16777216 | tf_op jit(solution)/shard_map/forward/pallas_call | solution.py:164
  58.6 13.8 %all_to_all.21 = f32[16,3,512]{2,1,0:T(4,128)S(1)} all-to-all(f32[16,3,512]{2,1,0:T(4,128)S(1)} %broadcast_in_dim.11), channel_id=1, replica_groups=mesh['x_lo'=2,'y'=4,'core'=2,'x_hi'=2,'z'=8] {'x_lo','y','x_hi'}, dimensions={0} | all-to-all | bytes 196608 | tf_op jit(solution)/shard_map/all_to_all | solution.py:51
  72.5 11.6 %all_to_all.22 = f32[16,3,512]{2,1,0:T(4,128)S(1)} all-to-all(f32[16,3,512]{2,1,0:T(4,128)S(1)} %broadcast_in_dim.12), channel_id=1, replica_groups=mesh['x_lo'=2,'y'=4,'core'=2,'x_hi'=2,'z'=8] {'core','z'}, dimensions={0} | all-to-all | bytes 196608 | tf_op jit(solution)/shard_map/all_to_all | solution.py:51
  84.2 5.0 %far_gradient.1 = (bf16[512,512]{1,0:T(8,128)(2,1)S(1)}, bf16[512,512]{1,0:T(8,128)(2,1)S(1)}, bf16[512,2304]{1,0:T(8,128)(2,1)}) custom-call(s32[4]{0:T(128)S(1)} %pad_add_fusion.place, s32[1,512]{1,0:T(1,128)S(1)} %bitcast.29, f32[512,512]{1,0:T(8,128)} %get-tuple-element.22.capped, f32[3,512]{1,0:T(4,128)S(1)} %reduce_sum.47.totals, bf16[512,4608]{1,0:T(8,128)(2,1)} %weight.5), custom_call_target="tpu_custom_call" | custom-call | flops 1207959552 | bytes 9437184 | tf_op jit(solution)/shard_map/far_gradient/pallas_call | solution.py:236
  89.4 4.7 %collective-permute-done.10.arrived = bf16[512,2304]{1,0:T(8,128)(2,1)S(1)} collective-permute-done((bf16[512,2304]{1,0:T(8,128)(2,1)}, bf16[512,2304]{1,0:T(8,128)(2,1)S(1)}, u32[]{:S(2)}, u32[]{:S(2)}) %collective-permute-start.10) | collective-permute-done | bytes 2359328 | tf_op jit(solution)/shard_map/ppermute | solution.py:46
  94.1 5.2 %near_gradient.1 = (bf16[9,16,2304]{2,1,0:T(8,128)(2,1)S(1)}, bf16[9,16,2304]{2,1,0:T(8,128)(2,1)S(1)}, bf16[9,16,2304]{2,1,0:T(8,128)(2,1)S(1)}, bf16[9,16,2304]{2,1,0:T(8,128)(2,1)S(1)}) custom-call(s32[4]{0:T(128)S(1)} %pad_add_fusion.place, bf16[512,512]{1,0:T(8,128)(2,1)S(1)} %get-tuple-element.24.turned, bf16[512,4608]{1,0:T(8,128)(2,1)} %weight.5, ...), custom_call_target="tpu_custom_call" | custom-call | flops 1207959552 | bytes 12582912 | tf_op jit(solution)/shard_map/near_gradient/pallas_call | solution.py:307
  99.9 2.2 %collective-permute-start.12 = (bf16[9,16,2304]{2,1,0:T(8,128)(2,1)S(1)}, bf16[9,16,2304]{2,1,0:T(8,128)(2,1)S(1)}, u32[]{:S(2)}, u32[]{:S(2)}) collective-permute-start(bf16[9,16,2304]{2,1,0:T(8,128)(2,1)S(1)} %get-tuple-element.31), channel_id=1, source_target_pairs={{0,64},{16,24},{32,96},{48,56},{64,0},{80,88},{96,32},{112,120},{1... | collective-permute-start | bytes 1990664 | tf_op jit(solution)/shard_map/ppermute | solution.py:42
  103.3 5.6 %weight_gradient.1 = bf16[512,4608]{1,0:T(8,128)(2,1)} custom-call(bf16[512,512]{1,0:T(8,128)(2,1)S(1)} %get-tuple-element.28.grad, bf16[512,4608]{1,0:T(8,128)(2,1)} %get-tuple-element.26.gathered), custom_call_target="tpu_custom_call" | custom-call | flops 2415919104 | bytes 10485760 | tf_op jit(solution)/shard_map/weight_gradient/pallas_call | solution.py:351
  108.9 9.6 %collective-permute-done.11 = bf16[9,16,2304]{2,1,0:T(8,128)(2,1)S(1)} collective-permute-done((bf16[9,16,2304]{2,1,0:T(8,128)(2,1)S(1)}, bf16[9,16,2304]{2,1,0:T(8,128)(2,1)S(1)}, u32[]{:S(2)}, u32[]{:S(2)}) %collective-permute-start.11) | collective-permute-done | bytes 663584 | tf_op jit(solution)/shard_map/ppermute | solution.py:42
  120.6 2.2 %collective-permute-start.15 = (bf16[3,16,2304]{2,1,0:T(8,128)(2,1)S(1)}, bf16[3,16,2304]{2,1,0:T(8,128)(2,1)S(1)}, u32[]{:S(2)}, u32[]{:S(2)}) collective-permute-start(bf16[3,16,2304]{2,1,0:T(8,128)(2,1)S(1)} %get-tuple-element.51), channel_id=1, source_target_pairs={{0,8},{16,80},{32,40},{48,112},{64,72},{80,16},{96,104},{112,48},{... | collective-permute-start | bytes 663560 | tf_op jit(solution)/shard_map/ppermute | solution.py:38
  123.9 5.7 %collective-permute-done.14 = bf16[3,16,2304]{2,1,0:T(8,128)(2,1)S(1)} collective-permute-done((bf16[3,16,2304]{2,1,0:T(8,128)(2,1)S(1)}, bf16[3,16,2304]{2,1,0:T(8,128)(2,1)S(1)}, u32[]{:S(2)}, u32[]{:S(2)}) %collective-permute-start.14) | collective-permute-done | bytes 221216 | tf_op jit(solution)/shard_map/ppermute | solution.py:38
  131.9 3.7 %all-to-all-start.3 = ((bf16[16,4,2304]{2,1,0:T(4,128)(2,1)}), bf16[16,4,2304]{2,1,0:T(4,128)(2,1)S(1)}, u32[]{:S(2)}, u32[]{:S(2)}) async-start(bf16[16,4,2304]{2,1,0:T(4,128)(2,1)} %pad_maximum_fusion.5), calls=%async_computation.3 | async-start | bytes 589824 | tf_op jit(solution)/shard_map/all_to_all | solution.py:415
  136.2 11.0 %all-to-all-done.3 = bf16[16,4,2304]{2,1,0:T(4,128)(2,1)S(1)} async-done(((bf16[16,4,2304]{2,1,0:T(4,128)(2,1)}), bf16[16,4,2304]{2,1,0:T(4,128)(2,1)S(1)}, u32[]{:S(2)}, u32[]{:S(2)}) %all-to-all-start.3) | async-done | bytes 294944 | tf_op jit(solution)/shard_map/all_to_all | solution.py:415
  (63 shorter events, 13.5 us)
Async XLA Ops:
  0.6 50.0 %copy-start = (s32[512]{0:T(512)S(1)}, s32[512]{0:T(512)}, u32[]{:S(2)}) copy-start(s32[512]{0:T(512)} %param.7) | copy-start | bytes 6148
  19.5 6.4 %collective-permute-start.2 = (bf16[2,16,2304]{2,1,0:T(8,128)(2,1)S(1)}, bf16[2,16,2304]{2,1,0:T(8,128)(2,1)S(1)}, u32[]{:S(2)}, u32[]{:S(2)}) collective-permute-start(bf16[2,16,2304]{2,1,0:T(8,128)(2,1)S(1)} %reshape.134), channel_id=1, source_target_pairs={{0,128},{16,48},{32,160},{48,80},{64,192},{80,112},{96,224},{112,1... | collective-permute-start | bytes 442376 | tf_op jit(solution)/shard_map/ppermute | solution.py:38
  21.1 7.4 %collective-permute-start.1 = (bf16[2,16,2304]{2,1,0:T(8,128)(2,1)S(1)}, bf16[2,16,2304]{2,1,0:T(8,128)(2,1)S(1)}, u32[]{:S(2)}, u32[]{:S(2)}) collective-permute-start(bf16[2,16,2304]{2,1,0:T(8,128)(2,1)S(1)} %reshape.134), channel_id=1, source_target_pairs={{0,8},{16,80},{32,40},{48,112},{64,72},{80,16},{96,104},{112,48},{... | collective-permute-start | bytes 442376 | tf_op jit(solution)/shard_map/ppermute | solution.py:38
  23.8 5.1 %collective-permute-start = (bf16[2,16,2304]{2,1,0:T(8,128)(2,1)S(1)}, bf16[2,16,2304]{2,1,0:T(8,128)(2,1)S(1)}, u32[]{:S(2)}, u32[]{:S(2)}) collective-permute-start(bf16[2,16,2304]{2,1,0:T(8,128)(2,1)S(1)} %reshape.134), channel_id=1, source_target_pairs={{0,136},{16,112},{32,168},{48,16},{64,200},{80,48},{96,232},{112,8... | collective-permute-start | bytes 442376 | tf_op jit(solution)/shard_map/ppermute | solution.py:38
  29.0 11.2 %collective-permute-start.5 = (bf16[4,2,16,2304]{3,2,1,0:T(8,128)(2,1)S(1)}, bf16[4,2,16,2304]{3,2,1,0:T(8,128)(2,1)S(1)}, u32[]{:S(2)}, u32[]{:S(2)}) collective-permute-start(bf16[4,2,16,2304]{3,2,1,0:T(8,128)(2,1)S(1)} %pad_maximum_fusion.rest_0_), channel_id=1, source_target_pairs={{0,32},{16,144},{32,64},{48,176},{64,96},{80,208},{96,0},{112,240}... | collective-permute-start | bytes 1769480 | tf_op jit(solution)/shard_map/ppermute | solution.py:42
  30.7 17.1 %collective-permute-start.4 = (bf16[4,2,16,2304]{3,2,1,0:T(8,128)(2,1)S(1)}, bf16[4,2,16,2304]{3,2,1,0:T(8,128)(2,1)S(1)}, u32[]{:S(2)}, u32[]{:S(2)}) collective-permute-start(bf16[4,2,16,2304]{3,2,1,0:T(8,128)(2,1)S(1)} %pad_maximum_fusion.rest_0_), channel_id=1, source_target_pairs={{0,64},{16,24},{32,96},{48,56},{64,0},{80,88},{96,32},{112,120},{1... | collective-permute-start | bytes 1769480 | tf_op jit(solution)/shard_map/ppermute | solution.py:42
  33.6 14.2 %collective-permute-start.3 = (bf16[4,2,16,2304]{3,2,1,0:T(8,128)(2,1)S(1)}, bf16[4,2,16,2304]{3,2,1,0:T(8,128)(2,1)S(1)}, u32[]{:S(2)}, u32[]{:S(2)}) collective-permute-start(bf16[4,2,16,2304]{3,2,1,0:T(8,128)(2,1)S(1)} %pad_maximum_fusion.rest_0_), channel_id=1, source_target_pairs={{0,96},{16,152},{32,0},{48,184},{64,32},{80,216},{96,64},{112,248}... | collective-permute-start | bytes 1769480 | tf_op jit(solution)/shard_map/ppermute | solution.py:42
  34.9 13.4 %collective-permute-start.6 = (bf16[4,2,16,2304]{3,2,1,0:T(8,128)(2,1)S(1)}, bf16[4,2,16,2304]{3,2,1,0:T(8,128)(2,1)S(1)}, u32[]{:S(2)}, u32[]{:S(2)}) collective-permute-start(bf16[4,2,16,2304]{3,2,1,0:T(8,128)(2,1)S(1)} %pad_maximum_fusion.rest_0_), channel_id=1, source_target_pairs={{0,16},{16,0},{1,17},{17,1},{2,18},{18,2},{3,19},{19,3},{4,20},{20... | collective-permute-start | bytes 1769480 | tf_op jit(solution)/shard_map/ppermute | solution.py:46
  40.2 8.2 %collective-permute-start.9 = (bf16[4,2,16,2304]{3,2,1,0:T(8,128)(2,1)S(1)}, bf16[4,2,16,2304]{3,2,1,0:T(8,128)(2,1)}, u32[]{:S(2)}, u32[]{:S(2)}) collective-permute-start(bf16[4,2,16,2304]{3,2,1,0:T(8,128)(2,1)S(1)} %collective-permute-done.5.rest_3_), channel_id=1, source_target_pairs={{0,16},{16,0},{1,17},{17,1},{2,18},{18,2},{3,19},{19,3},{4,20},{20... | collective-permute-start | bytes 1769480 | tf_op jit(solution)/shard_map/ppermute | solution.py:46
  47.7 2.9 %collective-permute-start.8 = (bf16[4,2,16,2304]{3,2,1,0:T(8,128)(2,1)S(1)}, bf16[4,2,16,2304]{3,2,1,0:T(8,128)(2,1)}, u32[]{:S(2)}, u32[]{:S(2)}) collective-permute-start(bf16[4,2,16,2304]{3,2,1,0:T(8,128)(2,1)S(1)} %collective-permute-done.4.rest_2_), channel_id=1, source_target_pairs={{0,16},{16,0},{1,17},{17,1},{2,18},{18,2},{3,19},{19,3},{4,20},{20... | collective-permute-start | bytes 1769480 | tf_op jit(solution)/shard_map/ppermute | solution.py:46
  47.7 2.9 %collective-permute-start.7 = (bf16[4,2,16,2304]{3,2,1,0:T(8,128)(2,1)S(1)}, bf16[4,2,16,2304]{3,2,1,0:T(8,128)(2,1)S(1)}, u32[]{:S(2)}, u32[]{:S(2)}) collective-permute-start(bf16[4,2,16,2304]{3,2,1,0:T(8,128)(2,1)S(1)} %collective-permute-done.3.rest_1_), channel_id=1, source_target_pairs={{0,16},{16,0},{1,17},{17,1},{2,18},{18,2},{3,19},{19,3},{4,20},{20... | collective-permute-start | bytes 1769480 | tf_op jit(solution)/shard_map/ppermute | solution.py:46
  89.3 4.8 %collective-permute-start.10 = (bf16[512,2304]{1,0:T(8,128)(2,1)}, bf16[512,2304]{1,0:T(8,128)(2,1)S(1)}, u32[]{:S(2)}, u32[]{:S(2)}) collective-permute-start(bf16[512,2304]{1,0:T(8,128)(2,1)} %get-tuple-element.25), channel_id=1, source_target_pairs={{0,16},{16,0},{1,17},{17,1},{2,18},{18,2},{3,19},{19,3},{4,20},{20... | collective-permute-start | bytes 7077896 | tf_op jit(solution)/shard_map/ppermute | solution.py:46
  99.3 19.3 %collective-permute-start.11 = (bf16[9,16,2304]{2,1,0:T(8,128)(2,1)S(1)}, bf16[9,16,2304]{2,1,0:T(8,128)(2,1)S(1)}, u32[]{:S(2)}, u32[]{:S(2)}) collective-permute-start(bf16[9,16,2304]{2,1,0:T(8,128)(2,1)S(1)} %get-tuple-element.30), channel_id=1, source_target_pairs={{0,32},{16,144},{32,64},{48,176},{64,96},{80,208},{96,0},{112,240}... | collective-permute-start | bytes 1990664 | tf_op jit(solution)/shard_map/ppermute | solution.py:42
  99.9 18.6 %collective-permute-start.12 = (bf16[9,16,2304]{2,1,0:T(8,128)(2,1)S(1)}, bf16[9,16,2304]{2,1,0:T(8,128)(2,1)S(1)}, u32[]{:S(2)}, u32[]{:S(2)}) collective-permute-start(bf16[9,16,2304]{2,1,0:T(8,128)(2,1)S(1)} %get-tuple-element.31), channel_id=1, source_target_pairs={{0,64},{16,24},{32,96},{48,56},{64,0},{80,88},{96,32},{112,120},{1... | collective-permute-start | bytes 1990664 | tf_op jit(solution)/shard_map/ppermute | solution.py:42
  102.2 17.3 %collective-permute-start.13 = (bf16[9,16,2304]{2,1,0:T(8,128)(2,1)S(1)}, bf16[9,16,2304]{2,1,0:T(8,128)(2,1)S(1)}, u32[]{:S(2)}, u32[]{:S(2)}) collective-permute-start(bf16[9,16,2304]{2,1,0:T(8,128)(2,1)S(1)} %get-tuple-element.32), channel_id=1, source_target_pairs={{0,96},{16,152},{32,0},{48,184},{64,32},{80,216},{96,64},{112,248}... | collective-permute-start | bytes 1990664 | tf_op jit(solution)/shard_map/ppermute | solution.py:42
  120.0 9.6 %collective-permute-start.14 = (bf16[3,16,2304]{2,1,0:T(8,128)(2,1)S(1)}, bf16[3,16,2304]{2,1,0:T(8,128)(2,1)S(1)}, u32[]{:S(2)}, u32[]{:S(2)}) collective-permute-start(bf16[3,16,2304]{2,1,0:T(8,128)(2,1)S(1)} %get-tuple-element.50), channel_id=1, source_target_pairs={{0,128},{16,48},{32,160},{48,80},{64,192},{80,112},{96,224},{112,1... | collective-permute-start | bytes 663560 | tf_op jit(solution)/shard_map/ppermute | solution.py:38
  120.6 9.0 %collective-permute-start.15 = (bf16[3,16,2304]{2,1,0:T(8,128)(2,1)S(1)}, bf16[3,16,2304]{2,1,0:T(8,128)(2,1)S(1)}, u32[]{:S(2)}, u32[]{:S(2)}) collective-permute-start(bf16[3,16,2304]{2,1,0:T(8,128)(2,1)S(1)} %get-tuple-element.51), channel_id=1, source_target_pairs={{0,8},{16,80},{32,40},{48,112},{64,72},{80,16},{96,104},{112,48},{... | collective-permute-start | bytes 663560 | tf_op jit(solution)/shard_map/ppermute | solution.py:38
  122.9 7.6 %collective-permute-start.16 = (bf16[3,16,2304]{2,1,0:T(8,128)(2,1)S(1)}, bf16[3,16,2304]{2,1,0:T(8,128)(2,1)S(1)}, u32[]{:S(2)}, u32[]{:S(2)}) collective-permute-start(bf16[3,16,2304]{2,1,0:T(8,128)(2,1)S(1)} %get-tuple-element.52), channel_id=1, source_target_pairs={{0,136},{16,112},{32,168},{48,16},{64,200},{80,48},{96,232},{112,8... | collective-permute-start | bytes 663560 | tf_op jit(solution)/shard_map/ppermute | solution.py:38
  130.6 16.8 %copy-start.1 = (f32[4608]{0:T(1024)S(1)}, f32[4608]{0:T(1024)}, u32[]{:S(2)}) copy-start(f32[4608]{0:T(1024)} %param.5) | copy-start | bytes 55300
  130.6 16.8 %copy-start.2 = (bf16[2,4608]{1,0:T(2,128)(2,1)S(1)}, bf16[2,4608]{1,0:T(2,128)(2,1)}, u32[]{:S(2)}) copy-start(bf16[2,4608]{1,0:T(2,128)(2,1)} %param.4) | copy-start | bytes 55300
  131.9 15.3 %all-to-all-start.3 = ((bf16[16,4,2304]{2,1,0:T(4,128)(2,1)}), bf16[16,4,2304]{2,1,0:T(4,128)(2,1)S(1)}, u32[]{:S(2)}, u32[]{:S(2)}) async-start(bf16[16,4,2304]{2,1,0:T(4,128)(2,1)} %pad_maximum_fusion.5), calls=%async_computation.3 | async-start | bytes 589824 | tf_op jit(solution)/shard_map/all_to_all | solution.py:415
